TPU v7x, 128 devices: a whole 4x4x4 slice. The times are simulated.
128 devices in a mesh: seq: 128 (over z, x, y, core).
Axes of the slice: x: 4, y: 4, z: 4, core: 2. Of those that a mesh axis runs over, the one named last changes fastest.
Arguments:
- tokens: bfloat16 [16384, 2048], P('seq'), may hold values from -6 to 6
- sequence_lengths: int32 [8], replicated, may hold values from 961 to 8192, as said below
- attention_gain: bfloat16 [2048], replicated, may hold values from 0.25 to 1.75
- query_weight: bfloat16 [2048, 2048], P('seq'), may hold values from -0.125 to 0.125
- key_weight: bfloat16 [2048, 256], P('seq'), may hold values from -0.125 to 0.125
- value_weight: bfloat16 [2048, 256], P('seq'), may hold values from -0.125 to 0.125
- output_weight_flipped: bfloat16 [2048, 2048], P('seq'), may hold values from -0.5 to 0.5
- query_adapter_down: bfloat16 [2048, 8], replicated, may hold values from -0.125 to 0.125
- query_adapter_up: bfloat16 [8, 2048], replicated, may hold values from -1 to 1
- key_adapter_down: bfloat16 [2048, 8], replicated, may hold values from -0.125 to 0.125
- key_adapter_up: bfloat16 [8, 256], replicated, may hold values from -1 to 1
- value_adapter_down: bfloat16 [2048, 8], replicated, may hold values from -0.125 to 0.125
- value_adapter_up: bfloat16 [8, 256], replicated, may hold values from -1 to 1
- output_adapter_down: bfloat16 [2048, 8], replicated, may hold values from -0.5 to 0.5
- output_adapter_up: bfloat16 [8, 2048], replicated, may hold values from -1 to 1
- query_feature_map: bfloat16 [32, 64, 64], replicated, may hold values from -3 to 3
- key_feature_map: bfloat16 [4, 64, 64], replicated, may hold values from -3 to 3
- feedforward_gain: bfloat16 [2048], replicated, may hold values from 0.25 to 1.75
- gate_weight: bfloat16 [2048, 5632], P('seq'), may hold values from -0.125 to 0.125
- up_weight: bfloat16 [2048, 5632], P('seq'), may hold values from -0.125 to 0.125
- down_weight_flipped: bfloat16 [2048, 5632], P('seq'), may hold values from -0.078125 to 0.078125
- output_gradient: bfloat16 [16384, 2048], P('seq'), may hold values from -6 to 6
Outputs:
- block_out: bfloat16 [16384, 2048], P('seq')
- grad_tokens: bfloat16 [16384, 2048], P('seq')
- grad_gain_attn: float32 [2048], replicated
- grad_lora_qa: float32 [2048, 8], replicated
- grad_lora_qb: float32 [8, 2048], replicated
- grad_lora_ka: float32 [2048, 8], replicated
- grad_lora_kb: float32 [8, 256], replicated
- grad_lora_va: float32 [2048, 8], replicated
- grad_lora_vb: float32 [8, 256], replicated
- grad_lora_oa: float32 [2048, 8], replicated
- grad_lora_ob: float32 [8, 2048], replicated
- grad_feat_query: float32 [32, 64, 64], replicated
- grad_feat_key: float32 [4, 64, 64], replicated
- grad_gain_mlp: float32 [2048], replicated
Inputs may be any that keep to these rules, and one draw needn't show every extreme that they name: `sequence_lengths`: the sequences lie end to end in the order given, each starting at a stretch boundary; their stretch counts ceil(length / 64) add up to 256, and each spans 16 stretches or more. The longest spans exactly 128 stretches and fills them all.
All inputs are finite; a program needn't handle non-finite values.
Results may differ from a plain program's by a relative error of at most 0.024.
Values may be sent and summed in bfloat16 or wider, within the bound.
A program may use at most 256 MiB of HBM per device.

v0:
```python
import math

import jax
import jax.numpy as jnp
from jax import lax
from jax.sharding import PartitionSpec as P

QUERY_HEADS = 32
KEY_VALUE_HEADS = 4
HEAD_SIZE = 64
FEAT = 64
STRETCH = 64


EPSILON = 1e-05
HIGHEST = lax.Precision.HIGHEST


def entering(array, axis, combine, identity, reverse):
    peers, position = (lax.axis_size(axis), lax.axis_index(axis))
    everything = jax.tree.map(
        lambda part, kind: lax.all_gather(part.astype(kind), axis),
        array,
        jax.tree.map(lambda a: jnp.bfloat16 if a.dtype == jnp.float32 else a.dtype, array),
    )
    start = jax.tree.map(
        lambda part, zero: jnp.broadcast_to(jnp.asarray(zero, part.dtype), part.shape),
        array,
        identity,
    )

    def step(k, before):
        at = peers - 1 - k if reverse else k
        reached = at > position if reverse else at < position
        new = combine(
            before, jax.tree.map(lambda part, own: part[at].astype(own.dtype), everything, array)
        )
        return jax.tree.map(lambda a, b: jnp.where(reached, a, b), new, before)

    return lax.fori_loop(0, peers, step, start)


def product_result(left, right):
    return jnp.dot(left, right, preferred_element_type=jnp.float32)


def flipped_product(left, right):
    return lax.dot_general(
        left, right, (((0,), (0,)), ((), ())), preferred_element_type=jnp.float32
    )


def product_flipped(left, right):
    return lax.dot_general(
        left, right, (((1,), (1,)), ((), ())), preferred_element_type=jnp.float32
    )


def layout(sequence_lengths, first_stretch, stretch_count):
    counts = (sequence_lengths + STRETCH - 1) // STRETCH
    seq_ends = jnp.cumsum(counts)
    starts = seq_ends - counts
    stretch_ids = first_stretch + jnp.arange(stretch_count)
    member = (
        (stretch_ids[:, None] >= starts[None]) & (stretch_ids[:, None] < seq_ends[None])
    ).astype(jnp.int32)
    seq_begin = jnp.sum(member * starts[None], 1)
    length = jnp.sum(member * sequence_lengths[None], 1)
    stretch_gates = (stretch_ids != seq_begin).astype(jnp.float32)
    offset = jnp.arange(STRETCH)
    valid_mask = (stretch_ids - seq_begin)[:, None] * STRETCH + offset[None] < length[:, None]
    return (stretch_gates, valid_mask)


def combine(earlier, later):
    return (
        later[0] + later[2] * earlier[0],
        later[1] + later[2] * earlier[1],
        later[2] * earlier[2],
    )


def identity_element():
    return (
        jnp.zeros((KEY_VALUE_HEADS, FEAT, HEAD_SIZE), jnp.float32),
        jnp.zeros((KEY_VALUE_HEADS, FEAT), jnp.float32),
        jnp.ones((), jnp.float32),
    )


def fold_local(block_states, block_norms, stretch_gates, backward):
    folded = identity_element()
    positions = list(range(stretch_gates.shape[0]))
    if backward:
        positions = positions[::-1]
    for position in positions:
        folded = combine(
            folded, (block_states[position], block_norms[position], stretch_gates[position])
        )
    return folded


def key_side(key4, value4, key_feature_map, valid_mask):
    logits = jnp.einsum("ctkd,kdf->ctkf", key4, key_feature_map, preferred_element_type=jnp.float32)
    key_feat = jax.nn.softmax(logits, -1)
    key_masked = key_feat * valid_mask.astype(jnp.float32)[:, :, None, None]
    stretch_state = jnp.einsum(
        "ctkf,ctkd->ckfd", key_masked, value4.astype(jnp.float32), precision=HIGHEST
    )
    stretch_norm = jnp.sum(key_masked, 1)
    return (key_feat, key_masked, stretch_state, stretch_norm)


def spread_states(prefix, stretch_state, stretch_norm, stretch_gates):
    carry_state, carry_norm = (prefix[0], prefix[1])
    states_in, norms_in = ([], [])
    for position in range(stretch_gates.shape[0]):
        carry_state = stretch_gates[position] * carry_state
        carry_norm = stretch_gates[position] * carry_norm
        states_in.append(carry_state)
        norms_in.append(carry_norm)
        carry_state = carry_state + stretch_state[position]
        carry_norm = carry_norm + stretch_norm[position]
    return (jnp.stack(states_in), jnp.stack(norms_in))


def query_side(query5, key4, value4, feat_q4, states_in, norms_in, allowed, score_scale):
    logits = jnp.einsum("ctkgd,kgdf->ctkgf", query5, feat_q4, preferred_element_type=jnp.float32)
    query_feat = jax.nn.softmax(logits, -1)
    scores = (
        jnp.einsum("ctkgd,cukd->ckgtu", query5, key4, preferred_element_type=jnp.float32)
        * score_scale
    )
    row_peak = jnp.max(jnp.where(allowed, scores, -1e30), -1)
    weights_p = jnp.exp(jnp.where(allowed, scores - row_peak[..., None], -1e30))
    damping = jnp.exp(-row_peak)
    linear_num = damping[..., None] * jnp.einsum(
        "ctkgf,ckfd->ckgtd", query_feat, states_in, precision=HIGHEST
    )
    linear_den = damping * jnp.einsum("ctkgf,ckf->ckgt", query_feat, norms_in, precision=HIGHEST)
    numerator = (
        jnp.einsum(
            "ckgtu,cukd->ckgtd",
            weights_p.astype(jnp.bfloat16),
            value4,
            preferred_element_type=jnp.float32,
        )
        + linear_num
    )
    denominator = jnp.sum(weights_p, -1) + linear_den
    return (query_feat, weights_p, damping, numerator, denominator)


def to_tokens(heads_first):
    return heads_first.transpose(0, 3, 1, 2, 4).reshape(-1, QUERY_HEADS * HEAD_SIZE)


def attention_back(
    heads_merged_gradient,
    query5,
    key4,
    value4,
    feat_q4,
    key_feature_map,
    key_feat,
    key_masked,
    query_feat,
    weights_p,
    damping,
    numerator,
    denominator,
    states_in,
    norms_in,
    stretch_gates,
    valid_mask,
    score_scale,
):
    stretches_dev = query5.shape[0]
    grad_heads = (
        heads_merged_gradient.astype(jnp.float32)
        .reshape(stretches_dev, STRETCH, KEY_VALUE_HEADS, QUERY_HEADS // KEY_VALUE_HEADS, HEAD_SIZE)
        .transpose(0, 2, 3, 1, 4)
    )
    mixed_full = numerator / denominator[..., None]
    numerator_grad = (grad_heads / denominator[..., None]).astype(jnp.bfloat16)
    denominator_grad = -jnp.sum(grad_heads * mixed_full, -1) / denominator
    prob_grad = (
        jnp.einsum("ckgtd,cukd->ckgtu", numerator_grad, value4, preferred_element_type=jnp.float32)
        + denominator_grad[..., None]
    )
    score_grad = (weights_p * prob_grad).astype(jnp.bfloat16)
    query_gradient = (
        jnp.einsum("ckgtu,cukd->ctkgd", score_grad, key4, preferred_element_type=jnp.float32)
        * score_scale
    )
    key_gradient = (
        jnp.einsum("ckgtu,ctkgd->cukd", score_grad, query5, preferred_element_type=jnp.float32)
        * score_scale
    )
    value_gradient = jnp.einsum(
        "ckgtu,ckgtd->cukd",
        weights_p.astype(jnp.bfloat16),
        numerator_grad,
        preferred_element_type=jnp.float32,
    )
    numer_wide = numerator_grad.astype(jnp.float32)
    damp_tokens = damping.transpose(0, 3, 1, 2)[..., None]
    denom_tokens = denominator_grad.transpose(0, 3, 1, 2)
    qfeat_grad = damp_tokens * (
        jnp.einsum("ckgtd,ckfd->ctkgf", numer_wide, states_in, precision=HIGHEST)
        + denom_tokens[..., None] * norms_in[:, None, :, None, :]
    )
    weighted = query_feat * damp_tokens
    state_in_grad = jnp.einsum("ctkgf,ckgtd->ckfd", weighted, numer_wide, precision=HIGHEST)
    norm_in_grad = jnp.einsum("ctkgf,ctkg->ckf", weighted, denom_tokens, precision=HIGHEST)
    suffix = entering(
        fold_local(
            stretch_gates[:, None, None, None] * state_in_grad,
            stretch_gates[:, None, None] * norm_in_grad,
            stretch_gates,
            True,
        ),
        "seq",
        combine,
        identity_element(),
        True,
    )
    carry_state, carry_norm = (suffix[0], suffix[1])
    state_grads, norm_grads = ([None] * stretches_dev, [None] * stretches_dev)
    for position in reversed(range(stretches_dev)):
        state_grads[position] = carry_state
        norm_grads[position] = carry_norm
        carry_state = stretch_gates[position] * (state_in_grad[position] + carry_state)
        carry_norm = stretch_gates[position] * (norm_in_grad[position] + carry_norm)
    stretch_state_grad = jnp.stack(state_grads)
    stretch_norm_grad = jnp.stack(norm_grads)
    kfeat_grad = (
        jnp.einsum(
            "ctkd,ckfd->ctkf", value4.astype(jnp.float32), stretch_state_grad, precision=HIGHEST
        )
        + stretch_norm_grad[:, None]
    ) * valid_mask.astype(jnp.float32)[:, :, None, None]
    value_gradient = value_gradient + jnp.einsum(
        "ctkf,ckfd->ctkd", key_masked, stretch_state_grad, precision=HIGHEST
    )
    key_logit_grad = (
        key_feat * (kfeat_grad - jnp.sum(key_feat * kfeat_grad, -1, keepdims=True))
    ).astype(jnp.bfloat16)
    query_logit_grad = (
        query_feat * (qfeat_grad - jnp.sum(query_feat * qfeat_grad, -1, keepdims=True))
    ).astype(jnp.bfloat16)
    key_gradient = key_gradient + jnp.einsum(
        "ctkf,kdf->ctkd", key_logit_grad, key_feature_map, preferred_element_type=jnp.float32
    )
    query_gradient = query_gradient + jnp.einsum(
        "ctkgf,kgdf->ctkgd", query_logit_grad, feat_q4, preferred_element_type=jnp.float32
    )
    feat_key_grad = jnp.einsum(
        "ctkd,ctkf->kdf", key4, key_logit_grad, preferred_element_type=jnp.float32
    )
    feat_query_grad = jnp.einsum(
        "ctkgd,ctkgf->kgdf", query5, query_logit_grad, preferred_element_type=jnp.float32
    ).reshape(QUERY_HEADS, HEAD_SIZE, FEAT)
    return (
        query_gradient.reshape(-1, QUERY_HEADS * HEAD_SIZE).astype(jnp.bfloat16),
        key_gradient.reshape(-1, KEY_VALUE_HEADS * HEAD_SIZE).astype(jnp.bfloat16),
        value_gradient.reshape(-1, KEY_VALUE_HEADS * HEAD_SIZE).astype(jnp.bfloat16),
        feat_query_grad,
        feat_key_grad,
    )


def body(
    tokens,
    sequence_lengths,
    attention_gain,
    query_weight,
    key_weight,
    value_weight,
    output_weight_flipped,
    query_adapter_down,
    query_adapter_up,
    key_adapter_down,
    key_adapter_up,
    value_adapter_down,
    value_adapter_up,
    output_adapter_down,
    output_adapter_up,
    query_feature_map,
    key_feature_map,
    feedforward_gain,
    gate_weight,
    up_weight,
    down_weight_flipped,
    output_gradient,
):
    rows_dev = tokens.shape[0]
    stretches_dev = rows_dev // STRETCH
    groups = QUERY_HEADS // KEY_VALUE_HEADS
    score_scale = 1.0 / math.sqrt(HEAD_SIZE)
    stretch_gates, valid_mask = layout(
        sequence_lengths, lax.axis_index("seq") * stretches_dev, stretches_dev
    )
    causal = jnp.tril(jnp.ones((STRETCH, STRETCH), bool))
    allowed = causal[None, None, None] & valid_mask[:, None, None, None, :]
    inputs = tokens.astype(jnp.float32)
    rms_one = lax.rsqrt(jnp.mean(inputs * inputs, -1, keepdims=True) + EPSILON)
    normed_one = inputs * rms_one
    gain_one = attention_gain.astype(jnp.float32)
    hidden_first = (normed_one * gain_one).astype(jnp.bfloat16)
    attention_whole = (
        lax.all_gather(query_weight, "seq", axis=0, tiled=True),
        lax.all_gather(key_weight, "seq", axis=0, tiled=True),
        lax.all_gather(value_weight, "seq", axis=0, tiled=True),
        lax.all_gather(output_weight_flipped, "seq", axis=0, tiled=True),
    )

    def apply_projection(weight_matrix, adapter_first_factor, adapter_second_factor):
        adapter_update = product_result(hidden_first, adapter_first_factor).astype(jnp.bfloat16)
        projection_result = product_result(hidden_first, weight_matrix) + 2.0 * product_result(
            adapter_update, adapter_second_factor
        )
        return (adapter_update, projection_result.astype(jnp.bfloat16))

    query_adapter_rows, query_matrix = apply_projection(
        attention_whole[0], query_adapter_down, query_adapter_up
    )
    key_adapter_rows, key_matrix = apply_projection(
        attention_whole[1], key_adapter_down, key_adapter_up
    )
    value_adapter_rows, value_matrix = apply_projection(
        attention_whole[2], value_adapter_down, value_adapter_up
    )
    query5 = query_matrix.reshape(stretches_dev, STRETCH, KEY_VALUE_HEADS, groups, HEAD_SIZE)
    key4 = key_matrix.reshape(stretches_dev, STRETCH, KEY_VALUE_HEADS, HEAD_SIZE)
    value4 = value_matrix.reshape(stretches_dev, STRETCH, KEY_VALUE_HEADS, HEAD_SIZE)
    feat_q4 = query_feature_map.reshape(KEY_VALUE_HEADS, groups, HEAD_SIZE, FEAT)
    key_feat, key_masked, stretch_state, stretch_norm = key_side(
        key4, value4, key_feature_map, valid_mask
    )
    prefix = entering(
        fold_local(stretch_state, stretch_norm, stretch_gates, False),
        "seq",
        combine,
        identity_element(),
        False,
    )
    states_in, norms_in = spread_states(prefix, stretch_state, stretch_norm, stretch_gates)
    query_feat, weights_p, damping, numerator, denominator = query_side(
        query5, key4, value4, feat_q4, states_in, norms_in, allowed, score_scale
    )
    heads_merged = to_tokens(numerator / denominator[..., None]).astype(jnp.bfloat16)
    output_adapter_rows = product_result(heads_merged, output_adapter_down).astype(jnp.bfloat16)
    branch_rows = product_flipped(heads_merged, attention_whole[3]) + 2.0 * product_result(
        output_adapter_rows, output_adapter_up
    )
    middle = inputs + branch_rows
    rms_two = lax.rsqrt(jnp.mean(middle * middle, -1, keepdims=True) + EPSILON)
    normed_two = middle * rms_two
    gain_two = feedforward_gain.astype(jnp.float32)
    hidden_two = (normed_two * gain_two).astype(jnp.bfloat16)
    mlp_full = (
        lax.all_gather(gate_weight, "seq", axis=0, tiled=True),
        lax.all_gather(up_weight, "seq", axis=0, tiled=True),
        lax.all_gather(down_weight_flipped, "seq", axis=0, tiled=True),
    )
    gate_act = product_result(hidden_two, mlp_full[0])
    up_act = product_result(hidden_two, mlp_full[1])
    sigmoid_gate = jax.nn.sigmoid(gate_act)
    swish_gate = gate_act * sigmoid_gate
    inner_act = (swish_gate * up_act).astype(jnp.bfloat16)
    block_out = (middle + product_flipped(inner_act, mlp_full[2])).astype(jnp.bfloat16)
    w_q_all, w_k_all, w_v_all, output_weight_whole, w_g_all, w_u_all, w_d_all = (
        lax.all_gather(query_weight, "seq", axis=0, tiled=True),
        lax.all_gather(key_weight, "seq", axis=0, tiled=True),
        lax.all_gather(value_weight, "seq", axis=0, tiled=True),
        lax.all_gather(output_weight_flipped, "seq", axis=0, tiled=True),
        lax.all_gather(gate_weight, "seq", axis=0, tiled=True),
        lax.all_gather(up_weight, "seq", axis=0, tiled=True),
        lax.all_gather(down_weight_flipped, "seq", axis=0, tiled=True),
    )
    inner_grad = product_result(output_gradient, w_d_all).astype(jnp.bfloat16).astype(jnp.float32)
    gate_grad = (
        inner_grad * up_act * sigmoid_gate * (1.0 + gate_act * (1.0 - sigmoid_gate))
    ).astype(jnp.bfloat16)
    up_grad = (inner_grad * swish_gate).astype(jnp.bfloat16)
    two_grad = product_flipped(gate_grad, w_g_all) + product_flipped(up_grad, w_u_all)
    gain_mlp_grad = jnp.sum(two_grad * normed_two, 0)
    scaled_two = two_grad * gain_two
    middle_grad = output_gradient.astype(jnp.float32) + rms_two * (
        scaled_two - normed_two * jnp.mean(scaled_two * normed_two, -1, keepdims=True)
    )
    branch_gradient = middle_grad.astype(jnp.bfloat16)
    output_adapter_gradient = (2.0 * product_flipped(branch_gradient, output_adapter_up)).astype(
        jnp.bfloat16
    )
    output_adapter_up_gradient = 2.0 * flipped_product(output_adapter_rows, branch_gradient)
    output_adapter_down_gradient = flipped_product(heads_merged, output_adapter_gradient)
    heads_merged_gradient = (
        product_result(branch_gradient, output_weight_whole)
        + product_flipped(output_adapter_gradient, output_adapter_down)
    ).astype(jnp.bfloat16)
    key_again, masked_again, state_again, norm_again = key_side(
        key4, value4, key_feature_map, valid_mask
    )
    prefix_again = entering(
        fold_local(state_again, norm_again, stretch_gates, False),
        "seq",
        combine,
        identity_element(),
        False,
    )
    states_back, norms_back = spread_states(prefix_again, state_again, norm_again, stretch_gates)
    qfeat_again, weights_again, damping_again, numer_again, denom_again = query_side(
        query5, key4, value4, feat_q4, states_back, norms_back, allowed, score_scale
    )
    kept_parts = (
        key_again,
        masked_again,
        qfeat_again,
        weights_again,
        damping_again,
        numer_again,
        denom_again,
        states_back,
        norms_back,
    )
    query_gradient, key_gradient, value_gradient, feat_query_grad, feat_key_grad = attention_back(
        heads_merged_gradient,
        query5,
        key4,
        value4,
        feat_q4,
        key_feature_map,
        kept_parts[0],
        kept_parts[1],
        kept_parts[2],
        kept_parts[3],
        kept_parts[4],
        kept_parts[5],
        kept_parts[6],
        kept_parts[7],
        kept_parts[8],
        stretch_gates,
        valid_mask,
        score_scale,
    )
    query_adapter_gradient = (2.0 * product_flipped(query_gradient, query_adapter_up)).astype(
        jnp.bfloat16
    )
    key_adapter_gradient = (2.0 * product_flipped(key_gradient, key_adapter_up)).astype(
        jnp.bfloat16
    )
    value_adapter_gradient = (2.0 * product_flipped(value_gradient, value_adapter_up)).astype(
        jnp.bfloat16
    )
    query_adapter_up_gradient = 2.0 * flipped_product(query_adapter_rows, query_gradient)
    key_adapter_up_gradient = 2.0 * flipped_product(key_adapter_rows, key_gradient)
    value_adapter_up_gradient = 2.0 * flipped_product(value_adapter_rows, value_gradient)
    query_adapter_down_gradient = flipped_product(hidden_first, query_adapter_gradient)
    key_adapter_down_gradient = flipped_product(hidden_first, key_adapter_gradient)
    value_adapter_down_gradient = flipped_product(hidden_first, value_adapter_gradient)
    one_grad = (
        product_flipped(query_gradient, w_q_all)
        + product_flipped(key_gradient, w_k_all)
        + product_flipped(value_gradient, w_v_all)
        + product_flipped(query_adapter_gradient, query_adapter_down)
        + product_flipped(key_adapter_gradient, key_adapter_down)
        + product_flipped(value_adapter_gradient, value_adapter_down)
    )
    gain_attn_grad = jnp.sum(one_grad * normed_one, 0)
    scaled_one = one_grad * gain_one
    grad_tokens = (
        middle_grad
        + rms_one * (scaled_one - normed_one * jnp.mean(scaled_one * normed_one, -1, keepdims=True))
    ).astype(jnp.bfloat16)
    summed = lax.psum(
        (
            gain_attn_grad,
            query_adapter_down_gradient,
            query_adapter_up_gradient,
            key_adapter_down_gradient,
            key_adapter_up_gradient,
            value_adapter_down_gradient,
            value_adapter_up_gradient,
            output_adapter_down_gradient,
            output_adapter_up_gradient,
            feat_query_grad,
            feat_key_grad,
            gain_mlp_grad,
        ),
        "seq",
    )
    return (
        block_out,
        grad_tokens,
        summed[0],
        summed[1],
        summed[2],
        summed[3],
        summed[4],
        summed[5],
        summed[6],
        summed[7],
        summed[8],
        summed[9],
        summed[10],
        summed[11],
    )


def solution(mesh):
    return jax.shard_map(
        body,
        mesh=mesh,
        in_specs=(
            P("seq", None),
            P(),
            P(),
            P("seq", None),
            P("seq", None),
            P("seq", None),
            P("seq", None),
            P(),
            P(),
            P(),
            P(),
            P(),
            P(),
            P(),
            P(),
            P(),
            P(),
            P(),
            P("seq", None),
            P("seq", None),
            P("seq", None),
            P("seq", None),
        ),
        out_specs=(
            P("seq", None),
            P("seq", None),
            P(),
            P(),
            P(),
            P(),
            P(),
            P(),
            P(),
            P(),
            P(),
            P(),
            P(),
            P(),
        ),
        check_vma=False,
    )
```

profile of v0, /device:TPU:1, one launch (start us, length us, event | category | flops | bytes accessed | tf_op | source)
XLA Modules:
  0.0 1400.8 jit_solution(16719432012293681357)
XLA Ops:
  16.9 61.1 %all-gather.14.cloned.1.call-done = bf16[2048,256]{1,0:T(8,128)(2,1)} async-done(((bf16[16,256]{1,0:T(8,128)(2,1)}), bf16[2048,256]{1,0:T(8,128)(2,1)}) %all-gather.14.cloned.1.call-update) | async-done | bytes 1048592 | tf_op jit(solution)/shard_map/all_gather | solution.py:314
  80.0 61.9 %all-gather.10.cloned.1.call-done = bf16[2048,256]{1,0:T(8,128)(2,1)} async-done(((bf16[16,256]{1,0:T(8,128)(2,1)}), bf16[2048,256]{1,0:T(8,128)(2,1)}) %all-gather.10.cloned.1.call-update) | async-done | bytes 1048592 | tf_op jit(solution)/shard_map/all_gather | solution.py:313
  152.1 63.5 %all-reduce = bf16[128]{0:T(256)(128)(2,1)S(1)} all-reduce(bf16[128]{0:T(256)(128)(2,1)S(1)} %dynamic-update-slice), channel_id=1, replica_groups=mesh['seq'=128] {'seq'}, use_global_device_ids=true, to_apply=%add | all-reduce | flops 128 | bytes 512
  217.8 34.0 %all_gather.64 = bf16[128,4,64]{2,1,0:T(4,128)(2,1)S(1)} all-gather(bf16[1,4,64]{2,1,0:T(4,128)(2,1)S(1)} %add_convert_fusion), channel_id=1, replica_groups=mesh['seq'=128] {'seq'}, dimensions={0}, use_global_device_ids=true | all-gather | bytes 66048 | tf_op jit(solution)/shard_map/all_gather | solution.py:22
  251.8 282.5 %while.40 = (s32[]{:T(128)}, f32[4,64,64]{2,1,0:T(8,128)S(1)}, f32[4,64]{1,0:T(4,128)S(1)}, s32[]{:T(128)}, bf16[128,4,64,64]{3,2,1,0:T(8,128)(2,1)}, /*index=5*...) while((s32[]{:T(128)}, f32[4,64,64]{2,1,0:T(8,128)S(1)}, ...), condition=%wide.region_9.10_spmd.clone, body=%wide.region_8.9_spmd.clone.sunk | while | flops 83205 | bytes 166553 | solution.py:40
  537.5 4.6 fusion.140
  552.1 3.7 fusion.22
  559.8 6.4 fusion.142
  566.7 12.7 fusion.125
  579.4 12.7 fusion.126
  592.1 38.8 %all-gather.24.cloned.1.call-done = bf16[2048,5632]{1,0:T(8,128)(2,1)} async-done(((bf16[16,5632]{1,0:T(8,128)(2,1)}), bf16[2048,5632]{1,0:T(8,128)(2,1)}) %all-gather.24.cloned.1.call-update) | async-done | bytes 23068688 | tf_op jit(solution)/shard_map/all_gather | solution.py:365
  630.9 12.3 fusion.5
  643.2 15.4 %fusion.38 = f32[128,2048]{1,0:T(8,128)} fusion(bf16[2048,5632]{1,0:T(8,128)(2,1)} %all-gather.20.cloned.1.call-done, f32[128,5632]{1,0:T(8,128)} %fusion.126, f32[128,5632]{1,0:T(8,128)} %fusion.5, f32[128,5632]{1,0:T(8,128)} %fusion.125), kind=kOutput, calls=%fused_computation.73 | convolution fusion | flops 2959998976 | bytes 32768000 | tf_op jit(solution)/shard_map/dot_general | solution.py:54
  658.6 15.4 %multiply_reduce_fusion.1 = (f32[2048]{0:T(1024)}, f32[128]{0:T(128)S(1)}, f32[128,2048]{1,0:T(8,128)}) fusion(f32[128,2048]{1,0:T(8,128)S(1)} %get-tuple-element.456, f32[128]{0:T(128)S(1)} %add_rsqrt_fusion, f32[2048]{0:T(1024)S(1)} %convert_element_type.261, f32[128,2048]{1,0:T(8,128)} %fusion.38, bf16[2048,5632]{1,0:T(8,128)(2,1)} %all-gather.22.cloned.1.call-done, ...), kind=kOutput, calls=%fused_computation.126 | convolution fusion | flops 2958948352 | bytes 31998976 | tf_op jit(solution)/shard_map/dot_general | solution.py:54
  676.0 4.7 fusion.115
  685.2 3.3 copy.213
  688.5 4.7 fusion.27
  714.6 4.1 fusion.28
  719.4 38.1 %all_gather.70 = bf16[128,4,64]{2,1,0:T(4,128)(2,1)} all-gather(bf16[1,4,64]{2,1,0:T(4,128)(2,1)S(1)} %fusion.110), channel_id=1, replica_groups=mesh['seq'=128] {'seq'}, dimensions={0}, use_global_device_ids=true | all-gather | bytes 66048 | tf_op jit(solution)/shard_map/all_gather | solution.py:22
  765.7 3.9 fusion.144
  769.5 14.3 %fusion.10 = bf16[128,2048]{1,0:T(8,128)(2,1)} fusion(f32[128,2048]{1,0:T(8,128)S(1)} %get-tuple-element.456, bf16[2048,5632]{1,0:T(8,128)(2,1)} %all-gather.24.cloned.1.call-done, f32[128,5632]{1,0:T(8,128)} %fusion.125, f32[128,5632]{1,0:T(8,128)} %fusion.126), kind=kOutput, calls=%fused_computation.29 | convolution fusion | flops 2957639680 | bytes 30408704 | tf_op jit(solution)/shard_map/dot_general | solution.py:54
  783.9 362.5 %while.41 = (s32[]{:T(128)}, f32[4,64,64]{2,1,0:T(8,128)S(1)}, f32[4,64]{1,0:T(4,128)S(1)}, s32[]{:T(128)}, bf16[128,4,64,64]{3,2,1,0:T(8,128)(2,1)}, /*index=5*...) while((s32[]{:T(128)}, f32[4,64,64]{2,1,0:T(8,128)S(1)}, ...), condition=%wide.region_18.19_spmd.clone, body=%wide.region_17.18_spmd.clone.sunk | while | flops 83209 | bytes 166615 | solution.py:40
  1169.6 63.6 %all-reduce.1 = (f32[2048]{0:T(1024)}, f32[8,256]{1,0:T(8,128)}, f32[8,256]{1,0:T(8,128)}, f32[2048]{0:T(1024)}) all-reduce(f32[2048]{0:T(1024)S(1)} %get-tuple-element.386, f32[8,256]{1,0:T(8,128)S(1)} %convolution_multiply_fusion.7, f32[8,256]{1,0:T(8,128)S(1)} %convolution_multiply_fusion.6, ...), channel_id=1, replica_groups=mesh['seq'=128] {'seq'}, use_global_device_ids=true, to_apply=%region_22.23 | all-reduce | flops 8192 | bytes 65536 | tf_op jit(solution)/shard_map/psum | solution.py:477
  1235.6 146.0 %all-reduce.5.cloned.1.call-done = (f32[2048,8]{0,1:T(8,128)}, f32[8,2048]{1,0:T(8,128)}, f32[2048,8]{0,1:T(8,128)}, f32[2048,8]{0,1:T(8,128)}, f32[2048,8]{0,1:...) async-done(((f32[2048,8]{0,1:T(8,128)}, f32[8,2048]{1,0:T(8,128)}, f32[2048,8]{0,1:T(8,128)}, f32[2048,8]{0,1:T(8,128)}, ...) | async-done | bytes 983056 | tf_op jit(solution)/shard_map/psum | solution.py:477
  (1127 shorter events, 583.7 us)
Async XLA Ops:
  7.2 539.5 %copy-start = (bf16[32,64,64]{2,1,0:T(8,128)(2,1)S(1)}, bf16[32,64,64]{2,1,0:T(8,128)(2,1)}, u32[]{:S(2)}) copy-start(bf16[32,64,64]{2,1,0:T(8,128)(2,1)} %param.41) | copy-start | bytes 786436
  7.2 70.8 %all-gather.14.cloned.1.call-start = ((), (), s32[]{:S(2)}) async-start(), calls=%async_computation.2 | async-start | bytes 1056768 | tf_op jit(solution)/shard_map/all_gather | solution.py:314
  7.9 133.9 %all-gather.10.cloned.1.call-start = ((), (), s32[]{:S(2)}) async-start(), calls=%async_computation | async-start | bytes 1056768 | tf_op jit(solution)/shard_map/all_gather | solution.py:313
  8.7 243.1 %all-gather.16.cloned.1.call-start = ((), (), s32[]{:S(2)}) async-start(), calls=%async_computation.3 | async-start | bytes 8454144 | tf_op jit(solution)/shard_map/all_gather | solution.py:22
  9.4 70.1 %copy-start.50 = (f32[2048]{0:T(1024)}, f32[2048]{0:T(1024)S(1)}, u32[]{:S(2)}) copy-start(f32[2048]{0:T(1024)S(1)} %convert_element_type.244) | copy-start | bytes 24580
  9.4 70.2 %copy-start.91 = (bf16[8,256]{1,0:T(8,128)(2,1)S(1)}, bf16[8,256]{1,0:T(8,128)(2,1)}, u32[]{:S(2)}) copy-start(bf16[8,256]{1,0:T(8,128)(2,1)} %param.38) | copy-start | bytes 12292
  14.4 129.9 %copy-start.100 = (f32[2,64]{1,0:T(2,128)}, f32[2,64]{1,0:T(2,128)S(1)}, u32[]{:S(2)}) copy-start(f32[2,64]{1,0:T(2,128)S(1)} %get-tuple-element.432) | copy-start | bytes 1540
  16.7 126.8 %copy-start.90 = (bf16[8,256]{1,0:T(8,128)(2,1)S(1)}, bf16[8,256]{1,0:T(8,128)(2,1)}, u32[]{:S(2)}) copy-start(bf16[8,256]{1,0:T(8,128)(2,1)} %param.36) | copy-start | bytes 12292
  16.9 126.5 %copy-start.85 = (bf16[128,8]{0,1:T(8,128)(2,1)}, bf16[128,8]{0,1:T(8,128)(2,1)S(1)}, u32[]{:S(2)}) copy-start(bf16[128,8]{0,1:T(8,128)(2,1)S(1)} %convolution_convert_fusion.4) | copy-start | bytes 6148
  16.9 127.0 %copy-start.45 = (bf16[4,64,64]{2,1,0:T(8,128)(2,1)S(1)}, bf16[4,64,64]{2,1,0:T(8,128)(2,1)}, u32[]{:S(2)}) copy-start(bf16[4,64,64]{2,1,0:T(8,128)(2,1)} %param.42) | copy-start | bytes 98308
  143.5 72.2 %copy-start.102 = (bf16[2048]{0:T(1024)(128)(2,1)S(1)}, bf16[2048]{0:T(1024)(128)(2,1)}, u32[]{:S(2)}) copy-start(bf16[2048]{0:T(1024)(128)(2,1)} %param.43) | copy-start | bytes 12292
  146.5 391.0 %all-gather.12.cloned.1.call-start = ((), (), s32[]{:S(2)}) async-start(), calls=%async_computation.1 | async-start | bytes 8454144 | tf_op jit(solution)/shard_map/all_gather | solution.py:312
  147.1 412.7 %all-gather.18.cloned.1.call-start = ((), (), s32[]{:S(2)}) async-start(), calls=%async_computation.4 | async-start | bytes 8454144 | tf_op jit(solution)/shard_map/all_gather | solution.py:315
  147.7 419.1 %all-gather.22.cloned.1.call-start = ((), (), s32[]{:S(2)}) async-start(), calls=%async_computation.6 | async-start | bytes 23248896 | tf_op jit(solution)/shard_map/all_gather | solution.py:364
  148.2 431.1 %all-gather.20.cloned.1.call-start = ((), (), s32[]{:S(2)}) async-start(), calls=%async_computation.5 | async-start | bytes 23248896 | tf_op jit(solution)/shard_map/all_gather | solution.py:363
  149.0 481.9 %all-gather.24.cloned.1.call-start = ((), (), s32[]{:S(2)}) async-start(), calls=%async_computation.7 | async-start | bytes 23248896 | tf_op jit(solution)/shard_map/all_gather | solution.py:365
  149.7 634.1 %all-gather.26.cloned.1.call-start = ((), (), s32[]{:S(2)}) async-start(), calls=%async_computation.8 | async-start | bytes 8454144 | tf_op jit(solution)/shard_map/all_gather | solution.py:22
  152.0 390.2 %copy-start.75 = (bf16[128,8]{0,1:T(8,128)(2,1)}, bf16[128,8]{0,1:T(8,128)(2,1)S(1)}, u32[]{:S(2)}) copy-start(bf16[128,8]{0,1:T(8,128)(2,1)S(1)} %convolution_convert_fusion.3) | copy-start | bytes 6148
  696.6 685.0 %all-reduce.5.cloned.1.call-start = ((), (), s32[]{:S(2)}) async-start(), calls=%async_computation.9 | async-start | bytes 3145728 | tf_op jit(solution)/shard_map/psum | solution.py:477
  769.5 376.9 %copy-start.93 = (f32[2,4,1,64,1]{3,2,4,1,0:T(1,128)S(1)}, f32[2,4,1,64,1]{3,2,4,1,0:T(1,128)}, u32[]{:S(2)}) copy-start(f32[2,4,1,64,1]{3,2,4,1,0:T(1,128)} %copy-done.92) | copy-start | bytes 6148
  783.8 365.0 %copy-start.24 = (f32[2,64,4,64]{1,3,0,2:T(8,128)S(1)}, f32[2,64,4,64]{1,3,0,2:T(8,128)}, u32[]{:S(2)}) copy-start(f32[2,64,4,64]{1,3,0,2:T(8,128)} %copy-done.23) | copy-start | bytes 393220
  783.8 365.0 %copy-start.29 = (bf16[2,64,4,64]{3,2,1,0:T(4,128)(2,1)S(1)}, bf16[2,64,4,64]{3,2,1,0:T(4,128)(2,1)}, u32[]{:S(2)}) copy-start(bf16[2,64,4,64]{3,2,1,0:T(4,128)(2,1)} %copy-done.27) | copy-start | bytes 196612
  783.8 365.0 %copy-start.74 = (f32[2,64,4]{1,0,2:T(2,128)S(1)}, f32[2,64,4]{1,0,2:T(2,128)}, u32[]{:S(2)}) copy-start(f32[2,64,4]{1,0,2:T(2,128)} %copy-done.73) | copy-start | bytes 6148
  783.9 365.0 %copy-start.101 = (f32[2,64]{1,0:T(2,128)S(1)}, f32[2,64]{1,0:T(2,128)}, u32[]{:S(2)}) copy-start(f32[2,64]{1,0:T(2,128)} %copy-done.100) | copy-start | bytes 1540
  (93 other events, 1050.1 us)
Sparse Core Ops, SparseCore 0:
  10.8 67.1 all-gather.13
  80.8 61.0 all-gather.9
  146.6 67.8 all-gather.15
  217.4 67.6 all-gather.11
  287.9 67.6 all-gather.17
  358.5 87.4 all-gather.21
  449.0 89.4 all-gather.19
  541.5 89.3 all-gather.23
  696.7 69.7 all-gather.25
  1233.3 148.2 all-reduce.4
where the time goes:
time: 1420 us; the launch traced here: 1400 us
  other arithmetic  351 us (25%)
  waiting for transfers between devices  312 us (22%)
  blocking collectives  199 us (14%)
  local copies, waits for them, and re-layouts  192 us (14%)
  loops' own time  173 us (12%)
  matrix products  154 us (11%)
  between operations  18.5 us (1%)
    select_n x512, other arithmetic, step(): return jax.tree.map(lambda a, b: jnp.where(reached, a, b), new, before)  322 us
    another operation x2, loops' own time, entering(): return lax.fori_loop(0, peers, step, start)  173 us
    dynamic_slice x256, local copies, waits for them, and re-layouts, step(): part[at].astype(own.dtype)  150 us
    psum x1, waiting for transfers between devices, body(): lax.psum((gain_attn_grad, query_adapter_down_gradient, query_adapter_up_g...  146 us
    all_gather x2, blocking collectives, entering(): lax.all_gather(part.astype(kind), axis)  72.1 us
    dot_general x15, matrix products, product_flipped(): lax.dot_general(left, right, (((1,), (1,)), ((), ())), preferred_element_...  64 us
    psum x1, blocking collectives, body(): lax.psum((gain_attn_grad, query_adapter_down_gradient, query_adapter_up_g...  63.6 us
    unnamed x1, blocking collectives  63.5 us
  transfers between devices with their start and end apart: 10, of which 4 were waited for; matrix products, arithmetic and copies ran while one was open for 22% of the time, Pallas kernels for 0%

commit v1 on v0

--- a/solution.py
+++ b/solution.py
@@ -16,28 +16,28 @@
 HIGHEST = lax.Precision.HIGHEST
 
 
-def entering(array, axis, combine, identity, reverse):
-    peers, position = (lax.axis_size(axis), lax.axis_index(axis))
-    everything = jax.tree.map(
-        lambda part, kind: lax.all_gather(part.astype(kind), axis),
-        array,
-        jax.tree.map(lambda a: jnp.bfloat16 if a.dtype == jnp.float32 else a.dtype, array),
-    )
-    start = jax.tree.map(
-        lambda part, zero: jnp.broadcast_to(jnp.asarray(zero, part.dtype), part.shape),
-        array,
-        identity,
-    )
-
-    def step(k, before):
-        at = peers - 1 - k if reverse else k
-        reached = at > position if reverse else at < position
-        new = combine(
-            before, jax.tree.map(lambda part, own: part[at].astype(own.dtype), everything, array)
-        )
-        return jax.tree.map(lambda a, b: jnp.where(reached, a, b), new, before)
-
-    return lax.fori_loop(0, peers, step, start)
+def sequence_of(sequence_lengths, stretch_ids):
+    counts = (sequence_lengths + STRETCH - 1) // STRETCH
+    seq_ends = jnp.cumsum(counts)
+    return jnp.sum((stretch_ids[:, None] >= seq_ends[None]).astype(jnp.int32), 1)
+
+
+def entering(folded, sequence_lengths, stretches_dev, reverse):
+    peers, position = (lax.axis_size("seq"), lax.axis_index("seq"))
+    state, norm = (folded[0], folded[1])
+    packed = jnp.concatenate([state, norm[:, :, None]], 2).astype(jnp.bfloat16)
+    everything = lax.all_gather(packed.reshape(1, -1), "seq", axis=0, tiled=True)
+    devices = jnp.arange(peers)
+    firsts = sequence_of(sequence_lengths, devices * stretches_dev)
+    lasts = sequence_of(sequence_lengths, devices * stretches_dev + stretches_dev - 1)
+    if reverse:
+        reached = (devices > position) & (firsts == lasts[position])
+    else:
+        reached = (devices < position) & (lasts == firsts[position])
+    total = jnp.dot(
+        reached.astype(jnp.bfloat16)[None], everything, preferred_element_type=jnp.float32
+    ).reshape(packed.shape)
+    return (total[:, :, :HEAD_SIZE], total[:, :, HEAD_SIZE])
 
 
 def product_result(left, right):
@@ -174,6 +174,7 @@
     stretch_gates,
     valid_mask,
     score_scale,
+    sequence_lengths,
 ):
     stretches_dev = query5.shape[0]
     grad_heads = (
@@ -215,14 +216,13 @@
     norm_in_grad = jnp.einsum("ctkgf,ctkg->ckf", weighted, denom_tokens, precision=HIGHEST)
     suffix = entering(
         fold_local(
-            stretch_gates[:, None, None, None] * state_in_grad,
-            stretch_gates[:, None, None] * norm_in_grad,
-            stretch_gates,
+            state_in_grad,
+            norm_in_grad,
+            jnp.concatenate([stretch_gates[1:], stretch_gates[:1]]),
             True,
         ),
-        "seq",
-        combine,
-        identity_element(),
+        sequence_lengths,
+        stretches_dev,
         True,
     )
     carry_state, carry_norm = (suffix[0], suffix[1])
@@ -308,11 +308,16 @@
     normed_one = inputs * rms_one
     gain_one = attention_gain.astype(jnp.float32)
     hidden_first = (normed_one * gain_one).astype(jnp.bfloat16)
+    attention_rows = jnp.concatenate(
+        [query_weight, key_weight, value_weight, output_weight_flipped], 1
+    )
+    attention_all = lax.all_gather(attention_rows, "seq", axis=0, tiled=True)
+    width, narrow = (query_weight.shape[1], key_weight.shape[1])
     attention_whole = (
-        lax.all_gather(query_weight, "seq", axis=0, tiled=True),
-        lax.all_gather(key_weight, "seq", axis=0, tiled=True),
-        lax.all_gather(value_weight, "seq", axis=0, tiled=True),
-        lax.all_gather(output_weight_flipped, "seq", axis=0, tiled=True),
+        attention_all[:, :width],
+        attention_all[:, width : width + narrow],
+        attention_all[:, width + narrow : width + 2 * narrow],
+        attention_all[:, width + 2 * narrow :],
     )
 
     def apply_projection(weight_matrix, adapter_first_factor, adapter_second_factor):
@@ -340,9 +345,8 @@
     )
     prefix = entering(
         fold_local(stretch_state, stretch_norm, stretch_gates, False),
-        "seq",
-        combine,
-        identity_element(),
+        sequence_lengths,
+        stretches_dev,
         False,
     )
     states_in, norms_in = spread_states(prefix, stretch_state, stretch_norm, stretch_gates)
@@ -370,15 +374,8 @@
     swish_gate = gate_act * sigmoid_gate
     inner_act = (swish_gate * up_act).astype(jnp.bfloat16)
     block_out = (middle + product_flipped(inner_act, mlp_full[2])).astype(jnp.bfloat16)
-    w_q_all, w_k_all, w_v_all, output_weight_whole, w_g_all, w_u_all, w_d_all = (
-        lax.all_gather(query_weight, "seq", axis=0, tiled=True),
-        lax.all_gather(key_weight, "seq", axis=0, tiled=True),
-        lax.all_gather(value_weight, "seq", axis=0, tiled=True),
-        lax.all_gather(output_weight_flipped, "seq", axis=0, tiled=True),
-        lax.all_gather(gate_weight, "seq", axis=0, tiled=True),
-        lax.all_gather(up_weight, "seq", axis=0, tiled=True),
-        lax.all_gather(down_weight_flipped, "seq", axis=0, tiled=True),
-    )
+    w_q_all, w_k_all, w_v_all, output_weight_whole = attention_whole
+    w_g_all, w_u_all, w_d_all = mlp_full
     inner_grad = product_result(output_gradient, w_d_all).astype(jnp.bfloat16).astype(jnp.float32)
     gate_grad = (
         inner_grad * up_act * sigmoid_gate * (1.0 + gate_act * (1.0 - sigmoid_gate))
@@ -400,30 +397,16 @@
         product_result(branch_gradient, output_weight_whole)
         + product_flipped(output_adapter_gradient, output_adapter_down)
     ).astype(jnp.bfloat16)
-    key_again, masked_again, state_again, norm_again = key_side(
-        key4, value4, key_feature_map, valid_mask
-    )
-    prefix_again = entering(
-        fold_local(state_again, norm_again, stretch_gates, False),
-        "seq",
-        combine,
-        identity_element(),
-        False,
-    )
-    states_back, norms_back = spread_states(prefix_again, state_again, norm_again, stretch_gates)
-    qfeat_again, weights_again, damping_again, numer_again, denom_again = query_side(
-        query5, key4, value4, feat_q4, states_back, norms_back, allowed, score_scale
-    )
     kept_parts = (
-        key_again,
-        masked_again,
-        qfeat_again,
-        weights_again,
-        damping_again,
-        numer_again,
-        denom_again,
-        states_back,
-        norms_back,
+        key_feat,
+        key_masked,
+        query_feat,
+        weights_p,
+        damping,
+        numerator,
+        denominator,
+        states_in,
+        norms_in,
     )
     query_gradient, key_gradient, value_gradient, feat_query_grad, feat_key_grad = attention_back(
         heads_merged_gradient,
@@ -444,6 +427,7 @@
         stretch_gates,
         valid_mask,
         score_scale,
+        sequence_lengths,
     )
     query_adapter_gradient = (2.0 * product_flipped(query_gradient, query_adapter_up)).astype(
         jnp.bfloat16
@@ -474,23 +458,26 @@
         middle_grad
         + rms_one * (scaled_one - normed_one * jnp.mean(scaled_one * normed_one, -1, keepdims=True))
     ).astype(jnp.bfloat16)
-    summed = lax.psum(
-        (
-            gain_attn_grad,
-            query_adapter_down_gradient,
-            query_adapter_up_gradient,
-            key_adapter_down_gradient,
-            key_adapter_up_gradient,
-            value_adapter_down_gradient,
-            value_adapter_up_gradient,
-            output_adapter_down_gradient,
-            output_adapter_up_gradient,
-            feat_query_grad,
-            feat_key_grad,
-            gain_mlp_grad,
-        ),
-        "seq",
-    )
+    parts = (
+        gain_attn_grad,
+        query_adapter_down_gradient,
+        query_adapter_up_gradient,
+        key_adapter_down_gradient,
+        key_adapter_up_gradient,
+        value_adapter_down_gradient,
+        value_adapter_up_gradient,
+        output_adapter_down_gradient,
+        output_adapter_up_gradient,
+        feat_query_grad,
+        feat_key_grad,
+        gain_mlp_grad,
+    )
+    flat = jnp.concatenate([part.reshape(-1) for part in parts]).reshape(-1, 1024)
+    flat = lax.psum(flat, "seq").reshape(-1)
+    summed, at = ([], 0)
+    for part in parts:
+        summed.append(flat[at : at + part.size].reshape(part.shape))
+        at += part.size
     return (
         block_out,
         grad_tokens,

time: 1420 us -> 819 us (0.58)
  other arithmetic: 351 us -> 27.5 us
  blocking collectives: 199 us -> 0 us
  loops' own time: 173 us -> 0 us
  waiting for transfers between devices: 312 us -> 478 us
  local copies, waits for them, and re-layouts: 192 us -> 119 us
  matrix products: 154 us -> 172 us
    select_n x512 -> x0, other arithmetic: 322 us -> none  [step(): return jax.tree.map(lambda a, b: jnp.where(reached, a, b), new, before)]
    another operation x2 -> x0, loops' own time: 173 us -> none  [entering(): return lax.fori_loop(0, peers, step, start)]
    dynamic_slice x256 -> x2, local copies, waits for them, and re-layouts: 150 us -> 1.89 us  [the longest x1 1.31 us: entering(): reached = (devices > position) & (firsts == lasts[position])]
    all_gather x1, waiting for transfers between devices: 0.02 us -> 79.8 us  [body(): lax.all_gather(up_weight, 'seq', axis=0, tiled=True)]
    all_gather x2 -> x0, blocking collectives: 72.1 us -> none  [entering(): lax.all_gather(part.astype(kind), axis)]
    psum x1 -> x0, blocking collectives: 63.6 us -> none  [body(): lax.psum((gain_attn_grad, query_adapter_down_gradient, query_adapter_up_g...]
    unnamed x1 -> x0, blocking collectives: 63.5 us -> none
    dot_general x0 -> x5, local copies, waits for them, and re-layouts: none -> 49.4 us  [the longest x4 49.3 us: entering(): jnp.dot(reached.astype(jnp.bfloat16)[None], everything, preferred_element...]
  transfers between devices with their start and end apart: 10 -> 7, of which waited for: 4 -> 7; matrix products, arithmetic and copies ran while one was open for 22% -> 21% of each run, Pallas kernels for 0% -> 0%
where the time goes in v1:
time: 819 us; the launch traced here: 814 us
  waiting for transfers between devices  478 us (58%)
  matrix products  172 us (21%)
  local copies, waits for them, and re-layouts  119 us (15%)
  other arithmetic  27.5 us (3%)
  between operations  16.8 us (2%)
    psum x1, waiting for transfers between devices, body(): flat = lax.psum(flat, 'seq').reshape(-1)  143 us
    all_gather x1, waiting for transfers between devices, body(): attention_all = lax.all_gather(attention_rows, 'seq', axis=0, tiled=True)  81.7 us
    all_gather x1, waiting for transfers between devices, body(): lax.all_gather(up_weight, 'seq', axis=0, tiled=True)  79.8 us
    all_gather x2, waiting for transfers between devices, entering(): lax.all_gather(packed.reshape(1, -1), 'seq', axis=0, tiled=True)  70.4 us
    dot_general x15, matrix products, product_flipped(): lax.dot_general(left, right, (((1,), (1,)), ((), ())), preferred_element_...  66.2 us
    all_gather x1, waiting for transfers between devices, body(): lax.all_gather(down_weight_flipped, 'seq', axis=0, tiled=True)  63.8 us
    dot_general x15, matrix products, product_result(): return jnp.dot(left, right, preferred_element_type=jnp.float32)  53.4 us
    dot_general x4, local copies, waits for them, and re-layouts, entering(): jnp.dot(reached.astype(jnp.bfloat16)[None], everything, preferred_element...  49.3 us
  transfers between devices with their start and end apart: 7, of which 7 were waited for; matrix products, arithmetic and copies ran while one was open for 21% of the time, Pallas kernels for 0%

profile of v1, /device:TPU:1, one launch (start us, length us, event | category | flops | bytes accessed | tf_op | source)
XLA Modules:
  0.0 813.7 jit_solution(15221137706642955990)
XLA Ops:
  17.1 81.7 %all-gather.9.cloned.1.call-done = bf16[2048,4608]{1,0:T(8,128)(2,1)} async-done(((bf16[16,4608]{1,0:T(8,128)(2,1)}), bf16[2048,4608]{1,0:T(8,128)(2,1)}) %all-gather.9.cloned.1.call-update) | async-done | bytes 18874384 | tf_op jit(solution)/shard_map/all_gather | solution.py:314
  111.7 4.7 fusion.7
  127.4 63.8 %all-gather.15.cloned.1.call-done = bf16[2048,5632]{1,0:T(8,128)(2,1)} async-done(((bf16[16,5632]{1,0:T(8,128)(2,1)}), bf16[2048,5632]{1,0:T(8,128)(2,1)}) %all-gather.15.cloned.1.call-update) | async-done | bytes 23068688 | tf_op jit(solution)/shard_map/all_gather | solution.py:369
  191.2 12.5 %fusion.9 = f32[128,5632]{1,0:T(8,128)} fusion(bf16[128,2048]{1,0:T(8,128)(2,1)} %param.43, bf16[2048,5632]{1,0:T(8,128)(2,1)} %all-gather.15.cloned.1.call-done), kind=kOutput, calls=%fused_computation.10 | convolution fusion | flops 2954231808 | bytes 26476544 | tf_op jit(solution)/shard_map/dot_general | solution.py:44
  203.7 60.7 %all-gather.17.cloned.1.call-done = bf16[128,1,16640]{2,1,0:T(2,128)(2,1)} async-done(((bf16[1,1,16640]{2,1,0:T(2,128)(2,1)}), bf16[128,1,16640]{2,1,0:T(2,128)(2,1)}) %all-gather.17.cloned.1.call-update) | async-done | bytes 4259856 | tf_op jit(solution)/shard_map/all_gather | solution.py:29
  264.4 17.3 %copy.471 = bf16[128,1,16640]{0,2,1:T(8,128)(2,1)} copy(bf16[128,1,16640]{2,1,0:T(2,128)(2,1)} %all-gather.17.cloned.1.call-done) | data formatting | bytes 8519680 | tf_op jit(solution)/shard_map/dot_general | solution.py:37
  281.7 7.4 dot_general.205
  289.1 6.5 fusion.123
  301.0 4.3 fusion.26
  310.0 6.3 fusion.3
  316.8 37.9 %all-gather.11.cloned.1.call-done = bf16[2048,5632]{1,0:T(8,128)(2,1)} async-done(((bf16[16,5632]{1,0:T(8,128)(2,1)}), bf16[2048,5632]{1,0:T(8,128)(2,1)}) %all-gather.11.cloned.1.call-update) | async-done | bytes 23068688 | tf_op jit(solution)/shard_map/all_gather | solution.py:367
  354.7 12.4 %fusion.152 = f32[128,5632]{1,0:T(8,128)} fusion(bf16[2048,5632]{1,0:T(8,128)(2,1)} %all-gather.11.cloned.1.call-done, f32[128,2048]{1,0:T(8,128)S(1)} %get-tuple-element.143, f32[2048]{0:T(1024)S(1)} %convert_element_type.187, f32[128]{0:T(128)S(1)} %add_rsqrt_fusion), kind=kOutput, calls=%fused_computation.269 | convolution fusion | flops 2953576448 | bytes 27009536 | tf_op jit(solution)/shard_map/dot_general | solution.py:44
  367.1 79.8 %all-gather.13.cloned.1.call-done = bf16[2048,5632]{1,0:T(8,128)(2,1)} async-done(((bf16[16,5632]{1,0:T(8,128)(2,1)}), bf16[2048,5632]{1,0:T(8,128)(2,1)}) %all-gather.13.cloned.1.call-update) | async-done | bytes 23068688 | tf_op jit(solution)/shard_map/all_gather | solution.py:368
  446.9 12.4 %fusion.151 = f32[128,5632]{1,0:T(8,128)} fusion(bf16[2048,5632]{1,0:T(8,128)(2,1)} %all-gather.13.cloned.1.call-done, f32[128,2048]{1,0:T(8,128)S(1)} %get-tuple-element.143, f32[2048]{0:T(1024)S(1)} %convert_element_type.187, f32[128]{0:T(128)S(1)} %add_rsqrt_fusion), kind=kOutput, calls=%fused_computation.268 | convolution fusion | flops 2953576448 | bytes 27009536 | tf_op jit(solution)/shard_map/dot_general | solution.py:44
  459.3 15.3 %fusion.42 = f32[128,2048]{1,0:T(8,128)} fusion(bf16[2048,5632]{1,0:T(8,128)(2,1)} %all-gather.11.cloned.1.call-done, f32[128,5632]{1,0:T(8,128)} %fusion.152, f32[128,5632]{1,0:T(8,128)} %fusion.9, f32[128,5632]{1,0:T(8,128)} %fusion.151), kind=kOutput, calls=%fused_computation.73 | convolution fusion | flops 2959998976 | bytes 32768000 | tf_op jit(solution)/shard_map/dot_general | solution.py:54
  474.6 15.6 %multiply_reduce_fusion.1 = (f32[2048]{0:T(1024)}, f32[128]{0:T(128)S(1)}, f32[128,2048]{1,0:T(8,128)}) fusion(f32[128,2048]{1,0:T(8,128)S(1)} %get-tuple-element.143, f32[128]{0:T(128)S(1)} %add_rsqrt_fusion, f32[2048]{0:T(1024)S(1)} %convert_element_type.187, f32[128,2048]{1,0:T(8,128)} %fusion.42, bf16[2048,5632]{1,0:T(8,128)(2,1)} %all-gather.13.cloned.1.call-done, ...), kind=kOutput, calls=%fused_computation.130 | convolution fusion | flops 2958948352 | bytes 31998976 | tf_op jit(solution)/shard_map/dot_general | solution.py:54
  492.1 4.8 fusion.1
  555.9 6.3 fusion.5
  562.2 15.0 %fusion.14 = bf16[128,2048]{1,0:T(8,128)(2,1)} fusion(f32[128,2048]{1,0:T(8,128)S(1)} %get-tuple-element.143, bf16[2048,5632]{1,0:T(8,128)(2,1)} %all-gather.15.cloned.1.call-done, f32[128,5632]{1,0:T(8,128)} %fusion.151, f32[128,5632]{1,0:T(8,128)} %fusion.152), kind=kOutput, calls=%fused_computation.29 | convolution fusion | flops 2957639680 | bytes 30408704 | tf_op jit(solution)/shard_map/dot_general | solution.py:54
  577.2 9.7 %all-gather.19.cloned.1.call-done = bf16[128,1,16640]{2,1,0:T(2,128)(2,1)} async-done(((bf16[1,1,16640]{2,1,0:T(2,128)(2,1)}), bf16[128,1,16640]{2,1,0:T(2,128)(2,1)}) %all-gather.19.cloned.1.call-update) | async-done | bytes 4259856 | tf_op jit(solution)/shard_map/all_gather | solution.py:29
  586.8 17.2 %copy.472 = bf16[128,1,16640]{0,2,1:T(8,128)(2,1)} copy(bf16[128,1,16640]{2,1,0:T(2,128)(2,1)} %all-gather.19.cloned.1.call-done) | data formatting | bytes 8519680 | tf_op jit(solution)/shard_map/dot_general | solution.py:37
  604.1 7.5 dot_general.231
  611.6 6.5 fusion.121
  648.4 143.0 %all-reduce.2.cloned.1.call-done = f32[248,1024]{1,0:T(8,128)} async-done(((f32[248,1024]{1,0:T(8,128)}), f32[248,1024]{1,0:T(8,128)}) %all-reduce.2.cloned.1.call-update) | async-done | bytes 1015824 | tf_op jit(solution)/shard_map/psum | solution.py:476
  (370 shorter events, 148.7 us)
Async XLA Ops:
  7.2 112.7 %copy-start = (bf16[32,64,64]{2,1,0:T(8,128)(2,1)S(1)}, bf16[32,64,64]{2,1,0:T(8,128)(2,1)}, u32[]{:S(2)}) copy-start(bf16[32,64,64]{2,1,0:T(8,128)(2,1)} %param.37) | copy-start | bytes 786436
  7.2 9.6 %copy-start.1 = (bf16[128,2048]{1,0:T(8,128)(2,1)S(1)}, bf16[128,2048]{1,0:T(8,128)(2,1)}, u32[]{:S(2)}) copy-start(bf16[128,2048]{1,0:T(8,128)(2,1)} %param.22) | copy-start | bytes 1572868
  7.2 9.6 %copy-start.69 = (bf16[2048,8]{0,1:T(8,128)(2,1)S(1)}, bf16[2048,8]{0,1:T(8,128)(2,1)}, u32[]{:S(2)}) copy-start(bf16[2048,8]{0,1:T(8,128)(2,1)} %param.33) | copy-start | bytes 98308
  7.2 91.5 %all-gather.9.cloned.1.call-start = ((), (), s32[]{:S(2)}) async-start(), calls=%async_computation | async-start | bytes 19021824 | tf_op jit(solution)/shard_map/all_gather | solution.py:314
  8.9 182.2 %all-gather.15.cloned.1.call-start = ((), (), s32[]{:S(2)}) async-start(), calls=%async_computation.3 | async-start | bytes 23248896 | tf_op jit(solution)/shard_map/all_gather | solution.py:369
  9.7 254.7 %all-gather.17.cloned.1.call-start = ((), (), s32[]{:S(2)}) async-start(), calls=%async_computation.5 | async-start | bytes 8586240 | tf_op jit(solution)/shard_map/all_gather | solution.py:29
  15.3 96.4 %copy-start.84 = (f32[128]{0:T(128)}, f32[128]{0:T(128)S(1)}, u32[]{:S(2)}) copy-start(f32[128]{0:T(128)S(1)} %add_rsqrt_fusion.1) | copy-start | bytes 1540
  15.4 87.8 %copy-start.92 = (f32[2,64]{1,0:T(2,128)}, f32[2,64]{1,0:T(2,128)S(1)}, u32[]{:S(2)}) copy-start(f32[2,64]{1,0:T(2,128)S(1)} %get-tuple-element.108) | copy-start | bytes 1540
  15.4 85.0 %copy-start.81 = (bf16[8,256]{1,0:T(8,128)(2,1)S(1)}, bf16[8,256]{1,0:T(8,128)(2,1)}, u32[]{:S(2)}) copy-start(bf16[8,256]{1,0:T(8,128)(2,1)} %param.34) | copy-start | bytes 12292
  16.8 85.5 %copy-start.91 = (bf16[128,8]{0,1:T(8,128)(2,1)}, bf16[128,8]{0,1:T(8,128)(2,1)S(1)}, u32[]{:S(2)}) copy-start(bf16[128,8]{0,1:T(8,128)(2,1)S(1)} %convolution_convert_fusion.4) | copy-start | bytes 6148
  17.1 85.2 %copy-start.89 = (bf16[128,8]{0,1:T(8,128)(2,1)}, bf16[128,8]{0,1:T(8,128)(2,1)S(1)}, u32[]{:S(2)}) copy-start(bf16[128,8]{0,1:T(8,128)(2,1)S(1)} %convolution_convert_fusion.2) | copy-start | bytes 6148
  17.1 85.2 %copy-start.79 = (bf16[8,256]{1,0:T(8,128)(2,1)S(1)}, bf16[8,256]{1,0:T(8,128)(2,1)}, u32[]{:S(2)}) copy-start(bf16[8,256]{1,0:T(8,128)(2,1)} %param.32) | copy-start | bytes 12292
  102.9 13.6 %copy-start.21 = (bf16[2,64,4,64]{1,3,0,2:T(8,128)(2,1)}, bf16[2,64,4,64]{1,3,0,2:T(8,128)(2,1)S(1)}, u32[]{:S(2)}) copy-start(bf16[2,64,4,64]{1,3,0,2:T(8,128)(2,1)S(1)} %copy.398) | copy-start | bytes 196612
  106.7 248.1 %all-gather.11.cloned.1.call-start = ((), (), s32[]{:S(2)}) async-start(), calls=%async_computation.1 | async-start | bytes 23248896 | tf_op jit(solution)/shard_map/all_gather | solution.py:367
  107.2 339.7 %all-gather.13.cloned.1.call-start = ((), (), s32[]{:S(2)}) async-start(), calls=%async_computation.2 | async-start | bytes 23248896 | tf_op jit(solution)/shard_map/all_gather | solution.py:368
  107.8 479.0 %all-gather.19.cloned.1.call-start = ((), (), s32[]{:S(2)}) async-start(), calls=%async_computation.6 | async-start | bytes 8586240 | tf_op jit(solution)/shard_map/all_gather | solution.py:29
  121.8 179.2 %copy-start.2 = (f32[4,8,2,64,64]{3,4,1,0,2:T(8,128)}, f32[4,8,2,64,64]{3,4,1,0,2:T(8,128)S(1)}, u32[]{:S(2)}) copy-start(f32[4,8,2,64,64]{3,4,1,0,2:T(8,128)S(1)} %get-tuple-element.137) | copy-start | bytes 3145732
  289.1 8.5 %copy-start.35 = (f32[2,64,4,8]{1,3,2,0:T(8,128)S(1)}, f32[2,64,4,8]{1,3,2,0:T(8,128)}, u32[]{:S(2)}) copy-start(f32[2,64,4,8]{1,3,2,0:T(8,128)} %copy-done.34) | copy-start | bytes 49156
  289.1 8.5 %copy-start.47 = (f32[2,64,4,8]{1,3,2,0:T(8,128)S(1)}, f32[2,64,4,8]{1,3,2,0:T(8,128)}, u32[]{:S(2)}) copy-start(f32[2,64,4,8]{1,3,2,0:T(8,128)} %fusion.37) | copy-start | bytes 49156
  316.8 157.8 %copy-start.83 = (f32[128]{0:T(128)}, f32[128]{0:T(128)S(1)}, u32[]{:S(2)}) copy-start(f32[128]{0:T(128)S(1)} %add_rsqrt_fusion) | copy-start | bytes 1540
  491.9 28.0 %copy-start.9 = (f32[128,2048]{1,0:T(8,128)}, f32[128,2048]{1,0:T(8,128)S(1)}, u32[]{:S(2)}) copy-start(f32[128,2048]{1,0:T(8,128)S(1)} %multiply_add_fusion) | copy-start | bytes 3145732
  517.0 274.3 %all-reduce.2.cloned.1.call-start = ((), (), s32[]{:S(2)}) async-start(), calls=%async_computation.4 | async-start | bytes 2031616 | tf_op jit(solution)/shard_map/psum | solution.py:476
  630.6 9.1 %copy-start.44 = (f32[16384]{0:T(1024)S(1)}, f32[16384]{0:T(1024)}, u32[]{:S(2)}) copy-start(f32[16384]{0:T(1024)} %reshape.425) | copy-start | bytes 196612
  631.2 9.1 %copy-start.46 = (f32[1,16,8,128]{3,1,2,0:T(8,128)S(1)}, f32[1,16,8,128]{3,1,2,0:T(8,128)}, u32[]{:S(2)}) copy-start(f32[1,16,8,128]{3,1,2,0:T(8,128)} %copy.476) | copy-start | bytes 196612
  (81 other events, 287.1 us)
Sparse Core Ops, SparseCore 0:
  11.7 86.9 all-gather.8
  101.7 89.4 all-gather.14
  194.7 69.6 all-gather.16
  267.2 87.4 all-gather.10
  357.5 89.3 all-gather.12
  517.2 69.6 all-gather.18
  647.3 144.0 all-reduce.1

commit v2 on v1

v2 whole, which is shorter than its diff:
```python
import math

import jax
import jax.numpy as jnp
from jax import lax
from jax.experimental import pallas as pl
from jax.experimental.pallas import tpu as pltpu
from jax.sharding import PartitionSpec as P

QUERY_HEADS = 32
KEY_VALUE_HEADS = 4
HEAD = 64
STRETCH = 64
WIDTH = 2048
FF = 5632
ROWS = 128
CHIP = 256
HALF = 1024
NARROW = 128
QKV = HALF + 2 * NARROW
ATT = QKV + HALF
SLICE = FF // 4
AUG = 80
RANK = 8
PIECE = 1280
EPSILON = 1e-05
MESH = pl.DeviceIdType.MESH
F32 = jnp.float32
BF = jnp.bfloat16

SHARES = (
    (1, 0, 0, 64, 128),
    (3, 0, 64, 64, 192),
    (0, 1, 0, 64, 256),
    (0, 3, 64, 64, 320),
    (1, 1, 0, 32, 384),
    (1, 3, 32, 32, 416),
    (3, 1, 64, 32, 448),
    (3, 3, 96, 32, 480),
)


def nn(left, right):
    return jnp.dot(left, right, preferred_element_type=F32)


def nt(left, right):
    return lax.dot_general(left, right, (((1,), (1,)), ((), ())), preferred_element_type=F32)


def wrap(value):
    return lax.rem(value, 4)


class Copies:
    def __init__(self, send, recv):
        self.send, self.recv, self.count, self.open = send, recv, 0, []

    def start(self, src, dst, device):
        copy = pltpu.make_async_remote_copy(
            src_ref=src,
            dst_ref=dst,
            send_sem=self.send.at[self.count],
            recv_sem=self.recv.at[self.count],
            device_id=(device,),
            device_id_type=MESH,
        )
        self.count += 1
        copy.start()
        self.open.append(copy)
        return copy

    def sent(self, copies):
        for copy in copies:
            copy.wait_send()
            self.open = [k for k in self.open if k is not copy]

    def drain(self):
        for copy in self.open:
            copy.wait_send()


class Stream:
    def __init__(self, copies, view, where, device, parts, rings):
        self.copies, self.view, self.where, self.device = copies, view, where, device
        self.parts, self.rings = parts, rings
        self.flying = {}

    def block(self, order, phase, at, first, count):
        index = {}
        for k, axis in enumerate(order):
            if k < phase:
                index[axis] = slice(None)
            elif k == phase:
                index[axis] = at
            else:
                index[axis] = self.where[axis]
        return self.view(index, first, count)

    def begin(self, phase):
        for part, (order, first, count) in enumerate(self.parts):
            axis = order[phase]
            ring = self.rings[axis]
            own = self.block(order, phase, self.where[axis], first, count)
            if ring == 2:
                steps = (2,)
            else:
                steps = (1, 3)
            self.flying[phase, part] = [
                self.copies.start(own, own, self.device({axis: step})) for step in steps
            ]

    def middle(self, phase):
        for part, (order, first, count) in enumerate(self.parts):
            axis = order[phase]
            if self.rings[axis] == 2:
                continue
            flying = self.flying[phase, part]
            for copy in flying:
                copy.wait_recv()
            one = (count // 256) * 128
            left = self.block(order, phase, wrap(self.where[axis] + 3), first, one)
            right = self.block(order, phase, wrap(self.where[axis] + 1), first + one, count - one)
            self.flying[phase, part] = [
                self.copies.start(left, left, self.device({axis: 1})),
                self.copies.start(right, right, self.device({axis: 3})),
            ]

    def end(self, phase):
        for part in range(len(self.parts)):
            for copy in self.flying[phase, part]:
                copy.wait_recv()


def kernel(
    tok, og, qw, kw, vw, ow, gw, uw, dw, aall, ball, oac, ob2, fq_t, fq, fk_t, fk, gain1, gain2, bias, vrow, scal,
    blk_out, gtok_out, red_out,
    wa, wf, tok2, hid1, low, qt, kt, vt, knat, vnat, kfeat, st, comb, comb_t, wts, qfeat, mixf, damp, den, mixn, lowo,
    outs, outr, mid, ht, ogx, gg, inner, ug, rbt, rbb, mgrad, bg, ngt, dgr, sig, qlg, gt, gnat, lowg, ones,
    kacc, vacc, fsend, frecv, hsend, hrecv, red, rr, rz, fin, apart, asib, send, recv, loc,
):
    me = lax.axis_index("seq")
    c = lax.rem(me, 2)
    y = lax.rem(me // 2, 4)
    x = lax.rem(me // 8, 4)
    z = me // 32

    def device(steps):
        zz, xx, yy = (wrap(v + steps.get(n, 0)) for n, v in (("z", z), ("x", x), ("y", y)))
        return ((zz * 4 + xx) * 4 + yy) * 2 + c

    sibling = me + 1 - 2 * c
    plane = x * 4 + y
    xl, yl = lax.rem(x, 2), lax.rem(y, 2)
    xh, yh = x // 2, y // 2

    barrier = pltpu.get_barrier_semaphore()
    peers = [sibling]
    peers += [device({"x": i, "y": j}) for i in range(4) for j in range(4) if i + j > 0]
    peers += [device({"z": i}) for i in (1, 2, 3)]
    for peer in peers:
        pl.semaphore_signal(barrier, inc=1, device_id=(peer,), device_id_type=MESH)
    pl.semaphore_wait(barrier, len(peers))

    copies = Copies(send, recv)
    local = []

    def here(src, dst):
        copy = pltpu.make_async_copy(src, dst, loc.at[len(local)])
        copy.start()
        local.append(copy)

    first = []
    own = wa.at[z, x, y, c]
    for src, at, count in ((qw, 0, HALF), (kw, HALF, NARROW), (vw, HALF + NARROW, NARROW), (ow, QKV, HALF)):
        mine = src.at[:, pl.ds(pl.multiple_of(c * count, count), count)]
        other = src.at[:, pl.ds(pl.multiple_of((1 - c) * count, count), count)]
        dst = own.at[:, pl.ds(at, count)]
        here(mine, dst)
        first.append(copies.start(other, dst, sibling))
    start_ff = []
    ff_own = wf.at[z, xh, xl, yh, yl, c]
    for slot, src in enumerate((gw, uw, dw)):
        dst = ff_own.at[:, pl.ds(slot * SLICE, SLICE)]
        here(src.at[:, pl.ds(pl.multiple_of((xl * 2 + yl) * SLICE, 128), SLICE)], dst)
        for i, j in ((1, 0), (0, 1), (1, 1)):
            tx, ty = lax.rem(xl + i, 2), lax.rem(yl + j, 2)
            chip = (z * 4 + xh * 2 + tx) * 4 + yh * 2 + ty
            cols = pl.ds(pl.multiple_of((tx * 2 + ty) * SLICE, 128), SLICE)
            start_ff.append(copies.start(src.at[:, cols], dst, chip * 2 + c))
    tok_copy = copies.start(tok, tok2.at[c], sibling)
    here(tok, tok2.at[c])
    here(og, ogx.at[pl.ds(0, ROWS)])

    for copy in local:
        copy.wait()
    for copy in first:
        copy.wait_recv()

    def att_view(index, at, count):
        return wa.at[index["z"], index["x"], index["y"], :, :, pl.ds(at, count)]

    def ff_view(index, at, count):
        return wf.at[index["z"], index["x"], :, index["y"], :, c, :, pl.ds(at, count)]

    where_a = {"z": z, "x": x, "y": y}
    where_f = {"z": z, "x": xh, "y": yh}
    ring_a = {"z": 4, "x": 4, "y": 4}
    ring_f = {"z": 4, "x": 2, "y": 2}
    orders = (("y", "x", "z"), ("x", "z", "y"), ("z", "y", "x"))
    s_qkv = Stream(
        copies, att_view, where_a, device,
        ((orders[0], 0, 512), (orders[1], 512, 384), (orders[2], 896, 384)), ring_a,
    )
    s_o = Stream(
        copies, att_view, where_a, device,
        ((orders[0], 1280, 256), (orders[1], 1536, 384), (orders[2], 1920, 384)), ring_a,
    )
    s_d = Stream(
        copies, ff_view, where_f, device,
        ((orders[0], 2816, 512), (orders[1], 3328, 384), (orders[2], 3712, 512)), ring_f,
    )
    s_gu = Stream(
        copies, ff_view, where_f, device,
        ((orders[0], 0, 1024), (orders[1], 1024, 896), (orders[2], 1920, 896)), ring_f,
    )
    s_qkv.begin(0)
    s_qkv.middle(0)
    s_o.begin(0)
    s_qkv.end(0)
    s_qkv.begin(1)

    tok_copy.wait_recv()

    def norm_rows(i, carry):
        rows = pl.ds(i * 32, 32)
        for half in range(2):
            t = tok2[half, rows, :].astype(F32)
            r = lax.rsqrt(jnp.mean(t * t, -1, keepdims=True) + EPSILON)
            hid1[pl.ds(half * ROWS + i * 32, 32), :] = (t * r * gain1[...]).astype(BF)
        return carry

    lax.fori_loop(0, ROWS // 32, norm_rows, 0)
    low[...] = nn(hid1[...], aall[...]).astype(BF)

    s_o.middle(0)
    s_qkv.middle(1)
    s_o.end(0)
    s_qkv.end(1)
    s_qkv.begin(2)
    s_o.begin(1)
    s_o.middle(1)
    s_o.end(1)
    for copy in start_ff:
        copy.wait_recv()
    s_d.begin(0)
    s_qkv.middle(2)
    s_qkv.end(2)
    s_o.begin(2)
    s_d.middle(0)

    kv = nn(hid1[...], wa[:, :, :, :, :, HALF:QKV].reshape(WIDTH, 2 * NARROW))
    kv = (kv + nn(low[...], ball[:, HALF:QKV])).astype(BF)
    kv_t = kv.astype(F32).T.astype(BF)
    lane = lax.broadcasted_iota(jnp.int32, (1, 128), 1)
    low_lane = lane < 64
    for g in range(2):
        keep = low_lane if g == 0 else ~low_lane
        knat[g] = jnp.where(keep, kv[:, :NARROW], jnp.zeros((), BF))
        vnat[g] = jnp.where(keep, kv[:, NARROW:], jnp.zeros((), BF))
        kt[g] = kv_t[g * HEAD : (g + 1) * HEAD]
        tail = lax.broadcasted_iota(jnp.int32, (64, CHIP), 0) == 0
        vt[g, :HEAD] = kv_t[NARROW + g * HEAD : NARROW + (g + 1) * HEAD]
        vt[g, HEAD:] = tail.astype(F32).astype(BF)
    lanes4 = lax.broadcasted_iota(jnp.int32, (1, CHIP), 1) // STRETCH

    def softmax_rows(logits):
        e = jnp.exp(logits - jnp.max(logits, 0, keepdims=True))
        return e / jnp.sum(e, 0, keepdims=True)

    for g in range(2):
        kfeat[g * HEAD : (g + 1) * HEAD] = softmax_rows(nn(fk_t[g], kt[g])) * vrow[:1]
    kf = kfeat[...]
    kf_high = kf.astype(BF)
    kf_rest = (kf - kf_high.astype(F32)).astype(BF)
    for s in range(4):
        got = []
        for g in range(2):
            va = jnp.where(lanes4 == s, vt[g, :AUG], jnp.zeros((), BF))
            got.append(nt(va, kf_high) + nt(va, kf_rest))
        st[s] = jnp.where(low_lane, got[0], got[1])

    def gather_plane(base, folded, slots):
        fsend[base] = folded.astype(BF)
        fly = []
        for i in range(4):
            for j in range(4):
                if i + j > 0:
                    fly.append(copies.start(fsend.at[base], frecv.at[base, plane], device({"x": i, "y": j})))
        frecv[base, plane] = folded.astype(BF)
        return fly

    def fold_plane(base, fly, near, total):
        for copy in fly:
            copy.wait_recv()
        part = jnp.zeros((AUG, 128), F32)
        whole = jnp.zeros((AUG, 128), F32)
        for k in range(16):
            f = frecv[base, k].astype(F32)
            part += scal[near + k] * f
            whole += scal[total + k] * f
        hsend[base] = whole.astype(BF)
        fly = [copies.start(hsend.at[base], hrecv.at[base, i - 1], device({"z": i})) for i in (1, 2, 3)]
        return part, fly

    def fold_line(base, part, fly, far):
        for i, copy in zip((1, 2, 3), fly):
            copy.wait_recv()
            part += scal[far + wrap(z + 4 - i)] * hrecv[base, i - 1].astype(F32)
        return part

    gates = [scal[80 + s] for s in range(4)]
    folded = st[0]
    for s in (1, 2, 3):
        folded = st[s] + gates[s] * folded
    fly = gather_plane(0, folded, None)

    def query_columns(n, carry):
        cols = pl.ds(pl.multiple_of(n * 256, 256), 256)
        q = nn(hid1[...], wa[:, :, :, :, :, cols].reshape(WIDTH, 256)) + nn(low[...], ball[:, cols])
        qt[cols, :] = q.T.astype(BF)
        return carry

    lax.fori_loop(0, 4, query_columns, 0)
    part, fly = fold_plane(0, fly, 0, 16)
    s_o.middle(2)
    s_d.end(0)
    s_d.begin(1)
    prefix = fold_line(0, part, fly, 32)

    def combine(states):
        for g in range(2):
            for p in range(2):
                one, two = states[2 * p], states[2 * p + 1]
                if g == 0:
                    both = jnp.where(low_lane, one, pltpu.roll(two, 64, 1))
                else:
                    both = jnp.where(low_lane, pltpu.roll(one, 64, 1), two)
                yield g * 2 + p, both

    def put_states(states, base):
        for k, both in combine(states):
            comb[base + k] = both.astype(BF)
            tall = jnp.concatenate([both, jnp.zeros((128 - AUG, 128), F32)], 0)
            comb_t[base + k] = tall.T.astype(BF)

    states = [prefix]
    for s in (1, 2, 3):
        states.append(gates[s] * (states[s - 1] + st[s - 1]))
    put_states(states, 0)

    zero_low = jnp.zeros((), BF)

    def head_forward(h, carry):
        g = h // 8
        rows = pl.ds(pl.multiple_of(h * HEAD, HEAD), HEAD)
        logits = nn(fq_t[h], qt[rows, :])
        feat = softmax_rows(logits)
        qfeat[rows, :] = feat
        for p in range(2):
            cols = slice(p * 128, (p + 1) * 128)
            q = qt[rows, cols]
            scores = nn(knat[g, cols, :], jnp.concatenate([q, q], 0)) * 0.125 + bias[p]
            peak = jnp.max(scores, 0, keepdims=True)
            w = jnp.exp(scores - peak).astype(BF)
            wts[h * 2 + p] = w
            dm = jnp.exp(-peak)
            dq = (feat[:, cols] * dm).astype(BF)
            stack = jnp.concatenate(
                [w, jnp.where(low_lane, dq, zero_low), jnp.where(low_lane, zero_low, dq)], 0
            )
            lhs = jnp.concatenate([vt[g, :AUG, cols], comb[g * 2 + p]], 1)
            both = nn(lhs, stack)
            rden = 1.0 / both[HEAD : HEAD + 1]
            damp[h * 2 + p, :1] = dm
            den[h * 2 + p, :1] = rden
            mixf[rows, cols] = both[:HEAD] * rden
        return carry

    lax.fori_loop(0, 8, head_forward, 0)
    s_o.end(2)
    s_d.middle(1)
    s_d.end(1)
    s_d.begin(2)
    s_gu.begin(0)
    s_gu.middle(0)
    def share(src, dst):
        return [
            copies.start(src.at[pl.ds(r, n)], dst.at[pl.ds(at, n)], device({"x": i, "y": j}))
            for i, j, r, n, at in SHARES
        ]

    og_fly = share(og, ogx)
    lax.fori_loop(8, 16, head_forward, 0)
    s_gu.end(0)
    s_gu.begin(1)

    def mix_rows(n, carry):
        cols = pl.ds(pl.multiple_of(n * 256, 256), 256)
        mixn[:, cols] = mixf[cols, :].T.astype(BF)
        return carry

    lax.fori_loop(0, 4, mix_rows, 0)
    lowo[...] = nn(mixn[...], oac[...]).astype(BF)

    def out_columns(n, carry):
        cols = pl.ds(pl.multiple_of(n * 256, 256), 256)
        w = wa[n // 2, pl.ds(pl.multiple_of(lax.rem(n, 2) * 2, 2), 2), :, :, :, QKV:ATT].reshape(256, HALF)
        o = nt(mixn[...], w) + nn(lowo[...], ob2[:, cols])
        mine = jnp.where(c == 0, o[:ROWS], o[ROWS:])
        other = jnp.where(c == 0, o[ROWS:], o[:ROWS])
        mid[:, cols] = mine + tok[:, cols].astype(F32)
        outs[:, cols] = other.astype(BF)
        return carry

    lax.fori_loop(0, 8, out_columns, 0)
    out_copy = copies.start(outs, outr, sibling)
    s_d.middle(2)
    s_d.end(2)
    s_gu.middle(1)
    s_gu.end(1)
    s_gu.begin(2)
    out_copy.wait_recv()

    def middle_rows(i, carry):
        rows = pl.ds(i * 32, 32)
        m = mid[rows, :] + outr[rows, :].astype(F32)
        mid[rows, :] = m
        r = lax.rsqrt(jnp.mean(m * m, -1, keepdims=True) + EPSILON)
        ht[rows, :] = (m * r * gain2[...]).astype(BF)
        return carry

    lax.fori_loop(0, ROWS // 32, middle_rows, 0)
    ht_fly = share(ht, ht)

    def die(at, count):
        v = wf.at[:, :, :, :, :, c, :, pl.ds(at, count)]
        return copies.start(v, v, sibling)

    d_die = die(2 * SLICE, SLICE)
    for copy in og_fly:
        copy.wait_recv()
    d_die.wait_recv()

    def ff_cols(first, count):
        return wf[:, :, :, :, :, :, :, pl.ds(first, count)].reshape(WIDTH, count)

    def inner_columns(at, count):
        gg[:, pl.ds(at, count)] = nn(ogx[...], ff_cols(2 * SLICE + at, count)).astype(BF)

    def chunks(fn):
        def step(n, carry):
            fn(pl.multiple_of(n * 256, 256), 256)
            return carry

        lax.fori_loop(0, 5, step, 0)
        fn(1280, 128)

    chunks(inner_columns)
    s_gu.middle(2)
    s_gu.end(2)
    gu_die = die(0, 2 * SLICE)
    for copy in ht_fly:
        copy.wait_recv()
    gu_die.wait_recv()

    def gate_columns(at, count):
        cols = pl.ds(at, count)
        gate = nn(ht[...], ff_cols(at, count))
        up = nn(ht[...], ff_cols(SLICE + at, count))
        s = 1.0 / (1.0 + jnp.exp(-gate))
        swish = gate * s
        inner[:, cols] = (swish * up).astype(BF)
        d = gg[:, cols].astype(F32)
        gg[:, cols] = (d * up * s * (1.0 + gate * (1.0 - s))).astype(BF)
        ug[:, cols] = (d * swish).astype(BF)

    chunks(gate_columns)

    def ff_rows(n, at):
        return wf[n // 2, lax.rem(n, 2), :, :, :, :, :, pl.ds(at, SLICE)].reshape(256, SLICE)

    copies.sent(ht_fly)
    copies.sent(og_fly)

    def two_columns(n, carry):
        cols = pl.ds(pl.multiple_of(n * 256, 256), 256)
        ogx[:, cols] = (nt(gg[...], ff_rows(n, 0)) + nt(ug[...], ff_rows(n, SLICE))).astype(BF)
        return carry

    def give_back(src, dst, cols):
        return [
            copies.start(src.at[pl.ds(at, n), cols], dst.at[k // 2 - (k > 5), pl.ds(r, n), cols], device({"x": (4 - i) % 4, "y": (4 - j) % 4}))
            for k, (i, j, r, n, at) in enumerate(SHARES)
        ]

    two_fly = []
    for q in range(4):
        lax.fori_loop(2 * q, 2 * q + 2, two_columns, 0)
        two_fly += give_back(ogx, rbt, pl.ds(q * 512, 512))

    def block_columns(n, carry):
        cols = pl.ds(pl.multiple_of(n * 256, 256), 256)
        ht[:, cols] = nt(inner[...], ff_rows(n, 2 * SLICE)).astype(BF)
        return carry

    lax.fori_loop(0, 8, block_columns, 0)
    for copy in two_fly:
        copy.wait_recv()
    blk_fly = give_back(ht, rbb, pl.ds(0, WIDTH))

    def middle_back(i, acc):
        rows = pl.ds(i * 16, 16)
        t = ogx[rows, :].astype(F32)
        for k in range(3):
            t += rbt[k, rows, :].astype(F32)
        m = mid[rows, :]
        r = lax.rsqrt(jnp.mean(m * m, -1, keepdims=True) + EPSILON)
        n = m * r
        acc += jnp.sum(t * n, 0, keepdims=True)
        t = t * gain2[...]
        g = og[rows, :].astype(F32) + r * (t - n * jnp.mean(t * n, -1, keepdims=True))
        mgrad[rows, :] = g
        bg[c, rows, :] = g.astype(BF)
        return acc

    gain_mlp = lax.fori_loop(0, ROWS // 16, middle_back, jnp.zeros((1, WIDTH), F32))
    bg_copy = copies.start(bg.at[c], bg.at[c], sibling)
    bg_copy.wait_recv()
    bgv = bg.at[:, :, :]
    olg = nt(bgv[...].reshape(CHIP, WIDTH), ob2[...])
    olg_low = olg.astype(BF)

    def mixed_columns(n, carry):
        cols = pl.ds(pl.multiple_of(n * 256, 256), 256)
        wcols = pl.ds(pl.multiple_of(QKV + n * 256, 256), 256)
        m = nn(bg[...].reshape(CHIP, WIDTH), wa[:, :, :, :, :, wcols].reshape(WIDTH, 256))
        m += nt(olg_low, oac[cols, :])
        ngt[cols, :] = m.T.astype(BF)
        return carry

    lax.fori_loop(0, 4, mixed_columns, 0)
    lowo_t = lowo[...].astype(F32).T.astype(BF)
    olg_t = olg.T.astype(BF)
    apart[24:32] = 2.0 * nn(lowo_t[:16], bg[...].reshape(CHIP, WIDTH))[:8]
    red[72:80, :HALF] = nn(olg_t[:16], mixn[...])[:8]

    for k in range(4):
        sig[k] = jnp.zeros((AUG, 128), F32)

    def head_states(h, carry):
        g = h // 8
        rows = pl.ds(pl.multiple_of(h * HEAD, HEAD), HEAD)
        for p in range(2):
            cols = slice(p * 128, (p + 1) * 128)
            rden = den[h * 2 + p, :1]
            m = ngt[rows, cols].astype(F32)
            ng = (m * rden).astype(BF)
            dg = -jnp.sum(m * mixf[rows, cols], 0, keepdims=True) * rden
            ngt[rows, cols] = ng
            dgr[h * 2 + p, :1] = dg
            dq = (qfeat[rows, cols] * damp[h * 2 + p, :1]).astype(BF)
            stack = jnp.concatenate([jnp.where(low_lane, dq, zero_low), jnp.where(low_lane, zero_low, dq)], 0)
            tail = jnp.where(lax.broadcasted_iota(jnp.int32, (AUG - HEAD, 128), 0) == 0, dg, 0.0).astype(BF)
            sig[g * 2 + p] = sig[g * 2 + p] + nt(jnp.concatenate([ng, tail], 0), stack)
        return carry

    lax.fori_loop(0, 16, head_states, 0)
    sg_states = []
    for p in range(2):
        a, b = sig[p], sig[2 + p]
        sg_states.append(jnp.where(low_lane, a, pltpu.roll(b, 64, 1)))
        sg_states.append(jnp.where(low_lane, pltpu.roll(a, 64, 1), b))
    for s in range(4):
        st[s] = sg_states[s]
    folded = sg_states[3]
    for s in (2, 1, 0):
        folded = sg_states[s] + gates[s + 1] * folded
    fly = gather_plane(1, folded, None)

    for k in range(4):
        kacc[k] = jnp.zeros((HEAD, 128), F32)
        vacc[k] = jnp.zeros((HEAD, 128), F32)

    def head_back(h, carry):
        g = h // 8
        rows = pl.ds(pl.multiple_of(h * HEAD, HEAD), HEAD)
        for p in range(2):
            cols = slice(p * 128, (p + 1) * 128)
            ng = ngt[rows, cols]
            dg = dgr[h * 2 + p, :1]
            w = wts[h * 2 + p]
            pt = nn(vnat[g, cols, :], jnp.concatenate([ng, ng], 0)) + dg
            sgr = (w.astype(F32) * pt).astype(BF)
            tail = jnp.where(lax.broadcasted_iota(jnp.int32, (HEAD, 128), 0) == 0, dg, 0.0).astype(BF)
            both = nn(comb_t[g * 2 + p], jnp.concatenate([ng, tail], 0))
            qg = jnp.where(low_lane, both[:HEAD], both[HEAD:]) * damp[h * 2 + p, :1]
            f = qfeat[rows, cols]
            ql = (f * (qg - jnp.sum(f * qg, 0, keepdims=True))).astype(BF)
            qlg[rows, cols] = ql
            gt[rows, cols] = (nn(kt[g, :, cols], sgr) * 0.125 + nn(fq[h], ql)).astype(BF)
            kacc[g * 2 + p] = kacc[g * 2 + p] + nt(qt[rows, cols], sgr)
            vacc[g * 2 + p] = vacc[g * 2 + p] + nt(ng, w)
        return carry

    lax.fori_loop(0, 8, head_back, 0)
    part, fly = fold_plane(1, fly, 36, 52)
    lax.fori_loop(8, 16, head_back, 0)
    suffix = fold_line(1, part, fly, 68)
    states = [None, None, None, suffix]
    for s in (2, 1, 0):
        states[s] = gates[s + 1] * (states[s + 1] + st[s + 1])
    put_states(states, 4)

    valid = vrow[:1]
    for g in range(2):
        f_rows = slice(g * HEAD, (g + 1) * HEAD)
        for p in range(2):
            k = g * 2 + p
            cols = slice(p * 128, (p + 1) * 128)
            f = kfeat[f_rows, cols]
            both = nn(comb_t[4 + k], vt[g, :, cols])
            fg = jnp.where(low_lane, both[:HEAD], both[HEAD:]) * valid[:, cols]
            kl = (f * (fg - jnp.sum(f * fg, 0, keepdims=True))).astype(BF)
            qlg[HALF + g * HEAD : HALF + (g + 1) * HEAD, cols] = kl
            gt[HALF + g * HEAD : HALF + (g + 1) * HEAD, cols] = (kacc[k] * 0.125 + nn(fk[g], kl)).astype(BF)
            fl = f.astype(BF)
            stack = jnp.concatenate([jnp.where(low_lane, fl, zero_low), jnp.where(low_lane, zero_low, fl)], 0)
            gt[HALF + NARROW + g * HEAD : HALF + NARROW + (g + 1) * HEAD, cols] = (
                vacc[k] + nn(comb[4 + k, :HEAD], stack)
            ).astype(BF)

    def feat_pairs(n, carry):
        rows = pl.ds(pl.multiple_of(n * 128, 128), 128)
        r = nt(qt[rows, :], qlg[rows, :])
        red[0:64, rows] = jnp.where(low_lane, r[:HEAD], r[HEAD:])
        return carry

    lax.fori_loop(0, 8, feat_pairs, 0)
    r = nt(kt[...].reshape(128, CHIP), qlg[HALF:, :])
    red[0:64, HALF : HALF + 128] = jnp.where(low_lane, r[:HEAD], r[HEAD:])

    lowg_t = nn(ball[...], gt[...])
    lowg[...] = lowg_t.T.astype(BF)
    lowg_t = lowg_t.astype(BF)
    low_t = low[...].astype(F32).T.astype(BF)
    up = 2.0 * nt(low_t[:32], gt[...])
    red[64:72, :HALF] = up[0:8, :HALF]
    red[64:72, HALF : HALF + NARROW] = up[8:16, HALF : HALF + NARROW]
    red[64:72, HALF + NARROW :] = up[16:24, HALF + NARROW :]
    apart[0:24] = nn(lowg_t[:32], hid1[...])[:24]

    def grad_rows(n, carry):
        rows = pl.ds(pl.multiple_of(n * 256, 256), 256)
        gnat[:, rows] = gt[rows, :].astype(F32).T.astype(BF)
        return carry

    lax.fori_loop(0, 5, grad_rows, 0)

    def one_columns(n, carry):
        cols = pl.ds(pl.multiple_of(n * 256, 256), 256)
        w = wa[n // 2, pl.ds(pl.multiple_of(lax.rem(n, 2) * 2, 2), 2), :, :, :, 0:QKV].reshape(256, QKV)
        o = nt(gnat[...], w) + nt(lowg[...], aall[cols, :])
        ones[:, cols] = jnp.where(c == 0, o[:ROWS], o[ROWS:])
        outs[:, cols] = jnp.where(c == 0, o[ROWS:], o[:ROWS]).astype(BF)
        return carry

    copies.sent([out_copy])
    lax.fori_loop(0, 8, one_columns, 0)
    one_copy = copies.start(outs, outr, sibling)

    for copy in blk_fly:
        copy.wait_recv()

    def block_rows(i, carry):
        rows = pl.ds(i * 16, 16)
        t = mid[rows, :] + ht[rows, :].astype(F32)
        for k in range(3):
            t += rbb[k, rows, :].astype(F32)
        blk_out[rows, :] = t.astype(BF)
        return carry

    lax.fori_loop(0, ROWS // 16, block_rows, 0)
    one_copy.wait_recv()

    def token_rows(i, acc):
        rows = pl.ds(i * 16, 16)
        o = ones[rows, :] + outr[rows, :].astype(F32)
        t = tok[rows, :].astype(F32)
        r = lax.rsqrt(jnp.mean(t * t, -1, keepdims=True) + EPSILON)
        n = t * r
        acc += jnp.sum(o * n, 0, keepdims=True)
        o = o * gain1[...]
        gtok_out[rows, :] = (mgrad[rows, :] + r * (o - n * jnp.mean(o * n, -1, keepdims=True))).astype(BF)
        return acc

    gain_attn = lax.fori_loop(0, ROWS // 16, token_rows, jnp.zeros((1, WIDTH), F32))
    row8 = lax.broadcasted_iota(jnp.int32, (8, 1), 0)
    apart[32:40] = jnp.where(row8 == 0, gain_attn, 0.0) + jnp.where(row8 == 1, gain_mlp, 0.0)

    theirs = pl.ds(pl.multiple_of((1 - c) * HALF, HALF), HALF)
    mine = pl.ds(pl.multiple_of(c * HALF, HALF), HALF)
    a_copy = copies.start(apart.at[:, theirs], asib, sibling)
    red[72:80, HALF:] = jnp.zeros((8, PIECE - HALF), F32)
    red[0:64, HALF + 128 :] = jnp.zeros((64, 128), F32)
    red[80:128, HALF:] = jnp.zeros((48, PIECE - HALF), F32)
    red[120:128, :HALF] = jnp.zeros((8, HALF), F32)
    a_copy.wait_recv()
    red[80:120, :HALF] = apart[:, mine] + asib[...]
    fly = []
    for i in range(4):
        for j in range(4):
            if i + j > 0:
                to = wrap(x + i) * 4 + wrap(y + j)
                src = red.at[pl.ds(pl.multiple_of(to * 8, 8), 8)]
                fly.append(copies.start(src, rr.at[plane], device({"x": i, "y": j})))
    rr[plane] = red[pl.ds(pl.multiple_of(plane * 8, 8), 8), :]
    for copy in fly:
        copy.wait_recv()
    total = rr[0]
    for k in range(1, 16):
        total += rr[k]
    rz[z] = total
    fly = [copies.start(rz.at[z], rz.at[z], device({"z": i})) for i in (1, 2, 3)]
    for copy in fly:
        copy.wait_recv()
    total = (rz[0] + rz[1]) + (rz[2] + rz[3])
    fin[c, plane] = total
    piece = fin.at[c, plane]
    fly = [
        copies.start(piece, piece, device({"x": i, "y": j})) for i in range(4) for j in range(4) if i + j > 0
    ]
    for copy in fly:
        copy.wait_recv()
    f_copy = copies.start(fin.at[c], fin.at[c], sibling)
    f_copy.wait_recv()
    red_out[...] = fin[...]
    copies.drain()


N_COPIES = 400


def scratch():
    v = pltpu.VMEM
    return [
        v((4, 4, 4, 2, 16, ATT), BF),
        v((4, 2, 2, 2, 2, 2, 16, 3 * SLICE), BF),
        v((2, ROWS, WIDTH), BF),
        v((CHIP, WIDTH), BF),
        v((CHIP, 128), BF),
        v((HALF, CHIP), BF),
        v((2, HEAD, CHIP), BF),
        v((2, 128, CHIP), BF),
        v((2, CHIP, 128), BF),
        v((2, CHIP, 128), BF),
        v((128, CHIP), F32),
        v((4, AUG, 128), F32),
        v((8, AUG, 128), BF),
        v((8, 128, 128), BF),
        v((32, 128, 128), BF),
        v((HALF, CHIP), F32),
        v((HALF, CHIP), F32),
        v((32, 8, 128), F32),
        v((32, 8, 128), F32),
        v((CHIP, HALF), BF),
        v((CHIP, 128), BF),
        v((ROWS, WIDTH), BF),
        v((ROWS, WIDTH), BF),
        v((ROWS, WIDTH), F32),
        v((512, WIDTH), BF),
        v((512, WIDTH), BF),
        v((512, SLICE), BF),
        v((512, SLICE), BF),
        v((512, SLICE), BF),
        v((3, ROWS, WIDTH), BF),
        v((3, ROWS, WIDTH), BF),
        v((ROWS, WIDTH), F32),
        v((2, ROWS, WIDTH), BF),
        v((HALF, CHIP), BF),
        v((32, 8, 128), F32),
        v((4, AUG, 128), F32),
        v((HALF + 128, CHIP), BF),
        v((QKV, CHIP), BF),
        v((CHIP, QKV), BF),
        v((CHIP, 128), BF),
        v((ROWS, WIDTH), F32),
        v((4, HEAD, 128), F32),
        v((4, HEAD, 128), F32),
        v((2, AUG, 128), BF),
        v((2, 16, AUG, 128), BF),
        v((2, AUG, 128), BF),
        v((2, 3, AUG, 128), BF),
        v((128, PIECE), F32),
        v((16, 8, PIECE), F32),
        v((4, 8, PIECE), F32),
        v((2, 16, 8, PIECE), F32),
        v((40, WIDTH), F32),
        v((40, HALF), F32),
        pltpu.SemaphoreType.DMA((N_COPIES,)),
        pltpu.SemaphoreType.DMA((N_COPIES,)),
        pltpu.SemaphoreType.DMA((16,)),
    ]


def body(
    tokens, sequence_lengths, attention_gain, query_weight, key_weight, value_weight, output_weight_flipped,
    query_adapter_down, query_adapter_up, key_adapter_down, key_adapter_up, value_adapter_down, value_adapter_up,
    output_adapter_down, output_adapter_up, query_feature_map, key_feature_map, feedforward_gain,
    gate_weight, up_weight, down_weight_flipped, output_gradient,
):
    me = lax.axis_index("seq")
    c = me % 2
    chip = me // 2
    plane, z = chip % 16, chip // 16
    heads = QUERY_HEADS // 2

    counts = (sequence_lengths + STRETCH - 1) // STRETCH
    ends = jnp.cumsum(counts)
    starts = ends - counts

    def sid(stretch):
        return jnp.sum((stretch[..., None] >= ends).astype(jnp.int32), -1)

    own = chip * 4 + jnp.arange(4)
    own_sid = sid(own)
    member = (own_sid[:, None] == jnp.arange(8)[None]).astype(jnp.int32)
    begin = jnp.sum(member * starts[None], 1)
    length = jnp.sum(member * sequence_lengths[None], 1)
    valid = ((own - begin)[:, None] * STRETCH + jnp.arange(STRETCH)[None] < length[:, None]).reshape(CHIP)
    valid_f = valid.astype(F32)
    vrow = jnp.broadcast_to(valid_f[None], (8, CHIP))
    at = jnp.arange(128)
    allowed = (at[:, None] <= at[None]) & (at[:, None] // STRETCH == at[None] // STRETCH)
    bias = jnp.where(allowed[None] & valid.reshape(2, 128)[:, :, None], 0.0, -1e30).astype(F32)

    chips = z * 16 + jnp.arange(16)
    first_sid, last_sid = sid(chips * 4), sid(chips * 4 + 3)
    planes = jnp.arange(4)
    plane_first, plane_last = sid(planes * 64), sid(planes * 64 + 63)
    k16 = jnp.arange(16)
    s0, s3 = own_sid[0], own_sid[3]
    same = jnp.concatenate([jnp.zeros((1,), bool), own_sid[1:] == own_sid[:-1]])
    scal = jnp.concatenate([
        (k16 < plane) & (last_sid == s0),
        last_sid == plane_last[z],
        (planes < z) & (plane_last == s0),
        (k16 > plane) & (first_sid == s3),
        first_sid == plane_first[z],
        (planes > z) & (plane_first == s3),
        jnp.zeros((8,), bool),
        same,
    ]).astype(F32)

    def core(array, axis):
        count = array.shape[axis] // 2
        return lax.dynamic_slice_in_dim(array, c * count, count, axis)

    aall = jnp.concatenate([query_adapter_down, key_adapter_down, value_adapter_down], 1)
    aall = jnp.pad(aall, ((0, 0), (0, 128 - 3 * RANK)))
    ball = jnp.zeros((128, QKV), BF)
    ball = lax.dynamic_update_slice(ball, 2 * core(query_adapter_up, 1), (0, 0))
    ball = lax.dynamic_update_slice(ball, 2 * core(key_adapter_up, 1), (RANK, HALF))
    ball = lax.dynamic_update_slice(ball, 2 * core(value_adapter_up, 1), (2 * RANK, HALF + NARROW))
    oac = jnp.pad(core(output_adapter_down, 0), ((0, 0), (0, 128 - RANK)))
    ob2 = jnp.pad(2 * output_adapter_up, ((0, 128 - RANK), (0, 0)))
    fq = core(query_feature_map, 0)
    fk = core(key_feature_map, 0)

    vmem = pl.BlockSpec(memory_space=pltpu.VMEM)
    smem = pl.BlockSpec(memory_space=pltpu.SMEM)
    block_out, grad_tokens, red = pl.pallas_call(
        kernel,
        out_shape=(
            jax.ShapeDtypeStruct((ROWS, WIDTH), BF),
            jax.ShapeDtypeStruct((ROWS, WIDTH), BF),
            jax.ShapeDtypeStruct((2, 16, 8, PIECE), F32),
        ),
        in_specs=[vmem] * 21 + [smem],
        out_specs=(vmem, vmem, vmem),
        scratch_shapes=scratch(),
        compiler_params=pltpu.CompilerParams(
            collective_id=0, has_side_effects=True, vmem_limit_bytes=64 * 1024 * 1024
        ),
    )(
        tokens, output_gradient, query_weight, key_weight, value_weight, output_weight_flipped,
        gate_weight, up_weight, down_weight_flipped, aall, ball, oac, ob2,
        fq.swapaxes(1, 2), fq, fk.swapaxes(1, 2), fk,
        attention_gain.astype(F32)[None], feedforward_gain.astype(F32)[None], bias, vrow, scal,
    )
    red = red.reshape(2, 128, PIECE)
    both = jnp.concatenate([red[0, 80:120, :HALF], red[1, 80:120, :HALF]], 1)

    def columns(rows, first, count):
        return jnp.concatenate([red[0, rows, first : first + count], red[1, rows, first : first + count]], 1)

    feat_q = columns(slice(0, 64), 0, HALF).reshape(HEAD, QUERY_HEADS, HEAD).swapaxes(0, 1)
    feat_k = columns(slice(0, 64), HALF, NARROW).reshape(HEAD, KEY_VALUE_HEADS, HEAD).swapaxes(0, 1)
    return (
        block_out,
        grad_tokens,
        both[32],
        both[0:8].T,
        columns(slice(64, 72), 0, HALF),
        both[8:16].T,
        columns(slice(64, 72), HALF, NARROW),
        both[16:24].T,
        columns(slice(64, 72), HALF + NARROW, NARROW),
        columns(slice(72, 80), 0, HALF).T,
        both[24:32],
        feat_q,
        feat_k,
        both[33],
    )


def solution(mesh):
    split, whole = P("seq", None), P()
    return jax.shard_map(
        body,
        mesh=mesh,
        in_specs=(
            (split, whole, whole) + (split,) * 4 + (whole,) * 11 + (split,) * 4
        ),
        out_specs=(split, split) + (whole,) * 12,
        check_vma=False,
    )
```

time: 819 us -> 286 us (0.35)
  waiting for transfers between devices: 478 us -> 0 us
  Pallas kernels: 0 us -> 247 us
  matrix products: 172 us -> 0 us
  local copies, waits for them, and re-layouts: 119 us -> 18.8 us
  between operations: 16.8 us -> 0.92 us
  other arithmetic: 27.5 us -> 18.2 us
    all_gather x6 -> x0, waiting for transfers between devices: 334 us -> none  [the longest x1 81.7 us: body(): attention_all = lax.all_gather(attention_rows, 'seq', axis=0, tiled=True)]
    pallas_call x0 -> x1, Pallas kernels: none -> 247 us  [body(): pl.pallas_call(kernel, out_shape=(jax.ShapeDtypeStruct((ROWS, WIDTH), BF)...]
    dot_general x59 -> x0, matrix products: 171 us -> none  [the longest x15 66.2 us: product_flipped(): lax.dot_general(left, right, (((1,), (1,)), ((), ())), preferred_element_...]
    psum x1 -> x0, waiting for transfers between devices: 143 us -> none  [body(): flat = lax.psum(flat, 'seq').reshape(-1)]
    dot_general x5 -> x0, local copies, waits for them, and re-layouts: 49.4 us -> none  [the longest x4 49.3 us: entering(): jnp.dot(reached.astype(jnp.bfloat16)[None], everything, preferred_element...]
    unnamed x220 -> x17, local copies, waits for them, and re-layouts: 25.3 us -> 4.02 us
    reshape x22 -> x0, local copies, waits for them, and re-layouts: 18.9 us -> none  [the longest x10 6.81 us: body(): summed.append(flat[at:at + part.size].reshape(part.shape))]
    convert_element_type x8 -> x1, local copies, waits for them, and re-layouts: 8.89 us -> 0.08 us  [body(): valid_f = valid.astype(F32)]
  transfers between devices with their start and end apart: 7 -> 0, of which waited for: 7 -> 0; matrix products, arithmetic and copies ran while one was open for 21% -> 0% of each run, Pallas kernels for 0% -> 0%
where the time goes in v2:
time: 286 us; the launch traced here: 285 us
  Pallas kernels  247 us (86%)
  local copies, waits for them, and re-layouts  18.8 us (7%)
  other arithmetic  18.2 us (6%)
    pallas_call x1, Pallas kernels, body(): pl.pallas_call(kernel, out_shape=(jax.ShapeDtypeStruct((ROWS, WIDTH), BF)...  247 us

profile of v2, /device:TPU:1, one launch (start us, length us, event | category | flops | bytes accessed | tf_op | source)
XLA Modules:
  0.0 284.9 jit_solution(15815436256374571976)
XLA Ops:
  3.8 0.9 select_reduce_fusion.1
  5.3 1.3 compare_and_fusion
  6.7 1.3 broadcast_compare_fusion
  8.0 1.3 broadcast_compare_fusion.1
  11.2 1.3 broadcast_in_dim.25
  12.5 1.3 broadcast_in_dim.26
  15.4 0.8 broadcast_multiply_fusion
  16.1 0.8 fusion.13
  17.6 1.4 constant_dynamic-slice_fusion.fk
  19.0 0.8 pad_maximum_fusion
  19.8 0.8 and_select_fusion.bias
  20.7 0.8 pad.14.oac
  21.5 0.8 copy.58.fq_t
  22.3 0.7 constant_dynamic-slice_fusion.1.fq
  23.1 0.7 dynamic_update_slice.9
  25.3 0.9 pad.13.aall
  26.2 0.8 pad.15.ob2
  27.0 247.0 %shard_map.317 = (bf16[128,2048]{1,0:T(8,128)(2,1)}, bf16[128,2048]{1,0:T(8,128)(2,1)}, f32[2,16,8,1280]{3,2,1,0:T(8,128)}) custom-call(bf16[128,2048]{1,0:T(8,128)(2,1)} %tok.1, bf16[128,2048]{1,0:T(8,128)(2,1)} %og.1, bf16[16,2048]{1,0:T(8,128)(2,1)} %qw.1, bf16[16,256]{1,0:T(8,128)(2,1)} %kw.1, bf16[16,256]{1,0:T(8,128)(2,1)} %vw.1, bf16[16,2048]{1,0:T(8,128)(2,1)} %ow.1, ...), custom_call_target="tpu_custom_call" | custom-call | tf_op jit(solution)/shard_map/pallas_call | solution.py:882
  274.0 0.8 slice_bitcast_fusion.7
  276.0 0.8 fusion.9
  277.8 0.8 slice_bitcast_fusion.3
  281.7 1.6 copy.60
  283.3 0.8 copy.67
  284.1 0.8 copy.68
  (67 shorter events, 14.8 us)
Async XLA Ops:
  0.6 20.8 %copy-start.1 = (bf16[32,64,64]{2,1,0:T(8,128)(2,1)S(1)}, bf16[32,64,64]{2,1,0:T(8,128)(2,1)}, u32[]{:S(2)}) copy-start(bf16[32,64,64]{2,1,0:T(8,128)(2,1)} %param.37) | copy-start | bytes 786436
  20.5 3.3 %copy-start.4 = (bf16[8,256]{1,0:T(8,128)(2,1)S(1)}, bf16[8,256]{1,0:T(8,128)(2,1)}, u32[]{:S(2)}) copy-start(bf16[8,256]{1,0:T(8,128)(2,1)} %param.32) | copy-start | bytes 12292
  20.5 3.9 %copy-start.5 = (bf16[8,256]{1,0:T(8,128)(2,1)S(1)}, bf16[8,256]{1,0:T(8,128)(2,1)}, u32[]{:S(2)}) copy-start(bf16[8,256]{1,0:T(8,128)(2,1)} %param.34) | copy-start | bytes 12292
  274.0 5.8 %copy-start = (f32[2,16,8,1280]{3,2,1,0:T(8,128)S(1)}, f32[2,16,8,1280]{3,2,1,0:T(8,128)}, u32[]{:S(2)}) copy-start(f32[2,16,8,1280]{3,2,1,0:T(8,128)} %get-tuple-element.19) | copy-start | bytes 3932164
  281.7 1.6 copy-start.3
  281.7 2.4 copy-start.2

commit v3 on v2

v3 whole, which is shorter than its diff:
```python
import math

import jax
import jax.numpy as jnp
from jax import lax
from jax.experimental import pallas as pl
from jax.experimental.pallas import tpu as pltpu
from jax.sharding import PartitionSpec as P

QUERY_HEADS = 32
KEY_VALUE_HEADS = 4
HEAD = 64
STRETCH = 64
WIDTH = 2048
FF = 5632
ROWS = 128
CHIP = 256
HALF = 1024
NARROW = 128
QKV = HALF + 2 * NARROW
ATT = QKV + HALF
SLICE = FF // 4
AUG = 80
RANK = 8
PIECE = 1280
EPSILON = 1e-05
MESH = pl.DeviceIdType.MESH
F32 = jnp.float32
BF = jnp.bfloat16

SHARES = (
    (1, 0, 0, 64, 128),
    (3, 0, 64, 64, 192),
    (0, 1, 0, 64, 256),
    (0, 3, 64, 64, 320),
    (1, 1, 0, 32, 384),
    (1, 3, 32, 32, 416),
    (3, 1, 64, 32, 448),
    (3, 3, 96, 32, 480),
)


def nn(left, right):
    return jnp.dot(left, right, preferred_element_type=F32)


def tn(left, right):
    return lax.dot_general(left, right, (((0,), (0,)), ((), ())), preferred_element_type=F32)


def nt(left, right):
    return lax.dot_general(left, right, (((1,), (1,)), ((), ())), preferred_element_type=F32)


def wrap(value):
    return lax.rem(value, 4)


class Copies:
    def __init__(self, send, recv):
        self.send, self.recv, self.count, self.open = send, recv, 0, {}

    def start(self, src, dst, device):
        slot = self.count % N_SENDS
        if slot in self.open:
            self.open.pop(slot).wait_send()
        copy = pltpu.make_async_remote_copy(
            src_ref=src,
            dst_ref=dst,
            send_sem=self.send.at[slot],
            recv_sem=self.recv.at[self.count],
            device_id=(device,),
            device_id_type=MESH,
        )
        self.count += 1
        copy.start()
        self.open[slot] = copy
        return copy

    def sent(self, copies):
        for slot in [k for k, copy in self.open.items() if any(copy is other for other in copies)]:
            self.open.pop(slot).wait_send()

    def drain(self):
        for copy in self.open.values():
            copy.wait_send()


class Heads:
    def __init__(self, copies, wa, where, device, parts, straight=False):
        self.copies, self.wa, self.where, self.device = copies, wa, where, device
        self.parts, self.straight = parts, straight
        self.flying = {}

    def block(self, order, phase, at, first, count):
        index = []
        for axis in "zxy":
            k = order.index(axis)
            index.append(slice(None) if k < phase else at if k == phase else self.where[axis])
        return self.wa.at[index[0], index[1], index[2], :, :, pl.ds(first, count)]

    def begin(self, phase):
        for part, (order, first, count) in enumerate(self.parts):
            axis = order[phase]
            own = self.block(order, phase, self.where[axis], first, count)
            steps = (1, 3) if phase == 2 and not self.straight else (1, 3, 2)
            self.flying[phase, part] = [self.copies.start(own, own, self.device({axis: step})) for step in steps]

    def middle(self, phase):
        for part, (order, first, count) in enumerate(self.parts):
            axis = order[phase]
            for copy in self.flying[phase, part]:
                copy.wait_recv()
            here = self.where[axis]
            one = (count // 256) * 128
            left = self.block(order, phase, wrap(here + 3), first, one)
            right = self.block(order, phase, wrap(here + 1), first + one, count - one)
            self.flying[phase, part] = [
                self.copies.start(left, left, self.device({axis: 1})),
                self.copies.start(right, right, self.device({axis: 3})),
            ]

    def end(self, phase):
        for part in range(len(self.parts)):
            for copy in self.flying[phase, part]:
                copy.wait_recv()


class Units:
    def __init__(self, copies, here, wf, stage, where, device, sibling, parts):
        self.copies, self.here, self.wf, self.stage = copies, here, wf, stage
        self.where, self.device, self.sibling, self.parts = where, device, sibling, parts
        self.flying, self.handed, self.own = {}, [], []

    def rows(self, order, along, across, cols):
        w = self.where
        a = (slice(None), slice(None)) if along is None else (along // 2, lax.rem(along, 2))
        b = (across // 2, lax.rem(across, 2))
        x, y = (a, b) if order == "xy" else (b, a)
        return self.wf.at[w["z"], x[0], x[1], y[0], y[1], w["c"], :, cols]

    def line(self, z, cols):
        return self.wf.at[z, :, :, :, :, self.where["c"], :, cols]

    def hand_on(self, block):
        self.handed.append(self.copies.start(block, block, self.sibling))

    def begin(self, phase):
        w = self.where
        for part, (order, src, at, first, count) in enumerate(self.parts):
            cols = pl.ds(first, count)
            a, b = order
            fly = []
            if phase == 0:
                for d in (1, 3, 2, 0):
                    for e in (0, 1):
                        pa, pb = lax.rem(w[a] + d, 2), lax.rem(w[b] + e, 2)
                        slot = pa * 2 + pb if order == "xy" else pb * 2 + pa
                        piece = src.at[:, pl.ds(pl.multiple_of(slot * SLICE + at, 128), count)]
                        if e == 0:
                            dst = self.rows(order, w[a], w[b], cols)
                        else:
                            dst = self.stage.at[w[a] // 2, lax.rem(w[a], 2), :, cols]
                        if d == 0:
                            self.own.append(self.here(piece, dst))
                        else:
                            fly.append(self.copies.start(piece, dst, self.device({a: d})))
            elif phase == 1:
                mine = self.rows(order, None, w[b], cols)
                other = self.stage.at[:, :, :, cols]
                fly = [
                    self.copies.start(other, mine, self.device({b: 1})),
                    self.copies.start(other, mine, self.device({b: 3})),
                    self.copies.start(mine, mine, self.device({b: 2})),
                ]
            else:
                block = self.line(w["z"], cols)
                self.hand_on(block)
                fly = [self.copies.start(block, block, self.device({"z": step})) for step in (1, 3)]
            self.flying[phase, part] = fly

    def middle(self, phase):
        z = self.where["z"]
        for part, (order, src, at, first, count) in enumerate(self.parts):
            for copy in self.flying[phase, part]:
                copy.wait_recv()
            one = (count // 256) * 128
            before, after = wrap(z + 3), wrap(z + 1)
            left = self.line(before, pl.ds(first, one))
            right = self.line(after, pl.ds(first + one, count - one))
            self.flying[phase, part] = [
                self.copies.start(left, left, self.device({"z": 1})),
                self.copies.start(right, right, self.device({"z": 3})),
            ]
            self.hand_on(self.line(before, pl.ds(first, count)))
            self.hand_on(self.line(after, pl.ds(first, count)))

    def end(self, phase):
        if phase == 0:
            for copy in self.own:
                copy.wait()
        for part, (order, src, at, first, count) in enumerate(self.parts):
            for copy in self.flying[phase, part]:
                copy.wait_recv()
            if phase == 2:
                self.hand_on(self.line(wrap(self.where["z"] + 2), pl.ds(first, count)))

    def settle(self):
        for copy in self.handed:
            copy.wait_recv()


EARLY = ("kv.b0", "q.b0", "o.b0", "d.b0", "g.b0",)
PLAN = (
    "kv.e0", "u.b0", "kv.b1", "q.e0", "o.e0", "q.b1", "d.e0", "d.b1", "u.e0", "g.e0", "o.b1", "d.e1",
    "q.e1", "g.b1", "kv.e1", "u.b1", "q.b2", "kv.b2", "d.b2", "g.e1", "d.m2", "q.m2", "o.e1", "g.b2",
    "kv.e2", "low", "kvc", "pls", "o.b2", "u.e1", "lns", "d.e2", "u.b2", "q.e2", "lnw", "qc",
    "o.m2", "ogs", "g.m2", "att", "o.e2", "ds", "oproj", "mid", "hts", "u.m2", "g.e2", "ogw",
    "ig", "u.e2", "gs", "us", "htw",
)


def kernel(
    tok, lens, gain_a, qw, kw, vw, ow, qa, qb, ka, kb, va, vb, oa, ob, fq, fk, gain_b, gw, uw, dw, og,
    blk_out, gtok_out, gain_a_out, qa_out, qb_out, ka_out, kb_out, va_out, vb_out, oa_out, ob_out, fq_out, fk_out,
    gain_b_out,
    wa, wf, stage, tok2, ogo, gains, r1, aall, ball, oac, ob2, masks, far_masks, bias, hid1, low, qt, kt, vt, knat, vnat,
    kfeat, st, comb, comb_t, wts, qfeat, mixf, damp, den, mixn, lowo, outs, outr, mid, ht, ogx, gg, inner, ug, rbt, rbb,
    mgrad, bg, ngt, dgr, sig, qlg, gt, gnat, lowg, ones, kacc, vacc, fsend, frecv, hsend, hrecv, red, redb, rr, rz, fin,
    apart, asib, send, recv, loc,
):
    me = lax.axis_index("seq")
    c = lax.rem(me, 2)
    y = lax.rem(me // 2, 4)
    x = lax.rem(me // 8, 4)
    z = me // 32

    def device(steps):
        zz, xx, yy = (wrap(v + steps.get(n, 0)) for n, v in (("z", z), ("x", x), ("y", y)))
        return ((zz * 4 + xx) * 4 + yy) * 2 + c

    sibling = me + 1 - 2 * c
    plane = x * 4 + y
    xl, yl = lax.rem(x, 2), lax.rem(y, 2)
    xh, yh = x // 2, y // 2

    barrier = pltpu.get_barrier_semaphore()
    peers = [sibling]
    peers += [device({"x": i, "y": j}) for i in range(4) for j in range(4) if i + j > 0]
    peers += [device({"z": i}) for i in (1, 2, 3)]
    for peer in peers:
        pl.semaphore_signal(barrier, inc=1, device_id=(peer,), device_id_type=MESH)
    pl.semaphore_wait(barrier, len(peers))

    copies = Copies(send, recv)
    local = []

    def here(src, dst):
        copy = pltpu.make_async_copy(src, dst, loc.at[len(local)])
        copy.start()
        local.append(copy)
        return copy

    tok_copy = copies.start(tok, tok2.at[c], sibling)
    first = []
    own = wa.at[z, x, y, c]
    for src, at, count in ((kw, HALF, NARROW), (vw, HALF + NARROW, NARROW), (qw, 0, HALF), (ow, QKV, HALF)):
        mine = src.at[:, pl.ds(pl.multiple_of(c * count, count), count)]
        other = src.at[:, pl.ds(pl.multiple_of((1 - c) * count, count), count)]
        dst = own.at[:, pl.ds(at, count)]
        here(mine, dst)
        first.append(copies.start(other, dst, sibling))
    here(tok, tok2.at[c])
    here(og, ogx.at[pl.ds(0, ROWS)])
    here(og, ogo)

    where = {"z": z, "x": x, "y": y, "c": c}
    streams = {
        "kv": Heads(copies, wa, where, device, (("xzy", 1024, 128), ("yzx", 1152, 128)), straight=True),
        "q": Heads(copies, wa, where, device, [(o, k * 256, 256) for k, o in enumerate(("xzy", "zyx", "zxy", "yzx"))]),
        "o": Heads(
            copies, wa, where, device, [(o, QKV + k * 256, 256) for k, o in enumerate(("xzy", "zyx", "zxy", "yzx"))]
        ),
        "d": Units(
            copies, here, wf, stage, where, device, sibling,
            (("xy", dw, 0, 2 * SLICE, 768), ("yx", dw, 768, 2 * SLICE + 768, 640)),
        ),
        "g": Units(copies, here, wf, stage, where, device, sibling, (("xy", gw, 0, 0, SLICE),)),
        "u": Units(copies, here, wf, stage, where, device, sibling, (("yx", uw, 0, SLICE, SLICE),)),
    }
    for k in range(4):
        local[k].wait()
        first[k].wait_recv()
    waiting = {}

    def advance(name):
        stream, step = name.split(".")
        stream = streams[stream]
        {"b": stream.begin, "m": stream.middle, "e": stream.end}[step[0]](int(step[1]))

    for name in EARLY:
        advance(name)

    for k, src in enumerate((gain_a, gain_b)):
        g = src[...].astype(F32)
        gains[k : k + 1, :] = jnp.concatenate([g[i : i + 1] for i in range(16)], 1)
    gain1, gain2 = gains.at[pl.ds(0, 1)], gains.at[pl.ds(1, 1)]

    def below(parts, rows, count):
        got = [part.astype(F32) for part in parts]
        used = RANK * len(parts)
        return jnp.concatenate(got + [jnp.zeros((rows - used, count), F32)], 0).astype(BF)

    aall[...] = below([qa[...], ka[...], va[...]], 128, WIDTH)
    half = pl.ds(pl.multiple_of(c * HALF, HALF), HALF)
    narrow = pl.ds(pl.multiple_of(c * NARROW, NARROW), NARROW)
    none = jnp.zeros((RANK, NARROW), F32)
    ball[:, :HALF] = below([2.0 * qb[:, half].astype(F32)], 128, HALF)
    ball[:, HALF : HALF + NARROW] = below([none, 2.0 * kb[:, narrow].astype(F32)], 128, NARROW)
    ball[:, HALF + NARROW :] = below([none, none, 2.0 * vb[:, narrow].astype(F32)], 128, NARROW)
    oac[...] = below([oa[:, half]], 128, HALF)
    ob2[...] = below([2.0 * ob[...].astype(F32)], 128, WIDTH)

    chip = me // 2
    starts, ends, total = [], [], jnp.int32(0)
    for k in range(8):
        starts.append(total)
        total = total + ((lens[k] + (STRETCH - 1)) >> 6)
        ends.append(total)

    def sequence(stretch):
        found = jnp.where(stretch >= ends[0], 1, 0)
        for k in range(1, 7):
            found = found + jnp.where(stretch >= ends[k], 1, 0)
        return found

    counts, gates = [], []
    for s in range(4):
        stretch = chip * 4 + s
        begin, length = starts[0], lens[0]
        for k in range(1, 8):
            inside = stretch >= starts[k]
            begin = jnp.where(inside, starts[k], begin)
            length = jnp.where(inside, lens[k], length)
        counts.append(length - (stretch - begin) * STRETCH)
        gates.append(jnp.where(stretch != begin, 1.0, 0.0))
    first_own, last_own = sequence(chip * 4), sequence(chip * 4 + 3)
    k16 = lax.broadcasted_iota(jnp.int32, (16, 128), 0)
    firsts = sequence((z * 16 + k16) * 4)
    lasts = sequence((z * 16 + k16) * 4 + 3)
    masks[0] = jnp.where((k16 < plane) & (lasts == first_own), 1.0, 0.0)
    masks[1] = jnp.where(lasts == sequence(z * 64 + 63), 1.0, 0.0)
    masks[2] = jnp.where((k16 > plane) & (firsts == last_own), 1.0, 0.0)
    masks[3] = jnp.where(firsts == sequence(z * 64), 1.0, 0.0)
    k8 = lax.broadcasted_iota(jnp.int32, (8, 128), 0)
    far_masks[0] = jnp.where((k8 < z) & (sequence(k8 * 64 + 63) == first_own), 1.0, 0.0)
    far_masks[1] = jnp.where((k8 > z) & (sequence(k8 * 64) == last_own), 1.0, 0.0)
    lane = lax.broadcasted_iota(jnp.int32, (1, 128), 1)
    low_lane = lane < 64
    in_stretch = lax.rem(lane, STRETCH)
    valid = jnp.concatenate(
        [jnp.where(in_stretch < jnp.where(low_lane, counts[2 * p], counts[2 * p + 1]), 1.0, 0.0) for p in range(2)], 1
    )
    iu = lax.broadcasted_iota(jnp.int32, (128, 128), 0)
    it = lax.broadcasted_iota(jnp.int32, (128, 128), 1)
    for p in range(2):
        room = jnp.where(iu < 64, counts[2 * p], counts[2 * p + 1])
        seen = (iu <= it) & ((iu < 64) == (it < 64)) & (lax.rem(iu, STRETCH) < room)
        bias[p] = jnp.where(seen, 0.0, -1e30)

    for copy in local[4:7]:
        copy.wait()
    tok_copy.wait_recv()

    def norm_rows(i, carry):
        rows = pl.ds(i * 32, 32)
        for side in range(2):
            t = tok2[side, rows, :].astype(F32)
            r = lax.rsqrt(jnp.mean(t * t, -1, keepdims=True) + EPSILON)
            r1[side, rows, :] = jnp.broadcast_to(r, (32, 128))
            hid1[pl.ds(side * ROWS + i * 32, 32), :] = (t * r * gain1[...]).astype(BF)
        return carry

    lax.fori_loop(0, ROWS // 32, norm_rows, 0)

    zero_low = jnp.zeros((), BF)

    def softmax_rows(logits):
        e = jnp.exp(logits - jnp.max(logits, 0, keepdims=True))
        return e / jnp.sum(e, 0, keepdims=True)

    def gather_plane(base, folded):
        fsend[base] = folded.astype(BF)
        fly = []
        for i in range(4):
            for j in range(4):
                if i + j > 0:
                    fly.append(copies.start(fsend.at[base], frecv.at[base, plane], device({"x": i, "y": j})))
        frecv[base, plane] = folded.astype(BF)
        return fly

    def fold_plane(base, fly):
        for copy in fly:
            copy.wait_recv()
        part = jnp.zeros((AUG, 128), F32)
        whole = jnp.zeros((AUG, 128), F32)
        for k in range(16):
            f = frecv[base, k].astype(F32)
            part += masks[2 * base, k : k + 1, :] * f
            whole += masks[2 * base + 1, k : k + 1, :] * f
        hsend[base] = whole.astype(BF)
        fly = [copies.start(hsend.at[base], hrecv.at[base, i - 1], device({"z": i})) for i in (1, 2, 3)]
        return part, fly

    def fold_line(base, part, fly):
        for i, copy in zip((1, 2, 3), fly):
            copy.wait_recv()
            part += far_masks[base, pl.ds(wrap(z + 4 - i), 1), :] * hrecv[base, i - 1].astype(F32)
        return part

    def combine(states):
        for g in range(2):
            for p in range(2):
                one, two = states[2 * p], states[2 * p + 1]
                if g == 0:
                    both = jnp.where(low_lane, one, pltpu.roll(two, 64, 1))
                else:
                    both = jnp.where(low_lane, pltpu.roll(one, 64, 1), two)
                yield g * 2 + p, both

    def put_states(states, base):
        for k, both in combine(states):
            comb[base + k] = both.astype(BF)
            tall = jnp.concatenate([both, jnp.zeros((128 - AUG, 128), F32)], 0)
            comb_t[base + k] = tall.T.astype(BF)

    def share(src, dst):
        return [
            copies.start(src.at[pl.ds(r, n)], dst.at[pl.ds(at, n)], device({"x": i, "y": j}))
            for i, j, r, n, at in SHARES
        ]

    def lower():
        low[...] = nt(hid1[...], aall[...]).astype(BF)

    def keys():
        kv = nn(hid1[...], wa[:, :, :, :, :, HALF:QKV].reshape(WIDTH, 2 * NARROW))
        kv = (kv + nn(low[...], ball[:, HALF:QKV])).astype(BF)
        kv_t = kv.astype(F32).T.astype(BF)
        for g in range(2):
            keep = low_lane if g == 0 else ~low_lane
            knat[g] = jnp.where(keep, kv[:, :NARROW], jnp.zeros((), BF))
            vnat[g] = jnp.where(keep, kv[:, NARROW:], jnp.zeros((), BF))
            kt[g] = kv_t[g * HEAD : (g + 1) * HEAD]
            tail = lax.broadcasted_iota(jnp.int32, (64, CHIP), 0) == 0
            vt[g, :HEAD] = kv_t[NARROW + g * HEAD : NARROW + (g + 1) * HEAD]
            vt[g, HEAD:] = tail.astype(F32).astype(BF)
        lanes4 = lax.broadcasted_iota(jnp.int32, (1, CHIP), 1) // STRETCH

        for g in range(2):
            kfeat[g * HEAD : (g + 1) * HEAD] = softmax_rows(tn(fk[c * 2 + g], kt[g])) * valid
        kf = kfeat[...]
        kf_high = kf.astype(BF)
        kf_rest = (kf - kf_high.astype(F32)).astype(BF)
        for s in range(4):
            got = []
            for g in range(2):
                va = jnp.where(lanes4 == s, vt[g, :AUG], jnp.zeros((), BF))
                got.append(nt(va, kf_high) + nt(va, kf_rest))
            st[s] = jnp.where(low_lane, got[0], got[1])


    def send_plane():
        folded = st[0]
        for s in (1, 2, 3):
            folded = st[s] + gates[s] * folded
        waiting["plane"] = gather_plane(0, folded)

    def send_line():
        waiting["part"], waiting["line"] = fold_plane(0, waiting["plane"])

    def take_line():
        prefix = fold_line(0, waiting["part"], waiting["line"])
        states = [prefix]
        for s in (1, 2, 3):
            states.append(gates[s] * (states[s - 1] + st[s - 1]))
        put_states(states, 0)

    def queries():
        def query_columns(n, carry):
            cols = pl.ds(pl.multiple_of(n * 256, 256), 256)
            q = nn(hid1[...], wa[:, :, :, :, :, cols].reshape(WIDTH, 256)) + nn(low[...], ball[:, cols])
            qt[cols, :] = q.T.astype(BF)
            return carry

        lax.fori_loop(0, 4, query_columns, 0)

    def lanes(parts):
        return jnp.concatenate(parts, 1)

    def split(wide):
        return [wide[:, k * 128 : (k + 1) * 128] for k in range(4)]

    def attend_four(n, carry):
        g = n // 2
        rows = [pl.ds(pl.multiple_of(n * 256 + k * HEAD, HEAD), HEAD) for k in range(4)]
        for k in range(4):
            qfeat[rows[k], :] = softmax_rows(tn(fq[c * 16 + n * 4 + k], qt[rows[k], :]))
        for p in range(2):
            cols = slice(p * 128, (p + 1) * 128)
            q = lanes([qt[r, cols] for r in rows])
            scores = split(nn(knat[g, cols, :], jnp.concatenate([q, q], 0)))
            stacks = []
            for k in range(4):
                sc = scores[k] * 0.125 + bias[p]
                peak = jnp.max(sc, 0, keepdims=True)
                w = jnp.exp(sc - peak).astype(BF)
                wts[(n * 4 + k) * 2 + p] = w
                dm = jnp.exp(-peak)
                damp[(n * 4 + k) * 2 + p, :1] = dm
                dq = (qfeat[rows[k], cols] * dm).astype(BF)
                stacks.append(
                    jnp.concatenate([w, jnp.where(low_lane, dq, zero_low), jnp.where(low_lane, zero_low, dq)], 0)
                )
            lhs = jnp.concatenate([vt[g, :AUG, cols], comb[g * 2 + p]], 1)
            both = split(nn(lhs, lanes(stacks)))
            for k in range(4):
                rden = 1.0 / both[k][HEAD : HEAD + 1]
                den[(n * 4 + k) * 2 + p, :1] = rden
                mixf[rows[k], cols] = both[k][:HEAD] * rden
        return carry

    def attend():
        lax.fori_loop(0, 4, attend_four, 0)


    def project():
        def mix_rows(n, carry):
            cols = pl.ds(pl.multiple_of(n * 256, 256), 256)
            mixn[:, cols] = mixf[cols, :].T.astype(BF)
            return carry

        lax.fori_loop(0, 4, mix_rows, 0)
        lowo[...] = nt(mixn[...], oac[...]).astype(BF)

        def out_columns(n, carry):
            cols = pl.ds(pl.multiple_of(n * 256, 256), 256)
            w = wa[n // 2, pl.ds(pl.multiple_of(lax.rem(n, 2) * 2, 2), 2), :, :, :, QKV:ATT].reshape(256, HALF)
            o = nt(mixn[...], w) + nn(lowo[...], ob2[:, cols])
            mine = jnp.where(c == 0, o[:ROWS], o[ROWS:])
            other = jnp.where(c == 0, o[ROWS:], o[:ROWS])
            mid[:, cols] = mine + tok2[c, :, cols].astype(F32)
            outs[:, cols] = other.astype(BF)
            return carry

        lax.fori_loop(0, 8, out_columns, 0)
        waiting["out"] = copies.start(outs, outr, sibling)

    def middle():
        waiting["out"].wait_recv()

        def middle_rows(i, carry):
            rows = pl.ds(i * 32, 32)
            m = mid[rows, :] + outr[rows, :].astype(F32)
            mid[rows, :] = m
            r = lax.rsqrt(jnp.mean(m * m, -1, keepdims=True) + EPSILON)
            ht[rows, :] = (m * r * gain2[...]).astype(BF)
            return carry

        lax.fori_loop(0, ROWS // 32, middle_rows, 0)

    def send_hidden():
        waiting["ht"] = share(ht, ht)

    def send_gradient():
        waiting["og"] = share(ogo, ogx)

    def arrived(name):
        for copy in waiting[name]:
            copy.wait_recv()

    def ff_cols(first, count):
        return wf[:, :, :, :, :, :, :, pl.ds(first, count)].reshape(WIDTH, count)

    def inner_columns(at, count):
        gg[:, pl.ds(at, count)] = nn(ogx[...], ff_cols(2 * SLICE + at, count)).astype(BF)

    def chunks(fn):
        def step(n, carry):
            fn(pl.multiple_of(n * 256, 256), 256)
            return carry

        lax.fori_loop(0, 5, step, 0)
        fn(1280, 128)

    def inner_gradient():
        chunks(inner_columns)

    steps = {
        "low": lower,
        "kvc": keys,
        "pls": send_plane,
        "lns": send_line,
        "lnw": take_line,
        "qc": queries,
        "att": attend,
        "oproj": project,
        "mid": middle,
        "hts": send_hidden,
        "htw": lambda: arrived("ht"),
        "ogs": send_gradient,
        "ogw": lambda: arrived("og"),
        "ds": streams["d"].settle,
        "gs": streams["g"].settle,
        "us": streams["u"].settle,
        "ig": inner_gradient,
    }
    for name in PLAN:
        if "." in name:
            advance(name)
        else:
            steps[name]()
    og_fly, ht_fly, out_copy = waiting["og"], waiting["ht"], waiting["out"]

    def gate_columns(at, count):
        cols = pl.ds(at, count)
        gate = nn(ht[...], ff_cols(at, count))
        up = nn(ht[...], ff_cols(SLICE + at, count))
        s = 1.0 / (1.0 + jnp.exp(-gate))
        swish = gate * s
        inner[:, cols] = (swish * up).astype(BF)
        d = gg[:, cols].astype(F32)
        gg[:, cols] = (d * up * s * (1.0 + gate * (1.0 - s))).astype(BF)
        ug[:, cols] = (d * swish).astype(BF)

    chunks(gate_columns)

    def ff_rows(n, at):
        return wf[n // 2, lax.rem(n, 2), :, :, :, :, :, pl.ds(at, SLICE)].reshape(256, SLICE)

    copies.sent(ht_fly)
    copies.sent(og_fly)

    def two_columns(n, carry):
        cols = pl.ds(pl.multiple_of(n * 256, 256), 256)
        ogx[:, cols] = (nt(gg[...], ff_rows(n, 0)) + nt(ug[...], ff_rows(n, SLICE))).astype(BF)
        return carry

    def give_back(src, dst, cols):
        return [
            copies.start(src.at[pl.ds(at, n), cols], dst.at[k // 2 - (k > 5), pl.ds(r, n), cols], device({"x": (4 - i) % 4, "y": (4 - j) % 4}))
            for k, (i, j, r, n, at) in enumerate(SHARES)
        ]

    two_fly = []
    for q in range(4):
        lax.fori_loop(2 * q, 2 * q + 2, two_columns, 0)
        two_fly += give_back(ogx, rbt, pl.ds(q * 512, 512))

    def block_columns(n, carry):
        cols = pl.ds(pl.multiple_of(n * 256, 256), 256)
        ht[:, cols] = nt(inner[...], ff_rows(n, 2 * SLICE)).astype(BF)
        return carry

    lax.fori_loop(0, 8, block_columns, 0)
    for copy in two_fly:
        copy.wait_recv()
    blk_fly = give_back(ht, rbb, pl.ds(0, WIDTH))

    def middle_back(i, acc):
        rows = pl.ds(i * 16, 16)
        t = ogx[rows, :].astype(F32)
        for k in range(3):
            t += rbt[k, rows, :].astype(F32)
        m = mid[rows, :]
        r = lax.rsqrt(jnp.mean(m * m, -1, keepdims=True) + EPSILON)
        n = m * r
        acc += jnp.sum(t * n, 0, keepdims=True)
        t = t * gain2[...]
        g = ogo[rows, :].astype(F32) + r * (t - n * jnp.mean(t * n, -1, keepdims=True))
        mgrad[rows, :] = g
        bg[c, rows, :] = g.astype(BF)
        return acc

    gain_mlp = lax.fori_loop(0, ROWS // 16, middle_back, jnp.zeros((1, WIDTH), F32))
    bg_copy = copies.start(bg.at[c], bg.at[c], sibling)
    bg_copy.wait_recv()
    bgv = bg.at[:, :, :]
    olg = nt(bgv[...].reshape(CHIP, WIDTH), ob2[...])
    olg_low = olg.astype(BF)

    def mixed_columns(n, carry):
        cols = pl.ds(pl.multiple_of(n * 256, 256), 256)
        wcols = pl.ds(pl.multiple_of(QKV + n * 256, 256), 256)
        m = nn(bg[...].reshape(CHIP, WIDTH), wa[:, :, :, :, :, wcols].reshape(WIDTH, 256))
        m += nn(olg_low, oac[:, cols])
        ngt[cols, :] = m.T.astype(BF)
        return carry

    lax.fori_loop(0, 4, mixed_columns, 0)
    lowo_t = lowo[...].astype(F32).T.astype(BF)
    olg_t = olg.T.astype(BF)
    apart[24:32] = 2.0 * nn(lowo_t[:16], bg[...].reshape(CHIP, WIDTH))[:8]
    red[72:80, :HALF] = nn(olg_t[:16], mixn[...])[:8]

    for k in range(4):
        sig[k] = jnp.zeros((AUG, 128), F32)

    def states_four(n, carry):
        g = n // 2
        rows = [pl.ds(pl.multiple_of(n * 256 + k * HEAD, HEAD), HEAD) for k in range(4)]
        for p in range(2):
            cols = slice(p * 128, (p + 1) * 128)
            left, right = [], []
            for k in range(4):
                h = (n * 4 + k) * 2 + p
                rden = den[h, :1]
                m = ngt[rows[k], cols].astype(F32)
                ng = (m * rden).astype(BF)
                dg = -jnp.sum(m * mixf[rows[k], cols], 0, keepdims=True) * rden
                ngt[rows[k], cols] = ng
                dgr[h, :1] = dg
                dq = (qfeat[rows[k], cols] * damp[h, :1]).astype(BF)
                right.append(jnp.concatenate([jnp.where(low_lane, dq, zero_low), jnp.where(low_lane, zero_low, dq)], 0))
                tail = jnp.where(lax.broadcasted_iota(jnp.int32, (AUG - HEAD, 128), 0) == 0, dg, 0.0).astype(BF)
                left.append(jnp.concatenate([ng, tail], 0))
            sig[g * 2 + p] = sig[g * 2 + p] + nt(lanes(left), lanes(right))
        return carry

    lax.fori_loop(0, 4, states_four, 0)
    sg_states = []
    for p in range(2):
        a, b = sig[p], sig[2 + p]
        sg_states.append(jnp.where(low_lane, a, pltpu.roll(b, 64, 1)))
        sg_states.append(jnp.where(low_lane, pltpu.roll(a, 64, 1), b))
    for s in range(4):
        st[s] = sg_states[s]
    folded = sg_states[3]
    for s in (2, 1, 0):
        folded = sg_states[s] + gates[s + 1] * folded
    fly = gather_plane(1, folded)

    for k in range(4):
        kacc[k] = jnp.zeros((HEAD, 128), F32)
        vacc[k] = jnp.zeros((HEAD, 128), F32)

    def back_four(n, carry):
        g = n // 2
        rows = [pl.ds(pl.multiple_of(n * 256 + k * HEAD, HEAD), HEAD) for k in range(4)]
        for p in range(2):
            cols = slice(p * 128, (p + 1) * 128)
            ngs = lanes([ngt[r, cols] for r in rows])
            dgs = [dgr[(n * 4 + k) * 2 + p, :1] for k in range(4)]
            dg = lanes(dgs)
            ws = lanes([wts[(n * 4 + k) * 2 + p] for k in range(4)])
            pt = nn(vnat[g, cols, :], jnp.concatenate([ngs, ngs], 0)) + dg
            sgr = (ws.astype(F32) * pt).astype(BF)
            tail = jnp.where(lax.broadcasted_iota(jnp.int32, (HEAD, 512), 0) == 0, dg, 0.0).astype(BF)
            both = split(nn(comb_t[g * 2 + p], jnp.concatenate([ngs, tail], 0)))
            for k in range(4):
                qg = jnp.where(low_lane, both[k][:HEAD], both[k][HEAD:]) * damp[(n * 4 + k) * 2 + p, :1]
                f = qfeat[rows[k], cols]
                qlg[rows[k], cols] = (f * (qg - jnp.sum(f * qg, 0, keepdims=True))).astype(BF)
            near = split(nn(kt[g, :, cols], sgr))
            for k in range(4):
                far = nn(fq[c * 16 + n * 4 + k], qlg[rows[k], cols])
                gt[rows[k], cols] = (near[k] * 0.125 + far).astype(BF)
            kacc[g * 2 + p] = kacc[g * 2 + p] + nt(lanes([qt[r, cols] for r in rows]), sgr)
            vacc[g * 2 + p] = vacc[g * 2 + p] + nt(ngs, ws)
        return carry

    lax.fori_loop(0, 2, back_four, 0)
    part, fly = fold_plane(1, fly)
    lax.fori_loop(2, 4, back_four, 0)
    suffix = fold_line(1, part, fly)
    states = [None, None, None, suffix]
    for s in (2, 1, 0):
        states[s] = gates[s + 1] * (states[s + 1] + st[s + 1])
    put_states(states, 4)

    for g in range(2):
        f_rows = slice(g * HEAD, (g + 1) * HEAD)
        for p in range(2):
            k = g * 2 + p
            cols = slice(p * 128, (p + 1) * 128)
            f = kfeat[f_rows, cols]
            both = nn(comb_t[4 + k], vt[g, :, cols])
            fg = jnp.where(low_lane, both[:HEAD], both[HEAD:]) * valid[:, cols]
            kl = (f * (fg - jnp.sum(f * fg, 0, keepdims=True))).astype(BF)
            qlg[HALF + g * HEAD : HALF + (g + 1) * HEAD, cols] = kl
            gt[HALF + g * HEAD : HALF + (g + 1) * HEAD, cols] = (kacc[k] * 0.125 + nn(fk[c * 2 + g], kl)).astype(BF)
            fl = f.astype(BF)
            stack = jnp.concatenate([jnp.where(low_lane, fl, zero_low), jnp.where(low_lane, zero_low, fl)], 0)
            gt[HALF + NARROW + g * HEAD : HALF + NARROW + (g + 1) * HEAD, cols] = (
                vacc[k] + nn(comb[4 + k, :HEAD], stack)
            ).astype(BF)

    def feat_pairs(n, carry):
        rows = pl.ds(pl.multiple_of(n * 128, 128), 128)
        r = nt(qt[rows, :], qlg[rows, :])
        red[0:64, rows] = jnp.where(low_lane, r[:HEAD], r[HEAD:])
        return carry

    lax.fori_loop(0, 8, feat_pairs, 0)
    r = nt(kt[...].reshape(128, CHIP), qlg[HALF:, :])
    red[0:64, HALF : HALF + 128] = jnp.where(low_lane, r[:HEAD], r[HEAD:])

    lowg_t = nn(ball[...], gt[...])
    lowg[...] = lowg_t.T.astype(BF)
    lowg_t = lowg_t.astype(BF)
    low_t = low[...].astype(F32).T.astype(BF)
    up = 2.0 * nt(low_t[:32], gt[...])
    red[64:72, :HALF] = up[0:8, :HALF]
    red[64:72, HALF : HALF + NARROW] = up[8:16, HALF : HALF + NARROW]
    red[64:72, HALF + NARROW :] = up[16:24, HALF + NARROW :]
    apart[0:24] = nn(lowg_t[:32], hid1[...])[:24]
    apart[32:40] = jnp.where(lax.broadcasted_iota(jnp.int32, (8, 1), 0) == 1, gain_mlp, 0.0)

    def grad_rows(n, carry):
        rows = pl.ds(pl.multiple_of(n * 256, 256), 256)
        gnat[:, rows] = gt[rows, :].astype(F32).T.astype(BF)
        return carry

    lax.fori_loop(0, 5, grad_rows, 0)

    def one_columns(n, carry):
        cols = pl.ds(pl.multiple_of(n * 256, 256), 256)
        w = wa[n // 2, pl.ds(pl.multiple_of(lax.rem(n, 2) * 2, 2), 2), :, :, :, 0:QKV].reshape(256, QKV)
        o = nt(gnat[...], w) + nn(lowg[...], aall[:, cols])
        normed = [tok2[side, :, cols].astype(F32) * r1[side, :, :1] for side in range(2)]
        apart[32:33, cols] = jnp.sum(o[:ROWS] * normed[0] + o[ROWS:] * normed[1], 0, keepdims=True)
        ones[:, cols] = jnp.where(c == 0, o[:ROWS], o[ROWS:])
        outs[:, cols] = jnp.where(c == 0, o[ROWS:], o[:ROWS]).astype(BF)
        return carry

    copies.sent([out_copy])
    lax.fori_loop(0, 8, one_columns, 0)
    one_copy = copies.start(outs, outr, sibling)

    theirs = pl.ds(pl.multiple_of((1 - c) * HALF, HALF), HALF)
    mine = pl.ds(pl.multiple_of(c * HALF, HALF), HALF)
    a_copy = copies.start(apart.at[:, theirs], asib, sibling)
    red[72:80, HALF:] = jnp.zeros((8, PIECE - HALF), F32)
    red[0:64, HALF + 128 :] = jnp.zeros((64, 128), F32)
    red[80:128, HALF:] = jnp.zeros((48, PIECE - HALF), F32)
    red[120:128, :HALF] = jnp.zeros((8, HALF), F32)
    a_copy.wait_recv()
    red[80:120, :HALF] = apart[:, mine] + asib[...]

    def fold_piece(k, carry):
        rows = pl.ds(pl.multiple_of(k * 8, 8), 8)
        redb[k] = jnp.concatenate([red[rows, : PIECE // 2], red[rows, PIECE // 2 :]], 0).astype(BF)
        return carry

    lax.fori_loop(0, 16, fold_piece, 0)
    fly = []
    for i in range(4):
        for j in range(4):
            if i + j > 0:
                to = wrap(x + i) * 4 + wrap(y + j)
                fly.append(copies.start(redb.at[to], rr.at[plane], device({"x": i, "y": j})))
    rr[plane] = redb[plane]
    for copy in blk_fly:
        copy.wait_recv()

    def block_rows(i, carry):
        rows = pl.ds(i * 16, 16)
        t = mid[rows, :] + ht[rows, :].astype(F32)
        for k in range(3):
            t += rbb[k, rows, :].astype(F32)
        blk_out[rows, :] = t.astype(BF)
        return carry

    lax.fori_loop(0, ROWS // 16, block_rows, 0)
    for copy in fly:
        copy.wait_recv()
    total = rr[0].astype(F32)
    for k in range(1, 16):
        total += rr[k].astype(F32)
    rz[z] = total
    line = [copies.start(rz.at[z], rz.at[z], device({"z": i})) for i in (1, 2, 3)]
    one_copy.wait_recv()

    def token_rows(i, carry):
        rows = pl.ds(i * 16, 16)
        o = ones[rows, :] + outr[rows, :].astype(F32)
        t = tok2[c, rows, :].astype(F32)
        r = r1[c, rows, :1]
        n = t * r
        o = o * gain1[...]
        gtok_out[rows, :] = (mgrad[rows, :] + r * (o - n * jnp.mean(o * n, -1, keepdims=True))).astype(BF)
        return carry

    lax.fori_loop(0, ROWS // 32, token_rows, 0)
    for copy in line:
        copy.wait_recv()
    total = (rz[0] + rz[1]) + (rz[2] + rz[3])
    fin[c, plane] = total.astype(BF)
    piece = fin.at[c, plane]
    fly = [
        copies.start(piece, piece, device({"x": i, "y": j})) for i in range(4) for j in range(4) if i + j > 0
    ]
    lax.fori_loop(ROWS // 32, ROWS // 16, token_rows, 0)
    for copy in fly:
        copy.wait_recv()
    f_copy = copies.start(fin.at[c], fin.at[c], sibling)
    f_copy.wait_recv()

    def wide(k, side):
        got = fin[side, k].astype(F32)
        return got[:8], got[8:]

    def feat_out(k, carry):
        rows = pl.ds(pl.multiple_of(k * 8, 8), 8)
        for side in range(2):
            left, right = wide(k, side)
            for j in range(9):
                v = left[:, j * 128 : (j + 1) * 128] if j < 5 else right[:, (j - 5) * 128 : (j - 4) * 128]
                out, head = (fq_out, side * 16 + 2 * j) if j < 8 else (fk_out, side * 2)
                out[head, rows, :] = v[:, :64]
                out[head + 1, rows, :] = pltpu.roll(v, 64, 1)[:, :64]
        return carry

    lax.fori_loop(0, 8, feat_out, 0)
    rest = HALF - PIECE // 2
    for side in range(2):
        for k, out in ((8, qb_out), (9, oa_out), (10, qa_out), (11, ka_out), (12, va_out), (13, ob_out)):
            left, right = wide(k, side)
            out[:, side * HALF : side * HALF + PIECE // 2] = left
            out[:, side * HALF + PIECE // 2 : (side + 1) * HALF] = right[:, :rest]
            if k == 8:
                kb_out[:, side * NARROW : (side + 1) * NARROW] = right[:, rest : rest + NARROW]
                vb_out[:, side * NARROW : (side + 1) * NARROW] = right[:, rest + NARROW :]
        left, right = wide(14, side)
        row = jnp.concatenate([left, right[:, :rest]], 1)
        for k, out in ((0, gain_a_out), (1, gain_b_out)):
            for i in range(8):
                out[side * 8 + i : side * 8 + i + 1, :] = row[k : k + 1, i * 128 : (i + 1) * 128]
    copies.drain()


N_COPIES = 301
N_SENDS = 64


def scratch():
    v = pltpu.VMEM
    return [
        v((4, 4, 4, 2, 16, ATT), BF),
        v((4, 2, 2, 2, 2, 2, 16, 3 * SLICE), BF),
        v((2, 2, 16, 3 * SLICE), BF),
        v((2, ROWS, WIDTH), BF),
        v((ROWS, WIDTH), BF),
        v((8, WIDTH), F32),
        v((2, ROWS, 128), F32),
        v((128, WIDTH), BF),
        v((128, QKV), BF),
        v((128, HALF), BF),
        v((128, WIDTH), BF),
        v((4, 16, 128), F32),
        v((2, 8, 128), F32),
        v((2, 128, 128), F32),
        v((CHIP, WIDTH), BF),
        v((CHIP, 128), BF),
        v((HALF, CHIP), BF),
        v((2, HEAD, CHIP), BF),
        v((2, 128, CHIP), BF),
        v((2, CHIP, 128), BF),
        v((2, CHIP, 128), BF),
        v((128, CHIP), F32),
        v((4, AUG, 128), F32),
        v((8, AUG, 128), BF),
        v((8, 128, 128), BF),
        v((32, 128, 128), BF),
        v((HALF, CHIP), F32),
        v((HALF, CHIP), F32),
        v((32, 8, 128), F32),
        v((32, 8, 128), F32),
        v((CHIP, HALF), BF),
        v((CHIP, 128), BF),
        v((ROWS, WIDTH), BF),
        v((ROWS, WIDTH), BF),
        v((ROWS, WIDTH), F32),
        v((512, WIDTH), BF),
        v((512, WIDTH), BF),
        v((512, SLICE), BF),
        v((512, SLICE), BF),
        v((512, SLICE), BF),
        v((3, ROWS, WIDTH), BF),
        v((3, ROWS, WIDTH), BF),
        v((ROWS, WIDTH), F32),
        v((2, ROWS, WIDTH), BF),
        v((HALF, CHIP), BF),
        v((32, 8, 128), F32),
        v((4, AUG, 128), F32),
        v((HALF + 128, CHIP), BF),
        v((QKV, CHIP), BF),
        v((CHIP, QKV), BF),
        v((CHIP, 128), BF),
        v((ROWS, WIDTH), F32),
        v((4, HEAD, 128), F32),
        v((4, HEAD, 128), F32),
        v((2, AUG, 128), BF),
        v((2, 16, AUG, 128), BF),
        v((2, AUG, 128), BF),
        v((2, 3, AUG, 128), BF),
        v((128, PIECE), F32),
        v((16, 16, PIECE // 2), BF),
        v((16, 16, PIECE // 2), BF),
        v((4, 16, PIECE // 2), F32),
        v((2, 16, 16, PIECE // 2), BF),
        v((40, WIDTH), F32),
        v((40, HALF), F32),
        pltpu.SemaphoreType.DMA((N_SENDS,)),
        pltpu.SemaphoreType.DMA((N_COPIES,)),
        pltpu.SemaphoreType.DMA((15,)),
    ]


def body(
    tokens, sequence_lengths, attention_gain, query_weight, key_weight, value_weight, output_weight_flipped,
    query_adapter_down, query_adapter_up, key_adapter_down, key_adapter_up, value_adapter_down, value_adapter_up,
    output_adapter_down, output_adapter_up, query_feature_map, key_feature_map, feedforward_gain,
    gate_weight, up_weight, down_weight_flipped, output_gradient,
):
    vmem = pl.BlockSpec(memory_space=pltpu.VMEM)
    smem = pl.BlockSpec(memory_space=pltpu.SMEM)
    anywhere = pl.BlockSpec(memory_space=pl.ANY)

    def array(*shape, dtype=F32):
        return jax.ShapeDtypeStruct(shape, dtype)

    out = pl.pallas_call(
        kernel,
        out_shape=(
            array(ROWS, WIDTH, dtype=BF), array(ROWS, WIDTH, dtype=BF), array(16, 128),
            array(RANK, WIDTH), array(RANK, WIDTH), array(RANK, WIDTH), array(RANK, 2 * NARROW),
            array(RANK, WIDTH), array(RANK, 2 * NARROW), array(RANK, WIDTH), array(RANK, WIDTH),
            array(QUERY_HEADS, HEAD, HEAD), array(KEY_VALUE_HEADS, HEAD, HEAD), array(16, 128),
        ),
        in_specs=[anywhere, smem, vmem] + [anywhere] * 4 + [vmem] * 11 + [anywhere] * 4,
        out_specs=(vmem,) * 14,
        scratch_shapes=scratch(),
        compiler_params=pltpu.CompilerParams(
            collective_id=0, has_side_effects=True, vmem_limit_bytes=64 * 1024 * 1024
        ),
    )(
        tokens, sequence_lengths, attention_gain.reshape(16, 128),
        query_weight, key_weight, value_weight, output_weight_flipped,
        query_adapter_down.T, query_adapter_up, key_adapter_down.T, key_adapter_up, value_adapter_down.T,
        value_adapter_up, output_adapter_down.T, output_adapter_up, query_feature_map, key_feature_map,
        feedforward_gain.reshape(16, 128), gate_weight, up_weight, down_weight_flipped, output_gradient,
    )
    (
        block_out, grad_tokens, gain_attn, qa, qb, ka, kb, va, vb, oa, ob, feat_q, feat_k, gain_mlp,
    ) = out
    return (
        block_out, grad_tokens, gain_attn.reshape(WIDTH), qa.T, qb, ka.T, kb, va.T, vb, oa.T, ob, feat_q, feat_k,
        gain_mlp.reshape(WIDTH),
    )


def solution(mesh):
    split, whole = P("seq", None), P()
    return jax.shard_map(
        body,
        mesh=mesh,
        in_specs=(
            (split, whole, whole) + (split,) * 4 + (whole,) * 11 + (split,) * 4
        ),
        out_specs=(split, split) + (whole,) * 12,
        check_vma=False,
    )
```

time: 286 us -> 201 us (0.70)
  Pallas kernels: 247 us -> 188 us
  other arithmetic: 18.2 us -> 0 us
  local copies, waits for them, and re-layouts: 18.8 us -> 11.5 us
    pallas_call x1, Pallas kernels: 247 us -> 188 us  [body(): pl.pallas_call(kernel, out_shape=(array(ROWS, WIDTH, dtype=BF), array(ROW...]
    unnamed x17 -> x40, local copies, waits for them, and re-layouts: 4.02 us -> 11.5 us
    dynamic_slice x5 -> x0, local copies, waits for them, and re-layouts: 4 us -> none  [the longest x3 2.83 us: core(): return lax.dynamic_slice_in_dim(array, c * count, count, axis)]
    concatenate x6 -> x0, other arithmetic: 3.94 us -> none  [the longest x3 1.83 us: columns(): jnp.concatenate([red[0, rows, first:first + count], red[1, rows, first:fi...]
where the time goes in v3:
time: 201 us; the launch traced here: 200 us
  Pallas kernels  188 us (94%)
  local copies, waits for them, and re-layouts  11.5 us (6%)
    pallas_call x1, Pallas kernels, body(): pl.pallas_call(kernel, out_shape=(array(ROWS, WIDTH, dtype=BF), array(ROW...  188 us
    unnamed x40, local copies, waits for them, and re-layouts  11.5 us

profile of v3, /device:TPU:1, one launch (start us, length us, event | category | flops | bytes accessed | tf_op | source)
XLA Modules:
  0.0 200.1 jit_solution(15489326788054954321)
XLA Ops:
  0.7 187.9 %shard_map.317 = (bf16[128,2048]{1,0:T(8,128)(2,1)}, bf16[128,2048]{1,0:T(8,128)(2,1)}, f32[16,128]{1,0:T(8,128)}, f32[8,2048]{1,0:T(8,128)}, f32[8,2048]{1,0:T(...) custom-call(bf16[128,2048]{1,0:T(8,128)(2,1)} %tok.1, ...), custom_call_target="tpu_custom_call" | custom-call | tf_op jit(solution)/shard_map/pallas_call | solution.py:1033
  188.5 0.0 copy-start.1
  188.6 0.0 copy-start.12
  188.6 1.9 copy.50
  190.5 0.8 copy.51
  191.3 0.6 copy.52
  191.9 0.6 copy.53
  192.6 0.2 copy-done.7
  192.8 0.6 copy.54
  193.4 0.2 copy-done.6
  193.7 0.6 copy.55
  194.3 0.1 copy-done.11
  194.3 0.6 copy.56
  195.0 0.6 copy.57
  195.6 0.1 copy-done.10
  195.6 0.6 copy.58
  196.2 0.6 copy.59
  196.9 0.2 copy-done.3
  197.1 0.6 copy.60
  197.7 1.0 copy.61
  198.7 0.1 copy-done.2
  198.8 0.7 copy.62
  199.4 0.0 copy-done.9
  199.5 0.6 copy.63
  (17 shorter events, 0.0 us)
Async XLA Ops:
  188.5 2.0 copy-start.1
  188.6 2.8 %copy-start.12 = (f32[16,128]{1,0:T(8,128)S(1)}, f32[16,128]{1,0:T(8,128)}, u32[]{:S(2)}) copy-start(f32[16,128]{1,0:T(8,128)} %get-tuple-element.30) | copy-start | bytes 24580
  188.6 3.4 %copy-start.8 = (f32[8,2048]{1,0:T(8,128)S(1)}, f32[8,2048]{1,0:T(8,128)}, u32[]{:S(2)}) copy-start(f32[8,2048]{1,0:T(8,128)} %get-tuple-element.31) | copy-start | bytes 196612
  190.5 7.2 %copy-start = (f32[32,64,64]{2,1,0:T(8,128)S(1)}, f32[32,64,64]{2,1,0:T(8,128)}, u32[]{:S(2)}) copy-start(f32[32,64,64]{2,1,0:T(8,128)} %get-tuple-element.67) | copy-start | bytes 1572868
  191.9 0.9 copy-start.7
  192.8 0.9 copy-start.6
  193.6 0.7 copy-start.11
  193.7 1.3 copy-start.5
  194.9 0.7 copy-start.10
  194.9 1.3 copy-start.4
  196.2 0.9 copy-start.3
  197.7 1.0 copy-start.2
  198.8 0.7 copy-start.9

commit v4 on v3

--- a/solution.py
+++ b/solution.py
@@ -103,7 +103,7 @@
         for part, (order, first, count) in enumerate(self.parts):
             axis = order[phase]
             own = self.block(order, phase, self.where[axis], first, count)
-            steps = (1, 3) if phase == 2 and not self.straight else (1, 3, 2)
+            steps = (1, 3) if phase > 0 and not self.straight else (1, 3, 2)
             self.flying[phase, part] = [self.copies.start(own, own, self.device({axis: step})) for step in steps]
 
     def middle(self, phase):
@@ -210,20 +210,19 @@
             copy.wait_recv()
 
 
-EARLY = ("kv.b0", "q.b0", "o.b0", "d.b0", "g.b0",)
+EARLY = ("kv.b0", "o.b0", "q.b0",)
 PLAN = (
-    "kv.e0", "u.b0", "kv.b1", "q.e0", "o.e0", "q.b1", "d.e0", "d.b1", "u.e0", "g.e0", "o.b1", "d.e1",
-    "q.e1", "g.b1", "kv.e1", "u.b1", "q.b2", "kv.b2", "d.b2", "g.e1", "d.m2", "q.m2", "o.e1", "g.b2",
-    "kv.e2", "low", "kvc", "pls", "o.b2", "u.e1", "lns", "d.e2", "u.b2", "q.e2", "lnw", "qc",
-    "o.m2", "ogs", "g.m2", "att", "o.e2", "ds", "oproj", "mid", "hts", "u.m2", "g.e2", "ogw",
-    "ig", "u.e2", "gs", "us", "htw",
+    "d.b0", "kv.e0", "kv.b1", "g.b0", "u.b0", "q.e0", "low", "o.e0", "d.e0", "d.b1", "q.b1", "o.b1",
+    "q.m1", "d.e1", "u.e0", "d.b2", "kv.e1", "g.e0", "g.b1", "kv.b2", "u.b1", "q.e1", "q.b2", "o.m1",
+    "g.e1", "u.e1", "d.m2", "kv.e2", "g.b2", "kvc", "pls", "o.e1", "o.b2", "lns", "d.e2", "q.m2",
+    "u.b2", "o.m2", "lnw", "q.e2", "ogs", "qc", "g.m2", "att", "o.e2", "ds", "oproj", "mid",
+    "hts", "u.m2", "ogw", "ig", "g.e2", "u.e2", "gs", "us", "htw",
 )
 
 
 def kernel(
     tok, lens, gain_a, qw, kw, vw, ow, qa, qb, ka, kb, va, vb, oa, ob, fq, fk, gain_b, gw, uw, dw, og,
-    blk_out, gtok_out, gain_a_out, qa_out, qb_out, ka_out, kb_out, va_out, vb_out, oa_out, ob_out, fq_out, fk_out,
-    gain_b_out,
+    blk_out, gtok_out, red_out,
     wa, wf, stage, tok2, ogo, gains, r1, aall, ball, oac, ob2, masks, far_masks, bias, hid1, low, qt, kt, vt, knat, vnat,
     kfeat, st, comb, comb_t, wts, qfeat, mixf, damp, den, mixn, lowo, outs, outr, mid, ht, ogx, gg, inner, ug, rbt, rbb,
     mgrad, bg, ngt, dgr, sig, qlg, gt, gnat, lowg, ones, kacc, vacc, fsend, frecv, hsend, hrecv, red, redb, rr, rz, fin,
@@ -250,8 +249,6 @@
     peers += [device({"z": i}) for i in (1, 2, 3)]
     for peer in peers:
         pl.semaphore_signal(barrier, inc=1, device_id=(peer,), device_id_type=MESH)
-    pl.semaphore_wait(barrier, len(peers))
-
     copies = Copies(send, recv)
     local = []
 
@@ -261,45 +258,14 @@
         local.append(copy)
         return copy
 
-    tok_copy = copies.start(tok, tok2.at[c], sibling)
-    first = []
     own = wa.at[z, x, y, c]
-    for src, at, count in ((kw, HALF, NARROW), (vw, HALF + NARROW, NARROW), (qw, 0, HALF), (ow, QKV, HALF)):
+    pieces = ((kw, HALF, NARROW), (vw, HALF + NARROW, NARROW), (qw, 0, HALF), (ow, QKV, HALF))
+    for src, at, count in pieces:
         mine = src.at[:, pl.ds(pl.multiple_of(c * count, count), count)]
-        other = src.at[:, pl.ds(pl.multiple_of((1 - c) * count, count), count)]
-        dst = own.at[:, pl.ds(at, count)]
-        here(mine, dst)
-        first.append(copies.start(other, dst, sibling))
+        here(mine, own.at[:, pl.ds(at, count)])
     here(tok, tok2.at[c])
     here(og, ogx.at[pl.ds(0, ROWS)])
     here(og, ogo)
-
-    where = {"z": z, "x": x, "y": y, "c": c}
-    streams = {
-        "kv": Heads(copies, wa, where, device, (("xzy", 1024, 128), ("yzx", 1152, 128)), straight=True),
-        "q": Heads(copies, wa, where, device, [(o, k * 256, 256) for k, o in enumerate(("xzy", "zyx", "zxy", "yzx"))]),
-        "o": Heads(
-            copies, wa, where, device, [(o, QKV + k * 256, 256) for k, o in enumerate(("xzy", "zyx", "zxy", "yzx"))]
-        ),
-        "d": Units(
-            copies, here, wf, stage, where, device, sibling,
-            (("xy", dw, 0, 2 * SLICE, 768), ("yx", dw, 768, 2 * SLICE + 768, 640)),
-        ),
-        "g": Units(copies, here, wf, stage, where, device, sibling, (("xy", gw, 0, 0, SLICE),)),
-        "u": Units(copies, here, wf, stage, where, device, sibling, (("yx", uw, 0, SLICE, SLICE),)),
-    }
-    for k in range(4):
-        local[k].wait()
-        first[k].wait_recv()
-    waiting = {}
-
-    def advance(name):
-        stream, step = name.split(".")
-        stream = streams[stream]
-        {"b": stream.begin, "m": stream.middle, "e": stream.end}[step[0]](int(step[1]))
-
-    for name in EARLY:
-        advance(name)
 
     for k, src in enumerate((gain_a, gain_b)):
         g = src[...].astype(F32)
@@ -368,6 +334,37 @@
         seen = (iu <= it) & ((iu < 64) == (it < 64)) & (lax.rem(iu, STRETCH) < room)
         bias[p] = jnp.where(seen, 0.0, -1e30)
 
+    pl.semaphore_wait(barrier, len(peers))
+    first = []
+    for src, at, count in pieces:
+        other = src.at[:, pl.ds(pl.multiple_of((1 - c) * count, count), count)]
+        first.append(copies.start(other, own.at[:, pl.ds(at, count)], sibling))
+    tok_copy = copies.start(tok, tok2.at[c], sibling)
+    where = {"z": z, "x": x, "y": y, "c": c}
+    streams = {
+        "kv": Heads(copies, wa, where, device, (("xzy", 1024, 128), ("yzx", 1152, 128)), straight=True),
+        "q": Heads(copies, wa, where, device, (("xzy", 0, 512), ("yzx", 512, 512))),
+        "o": Heads(copies, wa, where, device, (("zxy", QKV, 512), ("zyx", QKV + 512, 512))),
+        "d": Units(
+            copies, here, wf, stage, where, device, sibling,
+            (("xy", dw, 0, 2 * SLICE, 768), ("yx", dw, 768, 2 * SLICE + 768, 640)),
+        ),
+        "g": Units(copies, here, wf, stage, where, device, sibling, (("xy", gw, 0, 0, SLICE),)),
+        "u": Units(copies, here, wf, stage, where, device, sibling, (("yx", uw, 0, SLICE, SLICE),)),
+    }
+    for k in range(4):
+        local[k].wait()
+        first[k].wait_recv()
+    waiting = {}
+
+    def advance(name):
+        stream, step = name.split(".")
+        stream = streams[stream]
+        {"b": stream.begin, "m": stream.middle, "e": stream.end}[step[0]](int(step[1]))
+
+    for name in EARLY:
+        advance(name)
+
     for copy in local[4:7]:
         copy.wait()
     tok_copy.wait_recv()
@@ -582,19 +579,8 @@
     def ff_cols(first, count):
         return wf[:, :, :, :, :, :, :, pl.ds(first, count)].reshape(WIDTH, count)
 
-    def inner_columns(at, count):
-        gg[:, pl.ds(at, count)] = nn(ogx[...], ff_cols(2 * SLICE + at, count)).astype(BF)
-
-    def chunks(fn):
-        def step(n, carry):
-            fn(pl.multiple_of(n * 256, 256), 256)
-            return carry
-
-        lax.fori_loop(0, 5, step, 0)
-        fn(1280, 128)
-
     def inner_gradient():
-        chunks(inner_columns)
+        gg[...] = nn(ogx[...], ff_cols(2 * SLICE, SLICE)).astype(BF)
 
     steps = {
         "low": lower,
@@ -622,18 +608,19 @@
             steps[name]()
     og_fly, ht_fly, out_copy = waiting["og"], waiting["ht"], waiting["out"]
 
-    def gate_columns(at, count):
-        cols = pl.ds(at, count)
-        gate = nn(ht[...], ff_cols(at, count))
-        up = nn(ht[...], ff_cols(SLICE + at, count))
-        s = 1.0 / (1.0 + jnp.exp(-gate))
+    def activate(gate, up, cols):
+        s = 0.5 * jnp.tanh(0.5 * gate) + 0.5
         swish = gate * s
         inner[:, cols] = (swish * up).astype(BF)
         d = gg[:, cols].astype(F32)
         gg[:, cols] = (d * up * s * (1.0 + gate * (1.0 - s))).astype(BF)
         ug[:, cols] = (d * swish).astype(BF)
 
-    chunks(gate_columns)
+    for n in range(5):
+        cols = slice(n * 256, (n + 1) * 256)
+        activate(nn(ht[...], ff_cols(n * 256, 256)), nn(ht[...], ff_cols(SLICE + n * 256, 256)), cols)
+    both = nn(ht[...], jnp.concatenate([ff_cols(1280, 128), ff_cols(SLICE + 1280, 128)], 1))
+    activate(both[:, :128], both[:, 128:], slice(1280, SLICE))
 
     def ff_rows(n, at):
         return wf[n // 2, lax.rem(n, 2), :, :, :, :, :, pl.ds(at, SLICE)].reshape(256, SLICE)
@@ -653,19 +640,20 @@
         ]
 
     two_fly = []
-    for q in range(4):
-        lax.fori_loop(2 * q, 2 * q + 2, two_columns, 0)
-        two_fly += give_back(ogx, rbt, pl.ds(q * 512, 512))
+    for at, end in ((0, 1), (1, 3), (3, 5), (5, 8)):
+        lax.fori_loop(at, end, two_columns, 0)
+        two_fly += give_back(ogx, rbt, pl.ds(at * 256, (end - at) * 256))
 
     def block_columns(n, carry):
         cols = pl.ds(pl.multiple_of(n * 256, 256), 256)
         ht[:, cols] = nt(inner[...], ff_rows(n, 2 * SLICE)).astype(BF)
         return carry
 
-    lax.fori_loop(0, 8, block_columns, 0)
+    lax.fori_loop(0, 4, block_columns, 0)
+    blk_fly = give_back(ht, rbb, pl.ds(0, HALF))
+    lax.fori_loop(4, 8, block_columns, 0)
     for copy in two_fly:
         copy.wait_recv()
-    blk_fly = give_back(ht, rbb, pl.ds(0, WIDTH))
 
     def middle_back(i, acc):
         rows = pl.ds(i * 16, 16)
@@ -698,11 +686,6 @@
         return carry
 
     lax.fori_loop(0, 4, mixed_columns, 0)
-    lowo_t = lowo[...].astype(F32).T.astype(BF)
-    olg_t = olg.T.astype(BF)
-    apart[24:32] = 2.0 * nn(lowo_t[:16], bg[...].reshape(CHIP, WIDTH))[:8]
-    red[72:80, :HALF] = nn(olg_t[:16], mixn[...])[:8]
-
     for k in range(4):
         sig[k] = jnp.zeros((AUG, 128), F32)
 
@@ -739,6 +722,7 @@
     for s in (2, 1, 0):
         folded = sg_states[s] + gates[s + 1] * folded
     fly = gather_plane(1, folded)
+    blk_fly += give_back(ht, rbb, pl.ds(HALF, HALF))
 
     for k in range(4):
         kacc[k] = jnp.zeros((HEAD, 128), F32)
@@ -769,9 +753,46 @@
             vacc[g * 2 + p] = vacc[g * 2 + p] + nt(ngs, ws)
         return carry
 
-    lax.fori_loop(0, 2, back_four, 0)
+    lax.fori_loop(0, 4, back_four, 0)
+    lowo_t = lowo[...].astype(F32).T.astype(BF)
+    olg_t = olg.T.astype(BF)
+    apart[24:32] = 2.0 * nn(lowo_t[:16], bg[...].reshape(CHIP, WIDTH))[:8]
+    red[72:80, :HALF] = nn(olg_t[:16], mixn[...])[:8]
+
+
+    def grad_rows(n, carry):
+        rows = pl.ds(pl.multiple_of(n * 256, 256), 256)
+        gnat[:, rows] = gt[rows, :].astype(F32).T.astype(BF)
+        return carry
+
+    lax.fori_loop(0, 4, grad_rows, 0)
+
+    def feat_pairs(n, carry):
+        rows = pl.ds(pl.multiple_of(n * 128, 128), 128)
+        r = nt(qt[rows, :], qlg[rows, :])
+        red[0:64, rows] = jnp.where(low_lane, r[:HEAD], r[HEAD:])
+        return carry
+
+    lax.fori_loop(0, 8, feat_pairs, 0)
+
     part, fly = fold_plane(1, fly)
-    lax.fori_loop(2, 4, back_four, 0)
+
+    def one_queries(n, carry):
+        w = wa[n // 2, pl.ds(pl.multiple_of(lax.rem(n, 2) * 2, 2), 2), :, :, :, 0:HALF].reshape(256, HALF)
+        o = nt(gnat[:, :HALF], w)
+        rows = pl.ds(pl.multiple_of(lax.rem(n, 4) * 256, 256), 256)
+
+        @pl.when(n < 4)
+        def _():
+            qfeat[rows, :] = o
+
+        @pl.when(n >= 4)
+        def _():
+            mixf[rows, :] = o
+
+        return carry
+
+    lax.fori_loop(0, 8, one_queries, 0)
     suffix = fold_line(1, part, fly)
     states = [None, None, None, suffix]
     for s in (2, 1, 0):
@@ -795,51 +816,50 @@
                 vacc[k] + nn(comb[4 + k, :HEAD], stack)
             ).astype(BF)
 
-    def feat_pairs(n, carry):
-        rows = pl.ds(pl.multiple_of(n * 128, 128), 128)
-        r = nt(qt[rows, :], qlg[rows, :])
-        red[0:64, rows] = jnp.where(low_lane, r[:HEAD], r[HEAD:])
-        return carry
-
-    lax.fori_loop(0, 8, feat_pairs, 0)
-    r = nt(kt[...].reshape(128, CHIP), qlg[HALF:, :])
-    red[0:64, HALF : HALF + 128] = jnp.where(low_lane, r[:HEAD], r[HEAD:])
-
     lowg_t = nn(ball[...], gt[...])
     lowg[...] = lowg_t.T.astype(BF)
     lowg_t = lowg_t.astype(BF)
+
+    grad_rows(4, 0)
+
+    def one_columns(n, had):
+        cols = pl.ds(pl.multiple_of(n * 256, 256), 256)
+        w = wa[n // 2, pl.ds(pl.multiple_of(lax.rem(n, 2) * 2, 2), 2), :, :, :, HALF:QKV].reshape(256, 2 * NARROW)
+        o = had[pl.ds(pl.multiple_of(lax.rem(n, 4) * 256, 256), 256), :]
+        o = o + nt(gnat[:, HALF:], w) + nn(lowg[...], aall[:, cols])
+        normed = [tok2[side, :, cols].astype(F32) * r1[side, :, :1] for side in range(2)]
+        apart[32:33, cols] = jnp.sum(o[:ROWS] * normed[0] + o[ROWS:] * normed[1], 0, keepdims=True)
+        ones[:, cols] = jnp.where(c == 0, o[:ROWS], o[ROWS:])
+        outs[:, cols] = jnp.where(c == 0, o[ROWS:], o[:ROWS]).astype(BF)
+
+    def one_first(n, carry):
+        one_columns(n, qfeat)
+        return carry
+
+    def one_second(n, carry):
+        one_columns(n, mixf)
+        return carry
+
+    apart[0:24] = nn(lowg_t[:32], hid1[...])[:24]
+    apart[32:40] = jnp.where(lax.broadcasted_iota(jnp.int32, (8, 1), 0) == 1, gain_mlp, 0.0)
+    copies.sent([out_copy])
+    lax.fori_loop(0, 4, one_first, 0)
+    lax.fori_loop(4, 8, one_second, 0)
+    one_copy = copies.start(outs, outr, sibling)
+
+    theirs = pl.ds(pl.multiple_of((1 - c) * HALF, HALF), HALF)
+    mine = pl.ds(pl.multiple_of(c * HALF, HALF), HALF)
+    a_copy = copies.start(apart.at[:, theirs], asib, sibling)
+
+    r = nt(kt[...].reshape(128, CHIP), qlg[HALF:, :])
+    red[0:64, HALF : HALF + 128] = jnp.where(low_lane, r[:HEAD], r[HEAD:])
+
     low_t = low[...].astype(F32).T.astype(BF)
     up = 2.0 * nt(low_t[:32], gt[...])
     red[64:72, :HALF] = up[0:8, :HALF]
     red[64:72, HALF : HALF + NARROW] = up[8:16, HALF : HALF + NARROW]
     red[64:72, HALF + NARROW :] = up[16:24, HALF + NARROW :]
-    apart[0:24] = nn(lowg_t[:32], hid1[...])[:24]
-    apart[32:40] = jnp.where(lax.broadcasted_iota(jnp.int32, (8, 1), 0) == 1, gain_mlp, 0.0)
-
-    def grad_rows(n, carry):
-        rows = pl.ds(pl.multiple_of(n * 256, 256), 256)
-        gnat[:, rows] = gt[rows, :].astype(F32).T.astype(BF)
-        return carry
-
-    lax.fori_loop(0, 5, grad_rows, 0)
-
-    def one_columns(n, carry):
-        cols = pl.ds(pl.multiple_of(n * 256, 256), 256)
-        w = wa[n // 2, pl.ds(pl.multiple_of(lax.rem(n, 2) * 2, 2), 2), :, :, :, 0:QKV].reshape(256, QKV)
-        o = nt(gnat[...], w) + nn(lowg[...], aall[:, cols])
-        normed = [tok2[side, :, cols].astype(F32) * r1[side, :, :1] for side in range(2)]
-        apart[32:33, cols] = jnp.sum(o[:ROWS] * normed[0] + o[ROWS:] * normed[1], 0, keepdims=True)
-        ones[:, cols] = jnp.where(c == 0, o[:ROWS], o[ROWS:])
-        outs[:, cols] = jnp.where(c == 0, o[ROWS:], o[:ROWS]).astype(BF)
-        return carry
-
-    copies.sent([out_copy])
-    lax.fori_loop(0, 8, one_columns, 0)
-    one_copy = copies.start(outs, outr, sibling)
-
-    theirs = pl.ds(pl.multiple_of((1 - c) * HALF, HALF), HALF)
-    mine = pl.ds(pl.multiple_of(c * HALF, HALF), HALF)
-    a_copy = copies.start(apart.at[:, theirs], asib, sibling)
+
     red[72:80, HALF:] = jnp.zeros((8, PIECE - HALF), F32)
     red[0:64, HALF + 128 :] = jnp.zeros((64, 128), F32)
     red[80:128, HALF:] = jnp.zeros((48, PIECE - HALF), F32)
@@ -868,10 +888,12 @@
         t = mid[rows, :] + ht[rows, :].astype(F32)
         for k in range(3):
             t += rbb[k, rows, :].astype(F32)
-        blk_out[rows, :] = t.astype(BF)
-        return carry
-
+        ht[rows, :] = t.astype(BF)
+        return carry
+
+    copies.sent(blk_fly)
     lax.fori_loop(0, ROWS // 16, block_rows, 0)
+    here(ht.at[pl.ds(0, ROWS)], blk_out)
     for copy in fly:
         copy.wait_recv()
     total = rr[0].astype(F32)
@@ -880,6 +902,7 @@
     rz[z] = total
     line = [copies.start(rz.at[z], rz.at[z], device({"z": i})) for i in (1, 2, 3)]
     one_copy.wait_recv()
+    copies.sent([one_copy])
 
     def token_rows(i, carry):
         rows = pl.ds(i * 16, 16)
@@ -888,7 +911,7 @@
         r = r1[c, rows, :1]
         n = t * r
         o = o * gain1[...]
-        gtok_out[rows, :] = (mgrad[rows, :] + r * (o - n * jnp.mean(o * n, -1, keepdims=True))).astype(BF)
+        outs[rows, :] = (mgrad[rows, :] + r * (o - n * jnp.mean(o * n, -1, keepdims=True))).astype(BF)
         return carry
 
     lax.fori_loop(0, ROWS // 32, token_rows, 0)
@@ -901,10 +924,25 @@
         copies.start(piece, piece, device({"x": i, "y": j})) for i in range(4) for j in range(4) if i + j > 0
     ]
     lax.fori_loop(ROWS // 32, ROWS // 16, token_rows, 0)
+    here(outs, gtok_out)
     for copy in fly:
         copy.wait_recv()
     f_copy = copies.start(fin.at[c], fin.at[c], sibling)
     f_copy.wait_recv()
+
+    here(fin, red_out)
+    for copy in local[-3:]:
+        copy.wait()
+    copies.drain()
+
+
+def finish(
+    blk, gtok, fin,
+    blk_out, gtok_out, gain_a_out, qa_out, qb_out, ka_out, kb_out, va_out, vb_out, oa_out, ob_out, fq_out, fk_out,
+    gain_b_out,
+):
+    blk_out[...] = blk[...]
+    gtok_out[...] = gtok[...]
 
     def wide(k, side):
         got = fin[side, k].astype(F32)
@@ -936,10 +974,9 @@
         for k, out in ((0, gain_a_out), (1, gain_b_out)):
             for i in range(8):
                 out[side * 8 + i : side * 8 + i + 1, :] = row[k : k + 1, i * 128 : (i + 1) * 128]
-    copies.drain()
-
-
-N_COPIES = 301
+
+
+N_COPIES = 273
 N_SENDS = 64
 
 
@@ -1013,7 +1050,7 @@
         v((40, HALF), F32),
         pltpu.SemaphoreType.DMA((N_SENDS,)),
         pltpu.SemaphoreType.DMA((N_COPIES,)),
-        pltpu.SemaphoreType.DMA((15,)),
+        pltpu.SemaphoreType.DMA((18,)),
     ]
 
 
@@ -1030,16 +1067,13 @@
     def array(*shape, dtype=F32):
         return jax.ShapeDtypeStruct(shape, dtype)
 
-    out = pl.pallas_call(
+    parts = pl.pallas_call(
         kernel,
         out_shape=(
-            array(ROWS, WIDTH, dtype=BF), array(ROWS, WIDTH, dtype=BF), array(16, 128),
-            array(RANK, WIDTH), array(RANK, WIDTH), array(RANK, WIDTH), array(RANK, 2 * NARROW),
-            array(RANK, WIDTH), array(RANK, 2 * NARROW), array(RANK, WIDTH), array(RANK, WIDTH),
-            array(QUERY_HEADS, HEAD, HEAD), array(KEY_VALUE_HEADS, HEAD, HEAD), array(16, 128),
+            array(ROWS, WIDTH, dtype=BF), array(ROWS, WIDTH, dtype=BF), array(2, 16, 16, PIECE // 2, dtype=BF),
         ),
         in_specs=[anywhere, smem, vmem] + [anywhere] * 4 + [vmem] * 11 + [anywhere] * 4,
-        out_specs=(vmem,) * 14,
+        out_specs=(anywhere,) * 3,
         scratch_shapes=scratch(),
         compiler_params=pltpu.CompilerParams(
             collective_id=0, has_side_effects=True, vmem_limit_bytes=64 * 1024 * 1024
@@ -1051,6 +1085,17 @@
         value_adapter_up, output_adapter_down.T, output_adapter_up, query_feature_map, key_feature_map,
         feedforward_gain.reshape(16, 128), gate_weight, up_weight, down_weight_flipped, output_gradient,
     )
+    out = pl.pallas_call(
+        finish,
+        out_shape=(
+            array(ROWS, WIDTH, dtype=BF), array(ROWS, WIDTH, dtype=BF), array(16, 128),
+            array(RANK, WIDTH), array(RANK, WIDTH), array(RANK, WIDTH), array(RANK, 2 * NARROW),
+            array(RANK, WIDTH), array(RANK, 2 * NARROW), array(RANK, WIDTH), array(RANK, WIDTH),
+            array(QUERY_HEADS, HEAD, HEAD), array(KEY_VALUE_HEADS, HEAD, HEAD), array(16, 128),
+        ),
+        in_specs=[vmem] * 3,
+        out_specs=(vmem,) * 14,
+    )(*parts)
     (
         block_out, grad_tokens, gain_attn, qa, qb, ka, kb, va, vb, oa, ob, feat_q, feat_k, gain_mlp,
     ) = out

time: 201 us -> 182 us (0.905)
  local copies, waits for them, and re-layouts: 11.5 us -> 0 us
  Pallas kernels: 188 us -> 181 us
    unnamed x40 -> x0, local copies, waits for them, and re-layouts: 11.5 us -> none
    pallas_call x1, Pallas kernels: 188 us -> 177 us  [body(): pl.pallas_call(kernel, out_shape=(array(ROWS, WIDTH, dtype=BF), array(ROW...]
    pallas_call x0 -> x1, Pallas kernels: none -> 3.55 us  [body(): pl.pallas_call(finish, out_shape=(array(ROWS, WIDTH, dtype=BF), array(ROW...]
where the time goes in v4:
time: 182 us
  Pallas kernels  181 us (99%)
    pallas_call x1, Pallas kernels, body(): pl.pallas_call(kernel, out_shape=(array(ROWS, WIDTH, dtype=BF), array(ROW...  177 us

profile of v4, /device:TPU:1, one launch (start us, length us, event | category | flops | bytes accessed | tf_op | source)
XLA Modules:
  0.0 181.5 jit_solution(8518635269285433375)
XLA Ops:
  0.7 177.1 %shard_map.317 = (bf16[128,2048]{1,0:T(8,128)(2,1)}, bf16[128,2048]{1,0:T(8,128)(2,1)}, bf16[2,16,16,640]{3,2,1,0:T(8,128)(2,1)}) custom-call(bf16[128,2048]{1,0:T(8,128)(2,1)} %tok.1, s32[8]{0:T(128)} %lens.1, bf16[16,128]{1,0:T(8,128)(2,1)} %bitcast.16, bf16[16,2048]{1,0:T(8,128)(2,1)} %qw.1, bf16[16,256]{1,0:T(8,128)(2,1)} %kw.1, bf16[16,256]{1,0:T(8,128)(2,1)} %vw.1, ...), custom_call_target="tpu_custom_call" | custom-call | tf_op jit(solution)/shard_map/pallas_call | solution.py:1070
  177.8 3.5 %shard_map.318 = (bf16[128,2048]{1,0:T(8,128)(2,1)}, bf16[128,2048]{1,0:T(8,128)(2,1)}, f32[16,128]{1,0:T(8,128)}, f32[8,2048]{1,0:T(8,128)}, f32[8,2048]{1,0:T(...) custom-call(bf16[128,2048]{1,0:T(8,128)(2,1)} %get-tuple-element.31., ...), custom_call_target="tpu_custom_call" | custom-call | tf_op jit(solution)/shard_map/pallas_call | solution.py:1088

commit v5 on v4

--- a/solution.py
+++ b/solution.py
@@ -22,7 +22,7 @@
 SLICE = FF // 4
 AUG = 80
 RANK = 8
-PIECE = 1280
+PIECE = 512
 EPSILON = 1e-05
 MESH = pl.DeviceIdType.MESH
 F32 = jnp.float32
@@ -56,26 +56,50 @@
     return lax.rem(value, 4)
 
 
+class Copy:
+    def __init__(self, copy, index):
+        self.copy, self.index, self.landed = copy, index, False
+        self.wait_send = copy.wait_send
+
+    def wait_recv(self):
+        self.copy.wait_recv()
+        self.landed = True
+
+
 class Copies:
     def __init__(self, send, recv):
         self.send, self.recv, self.count, self.open = send, recv, 0, {}
+        self.all, self.heard, self.free, self.indices = [], [], [], 0
 
     def start(self, src, dst, device):
         slot = self.count % N_SENDS
         if slot in self.open:
             self.open.pop(slot).wait_send()
+        if self.free:
+            index = self.free.pop()
+        else:
+            index = self.indices
+            self.indices += 1
         copy = pltpu.make_async_remote_copy(
             src_ref=src,
             dst_ref=dst,
             send_sem=self.send.at[slot],
-            recv_sem=self.recv.at[self.count],
+            recv_sem=self.recv.at[index],
             device_id=(device,),
             device_id_type=MESH,
         )
         self.count += 1
         copy.start()
+        copy = Copy(copy, index)
         self.open[slot] = copy
+        self.all.append(copy)
         return copy
+
+    def note(self):
+        self.heard = [copy.index for copy in self.all if copy.landed]
+
+    def reuse(self):
+        self.free = self.heard
 
     def sent(self, copies):
         for slot in [k for k, copy in self.open.items() if any(copy is other for other in copies)]:
@@ -87,40 +111,51 @@
 
 
 class Heads:
-    def __init__(self, copies, wa, where, device, parts, straight=False):
+    def __init__(self, copies, wa, where, device, settled, parts):
         self.copies, self.wa, self.where, self.device = copies, wa, where, device
-        self.parts, self.straight = parts, straight
+        self.settled, self.parts = settled, parts
         self.flying = {}
 
-    def block(self, order, phase, at, first, count):
+    def block(self, order, phase, at, cols, core=slice(None)):
         index = []
         for axis in "zxy":
             k = order.index(axis)
             index.append(slice(None) if k < phase else at if k == phase else self.where[axis])
-        return self.wa.at[index[0], index[1], index[2], :, :, pl.ds(first, count)]
+        return self.wa.at[index[0], index[1], index[2], core, :, cols]
 
     def begin(self, phase):
-        for part, (order, first, count) in enumerate(self.parts):
+        c = self.where["c"]
+        for part, (order, src, at, first, count) in enumerate(self.parts):
             axis = order[phase]
-            own = self.block(order, phase, self.where[axis], first, count)
-            steps = (1, 3) if phase > 0 and not self.straight else (1, 3, 2)
-            self.flying[phase, part] = [self.copies.start(own, own, self.device({axis: step})) for step in steps]
+            cols = pl.ds(first, count)
+            fly = []
+            if phase == 0:
+                for step in (1, 3, 2):
+                    for cross in (0, 1):
+                        core = 1 - c if cross else c
+                        piece = src.at[:, pl.ds(pl.multiple_of(core * (src.shape[1] // 2) + at, 128), count)]
+                        dst = self.wa.at[self.where["z"], self.where["x"], self.where["y"], c, :, cols]
+                        fly.append(self.copies.start(piece, dst, self.device({axis: step}, cross)))
+            else:
+                own = self.block(order, phase, self.where[axis], cols)
+                fly = [self.copies.start(own, own, self.device({axis: step})) for step in (1, 3)]
+            self.flying[phase, part] = fly
 
     def middle(self, phase):
-        for part, (order, first, count) in enumerate(self.parts):
+        for part, (order, src, at, first, count) in enumerate(self.parts):
             axis = order[phase]
             for copy in self.flying[phase, part]:
                 copy.wait_recv()
             here = self.where[axis]
-            one = (count // 256) * 128
-            left = self.block(order, phase, wrap(here + 3), first, one)
-            right = self.block(order, phase, wrap(here + 1), first + one, count - one)
+            left = self.block(order, phase, wrap(here + 3), pl.ds(first, count), 0)
+            right = self.block(order, phase, wrap(here + 1), pl.ds(first, count), 1)
             self.flying[phase, part] = [
                 self.copies.start(left, left, self.device({axis: 1})),
                 self.copies.start(right, right, self.device({axis: 3})),
             ]
 
     def end(self, phase):
+        self.settled()
         for part in range(len(self.parts)):
             for copy in self.flying[phase, part]:
                 copy.wait_recv()
@@ -210,13 +245,13 @@
             copy.wait_recv()
 
 
-EARLY = ("kv.b0", "o.b0", "q.b0",)
+EARLY = ("kv.b0", "q.b0", "o.b0", "d.b0", "kv.e0", "u.b0", "g.b0", "kv.b1",)
 PLAN = (
-    "d.b0", "kv.e0", "kv.b1", "g.b0", "u.b0", "q.e0", "low", "o.e0", "d.e0", "d.b1", "q.b1", "o.b1",
-    "q.m1", "d.e1", "u.e0", "d.b2", "kv.e1", "g.e0", "g.b1", "kv.b2", "u.b1", "q.e1", "q.b2", "o.m1",
-    "g.e1", "u.e1", "d.m2", "kv.e2", "g.b2", "kvc", "pls", "o.e1", "o.b2", "lns", "d.e2", "q.m2",
-    "u.b2", "o.m2", "lnw", "q.e2", "ogs", "qc", "g.m2", "att", "o.e2", "ds", "oproj", "mid",
-    "hts", "u.m2", "ogw", "ig", "g.e2", "u.e2", "gs", "us", "htw",
+    "o.e0", "q.e0", "q.b1", "d.e0", "kv.m1", "d.b1", "o.b1", "q.m1", "kv.e1", "g.e0", "u.e0", "kv.b2",
+    "d.e1", "d.b2", "q.e1", "o.m1", "g.b1", "u.b1", "kv.m2", "q.b2", "g.e1", "g.b2", "o.e1", "kv.e2",
+    "low", "d.m2", "u.e1", "kvc", "pls", "o.b2", "lns", "q.m2", "u.b2", "o.m2", "g.m2", "d.e2",
+    "lnw", "q.e2", "qc", "ogs", "att", "o.e2", "oproj", "mid", "u.m2", "hts", "g.e2", "ogw",
+    "ds", "ig", "u.e2", "gs", "us", "htw",
 )
 
 
@@ -226,7 +261,7 @@
     wa, wf, stage, tok2, ogo, gains, r1, aall, ball, oac, ob2, masks, far_masks, bias, hid1, low, qt, kt, vt, knat, vnat,
     kfeat, st, comb, comb_t, wts, qfeat, mixf, damp, den, mixn, lowo, outs, outr, mid, ht, ogx, gg, inner, ug, rbt, rbb,
     mgrad, bg, ngt, dgr, sig, qlg, gt, gnat, lowg, ones, kacc, vacc, fsend, frecv, hsend, hrecv, red, redb, rr, rz, fin,
-    apart, asib, send, recv, loc,
+    apart, asib, gsum, send, recv, loc,
 ):
     me = lax.axis_index("seq")
     c = lax.rem(me, 2)
@@ -234,9 +269,9 @@
     x = lax.rem(me // 8, 4)
     z = me // 32
 
-    def device(steps):
+    def device(steps, cross=0):
         zz, xx, yy = (wrap(v + steps.get(n, 0)) for n, v in (("z", z), ("x", x), ("y", y)))
-        return ((zz * 4 + xx) * 4 + yy) * 2 + c
+        return ((zz * 4 + xx) * 4 + yy) * 2 + (1 - c if cross else c)
 
     sibling = me + 1 - 2 * c
     plane = x * 4 + y
@@ -247,6 +282,7 @@
     peers = [sibling]
     peers += [device({"x": i, "y": j}) for i in range(4) for j in range(4) if i + j > 0]
     peers += [device({"z": i}) for i in (1, 2, 3)]
+    peers += [device({axis: i}, 1) for axis in "xyz" for i in (1, 2, 3)]
     for peer in peers:
         pl.semaphore_signal(barrier, inc=1, device_id=(peer,), device_id_type=MESH)
     copies = Copies(send, recv)
@@ -266,6 +302,44 @@
     here(tok, tok2.at[c])
     here(og, ogx.at[pl.ds(0, ROWS)])
     here(og, ogo)
+
+    pl.semaphore_wait(barrier, len(peers))
+    first = []
+    for src, at, count in pieces:
+        other = src.at[:, pl.ds(pl.multiple_of((1 - c) * count, count), count)]
+        first.append(copies.start(other, own.at[:, pl.ds(at, count)], sibling))
+    tok_copy = copies.start(tok, tok2.at[c], sibling)
+    where = {"z": z, "x": x, "y": y, "c": c}
+    pending = [local[:4] + first]
+
+    def settled():
+        if pending:
+            done = pending.pop()
+            for copy in done[:4]:
+                copy.wait()
+            for copy in done[4:]:
+                copy.wait_recv()
+
+    streams = {
+        "kv": Heads(copies, wa, where, device, settled, (("xzy", kw, 0, HALF, NARROW), ("yzx", vw, 0, HALF + NARROW, NARROW))),
+        "q": Heads(copies, wa, where, device, settled, (("xzy", qw, 0, 0, 512), ("yzx", qw, 512, 0 + 512, 512))),
+        "o": Heads(copies, wa, where, device, settled, (("zxy", ow, 0, QKV, 512), ("zyx", ow, 512, QKV + 512, 512))),
+        "d": Units(
+            copies, here, wf, stage, where, device, sibling,
+            (("xy", dw, 0, 2 * SLICE, 768), ("yx", dw, 768, 2 * SLICE + 768, 640)),
+        ),
+        "g": Units(copies, here, wf, stage, where, device, sibling, (("xy", gw, 0, 0, SLICE),)),
+        "u": Units(copies, here, wf, stage, where, device, sibling, (("yx", uw, 0, SLICE, SLICE),)),
+    }
+    waiting = {}
+
+    def advance(name):
+        stream, step = name.split(".")
+        stream = streams[stream]
+        {"b": stream.begin, "m": stream.middle, "e": stream.end}[step[0]](int(step[1]))
+
+    for name in EARLY:
+        advance(name)
 
     for k, src in enumerate((gain_a, gain_b)):
         g = src[...].astype(F32)
@@ -334,37 +408,6 @@
         seen = (iu <= it) & ((iu < 64) == (it < 64)) & (lax.rem(iu, STRETCH) < room)
         bias[p] = jnp.where(seen, 0.0, -1e30)
 
-    pl.semaphore_wait(barrier, len(peers))
-    first = []
-    for src, at, count in pieces:
-        other = src.at[:, pl.ds(pl.multiple_of((1 - c) * count, count), count)]
-        first.append(copies.start(other, own.at[:, pl.ds(at, count)], sibling))
-    tok_copy = copies.start(tok, tok2.at[c], sibling)
-    where = {"z": z, "x": x, "y": y, "c": c}
-    streams = {
-        "kv": Heads(copies, wa, where, device, (("xzy", 1024, 128), ("yzx", 1152, 128)), straight=True),
-        "q": Heads(copies, wa, where, device, (("xzy", 0, 512), ("yzx", 512, 512))),
-        "o": Heads(copies, wa, where, device, (("zxy", QKV, 512), ("zyx", QKV + 512, 512))),
-        "d": Units(
-            copies, here, wf, stage, where, device, sibling,
-            (("xy", dw, 0, 2 * SLICE, 768), ("yx", dw, 768, 2 * SLICE + 768, 640)),
-        ),
-        "g": Units(copies, here, wf, stage, where, device, sibling, (("xy", gw, 0, 0, SLICE),)),
-        "u": Units(copies, here, wf, stage, where, device, sibling, (("yx", uw, 0, SLICE, SLICE),)),
-    }
-    for k in range(4):
-        local[k].wait()
-        first[k].wait_recv()
-    waiting = {}
-
-    def advance(name):
-        stream, step = name.split(".")
-        stream = streams[stream]
-        {"b": stream.begin, "m": stream.middle, "e": stream.end}[step[0]](int(step[1]))
-
-    for name in EARLY:
-        advance(name)
-
     for copy in local[4:7]:
         copy.wait()
     tok_copy.wait_recv()
@@ -471,6 +514,7 @@
         folded = st[0]
         for s in (1, 2, 3):
             folded = st[s] + gates[s] * folded
+        copies.note()
         waiting["plane"] = gather_plane(0, folded)
 
     def send_line():
@@ -550,11 +594,14 @@
             outs[:, cols] = other.astype(BF)
             return carry
 
-        lax.fori_loop(0, 8, out_columns, 0)
-        waiting["out"] = copies.start(outs, outr, sibling)
+        waiting["out"] = []
+        for at in (0, 4):
+            lax.fori_loop(at, at + 4, out_columns, 0)
+            cols = pl.ds(at * 256, HALF)
+            waiting["out"].append(copies.start(outs.at[:, cols], outr.at[:, cols], sibling))
 
     def middle():
-        waiting["out"].wait_recv()
+        arrived("out")
 
         def middle_rows(i, carry):
             rows = pl.ds(i * 32, 32)
@@ -606,6 +653,7 @@
             advance(name)
         else:
             steps[name]()
+    copies.reuse()
     og_fly, ht_fly, out_copy = waiting["og"], waiting["ht"], waiting["out"]
 
     def activate(gate, up, cols):
@@ -640,7 +688,7 @@
         ]
 
     two_fly = []
-    for at, end in ((0, 1), (1, 3), (3, 5), (5, 8)):
+    for at, end in ((0, 2), (2, 4), (4, 6), (6, 8)):
         lax.fori_loop(at, end, two_columns, 0)
         two_fly += give_back(ogx, rbt, pl.ds(at * 256, (end - at) * 256))
 
@@ -670,9 +718,14 @@
         bg[c, rows, :] = g.astype(BF)
         return acc
 
-    gain_mlp = lax.fori_loop(0, ROWS // 16, middle_back, jnp.zeros((1, WIDTH), F32))
-    bg_copy = copies.start(bg.at[c], bg.at[c], sibling)
-    bg_copy.wait_recv()
+    gain_mlp = jnp.zeros((1, WIDTH), F32)
+    bg_fly = []
+    for at in (0, ROWS // 2):
+        gain_mlp = lax.fori_loop(at // 16, at // 16 + ROWS // 32, middle_back, gain_mlp)
+        part = bg.at[c, pl.ds(at, ROWS // 2)]
+        bg_fly.append(copies.start(part, part, sibling))
+    for copy in bg_fly:
+        copy.wait_recv()
     bgv = bg.at[:, :, :]
     olg = nt(bgv[...].reshape(CHIP, WIDTH), ob2[...])
     olg_low = olg.astype(BF)
@@ -828,7 +881,9 @@
         o = had[pl.ds(pl.multiple_of(lax.rem(n, 4) * 256, 256), 256), :]
         o = o + nt(gnat[:, HALF:], w) + nn(lowg[...], aall[:, cols])
         normed = [tok2[side, :, cols].astype(F32) * r1[side, :, :1] for side in range(2)]
-        apart[32:33, cols] = jnp.sum(o[:ROWS] * normed[0] + o[ROWS:] * normed[1], 0, keepdims=True)
+        gain = jnp.sum(o[:ROWS] * normed[0] + o[ROWS:] * normed[1], 0, keepdims=True)
+        gsum[0, pl.ds(2 * n, 1), :] = gain[:, :128]
+        gsum[0, pl.ds(2 * n + 1, 1), :] = gain[:, 128:]
         ones[:, cols] = jnp.where(c == 0, o[:ROWS], o[ROWS:])
         outs[:, cols] = jnp.where(c == 0, o[ROWS:], o[:ROWS]).astype(BF)
 
@@ -841,15 +896,15 @@
         return carry
 
     apart[0:24] = nn(lowg_t[:32], hid1[...])[:24]
-    apart[32:40] = jnp.where(lax.broadcasted_iota(jnp.int32, (8, 1), 0) == 1, gain_mlp, 0.0)
-    copies.sent([out_copy])
+    for k in range(16):
+        gsum[1, k : k + 1, :] = gain_mlp[:, k * 128 : (k + 1) * 128]
+    theirs = pl.ds(pl.multiple_of((1 - c) * HALF, HALF), HALF)
+    mine = pl.ds(pl.multiple_of(c * HALF, HALF), HALF)
+    a_copy = copies.start(apart.at[:, theirs], asib, sibling)
+    copies.sent(out_copy)
     lax.fori_loop(0, 4, one_first, 0)
     lax.fori_loop(4, 8, one_second, 0)
     one_copy = copies.start(outs, outr, sibling)
-
-    theirs = pl.ds(pl.multiple_of((1 - c) * HALF, HALF), HALF)
-    mine = pl.ds(pl.multiple_of(c * HALF, HALF), HALF)
-    a_copy = copies.start(apart.at[:, theirs], asib, sibling)
 
     r = nt(kt[...].reshape(128, CHIP), qlg[HALF:, :])
     red[0:64, HALF : HALF + 128] = jnp.where(low_lane, r[:HEAD], r[HEAD:])
@@ -860,19 +915,28 @@
     red[64:72, HALF : HALF + NARROW] = up[8:16, HALF : HALF + NARROW]
     red[64:72, HALF + NARROW :] = up[16:24, HALF + NARROW :]
 
-    red[72:80, HALF:] = jnp.zeros((8, PIECE - HALF), F32)
-    red[0:64, HALF + 128 :] = jnp.zeros((64, 128), F32)
-    red[80:128, HALF:] = jnp.zeros((48, PIECE - HALF), F32)
-    red[120:128, :HALF] = jnp.zeros((8, HALF), F32)
+    def block(k, value):
+        redb[k // 4, :, (k % 4) * 128 : (k % 4 + 1) * 128] = value.astype(BF)
+
+    def feat_blocks(k, carry):
+        rows = pl.ds(pl.multiple_of(k * 16, 16), 16)
+        for j in range(8):
+            redb[2 * k + j // 4, :, (j % 4) * 128 : (j % 4 + 1) * 128] = red[rows, j * 128 : (j + 1) * 128].astype(BF)
+        redb[8, :, pl.ds(pl.multiple_of(k * 128, 128), 128)] = red[rows, HALF : HALF + 128].astype(BF)
+        return carry
+
+    lax.fori_loop(0, 4, feat_blocks, 0)
+    for j in range(8):
+        block(36 + j, red[64:80, j * 128 : (j + 1) * 128])
+    block(44, jnp.concatenate([red[64:72, HALF : HALF + NARROW], red[64:72, HALF + NARROW :]], 0))
     a_copy.wait_recv()
-    red[80:120, :HALF] = apart[:, mine] + asib[...]
-
-    def fold_piece(k, carry):
-        rows = pl.ds(pl.multiple_of(k * 8, 8), 8)
-        redb[k] = jnp.concatenate([red[rows, : PIECE // 2], red[rows, PIECE // 2 :]], 0).astype(BF)
-        return carry
-
-    lax.fori_loop(0, 16, fold_piece, 0)
+    summed = apart[:, mine] + asib[...]
+    for j in range(8):
+        block(45 + j, summed[:16, j * 128 : (j + 1) * 128])
+        block(53 + j, summed[16:, j * 128 : (j + 1) * 128])
+    block(61, gsum[0])
+    block(62, gsum[1])
+    block(63, jnp.zeros((16, 128), F32))
     fly = []
     for i in range(4):
         for j in range(4):
@@ -899,7 +963,7 @@
     total = rr[0].astype(F32)
     for k in range(1, 16):
         total += rr[k].astype(F32)
-    rz[z] = total
+    rz[z] = total.astype(BF)
     line = [copies.start(rz.at[z], rz.at[z], device({"z": i})) for i in (1, 2, 3)]
     one_copy.wait_recv()
     copies.sent([one_copy])
@@ -917,7 +981,7 @@
     lax.fori_loop(0, ROWS // 32, token_rows, 0)
     for copy in line:
         copy.wait_recv()
-    total = (rz[0] + rz[1]) + (rz[2] + rz[3])
+    total = sum((rz[k].astype(F32) for k in range(1, 4)), rz[0].astype(F32))
     fin[c, plane] = total.astype(BF)
     piece = fin.at[c, plane]
     fly = [
@@ -928,10 +992,11 @@
     for copy in fly:
         copy.wait_recv()
     f_copy = copies.start(fin.at[c], fin.at[c], sibling)
+    here(fin.at[c], red_out.at[c])
     f_copy.wait_recv()
 
-    here(fin, red_out)
-    for copy in local[-3:]:
+    here(fin.at[1 - c], red_out.at[1 - c])
+    for copy in local[-4:]:
         copy.wait()
     copies.drain()
 
@@ -939,44 +1004,40 @@
 def finish(
     blk, gtok, fin,
     blk_out, gtok_out, gain_a_out, qa_out, qb_out, ka_out, kb_out, va_out, vb_out, oa_out, ob_out, fq_out, fk_out,
-    gain_b_out,
+    gain_b_out, sem,
 ):
-    blk_out[...] = blk[...]
-    gtok_out[...] = gtok[...]
-
-    def wide(k, side):
-        got = fin[side, k].astype(F32)
-        return got[:8], got[8:]
-
-    def feat_out(k, carry):
-        rows = pl.ds(pl.multiple_of(k * 8, 8), 8)
-        for side in range(2):
-            left, right = wide(k, side)
+    copies = [pltpu.make_async_copy(a, b, sem.at[k]) for k, (a, b) in enumerate(((blk, blk_out), (gtok, gtok_out)))]
+    for copy in copies:
+        copy.start()
+
+    def block(side, k):
+        return fin[side, k // 4, :, (k % 4) * 128 : (k % 4 + 1) * 128].astype(F32)
+
+    for side in range(2):
+        at = side * HALF
+        for k in range(4):
+            rows = slice(k * 16, (k + 1) * 16)
             for j in range(9):
-                v = left[:, j * 128 : (j + 1) * 128] if j < 5 else right[:, (j - 5) * 128 : (j - 4) * 128]
+                v = block(side, k * 8 + j if j < 8 else 32 + k)
                 out, head = (fq_out, side * 16 + 2 * j) if j < 8 else (fk_out, side * 2)
                 out[head, rows, :] = v[:, :64]
                 out[head + 1, rows, :] = pltpu.roll(v, 64, 1)[:, :64]
-        return carry
-
-    lax.fori_loop(0, 8, feat_out, 0)
-    rest = HALF - PIECE // 2
-    for side in range(2):
-        for k, out in ((8, qb_out), (9, oa_out), (10, qa_out), (11, ka_out), (12, va_out), (13, ob_out)):
-            left, right = wide(k, side)
-            out[:, side * HALF : side * HALF + PIECE // 2] = left
-            out[:, side * HALF + PIECE // 2 : (side + 1) * HALF] = right[:, :rest]
-            if k == 8:
-                kb_out[:, side * NARROW : (side + 1) * NARROW] = right[:, rest : rest + NARROW]
-                vb_out[:, side * NARROW : (side + 1) * NARROW] = right[:, rest + NARROW :]
-        left, right = wide(14, side)
-        row = jnp.concatenate([left, right[:, :rest]], 1)
-        for k, out in ((0, gain_a_out), (1, gain_b_out)):
-            for i in range(8):
-                out[side * 8 + i : side * 8 + i + 1, :] = row[k : k + 1, i * 128 : (i + 1) * 128]
-
-
-N_COPIES = 273
+        for j in range(8):
+            cols = slice(at + j * 128, at + (j + 1) * 128)
+            for k, over, under in ((36, qb_out, oa_out), (45, qa_out, ka_out), (53, va_out, ob_out)):
+                v = block(side, k + j)
+                over[:, cols] = v[:8]
+                under[:, cols] = v[8:]
+        v = block(side, 44)
+        kb_out[:, side * NARROW : (side + 1) * NARROW] = v[:8]
+        vb_out[:, side * NARROW : (side + 1) * NARROW] = v[8:]
+    gain_a_out[...] = block(0, 61) + block(1, 61)
+    gain_b_out[...] = block(0, 62) + block(1, 62)
+    for copy in copies:
+        copy.wait()
+
+
+N_COPIES = 193
 N_SENDS = 64
 
 
@@ -1041,16 +1102,17 @@
         v((2, 16, AUG, 128), BF),
         v((2, AUG, 128), BF),
         v((2, 3, AUG, 128), BF),
-        v((128, PIECE), F32),
-        v((16, 16, PIECE // 2), BF),
-        v((16, 16, PIECE // 2), BF),
-        v((4, 16, PIECE // 2), F32),
-        v((2, 16, 16, PIECE // 2), BF),
-        v((40, WIDTH), F32),
-        v((40, HALF), F32),
+        v((80, QKV), F32),
+        v((16, 16, PIECE), BF),
+        v((16, 16, PIECE), BF),
+        v((4, 16, PIECE), BF),
+        v((2, 16, 16, PIECE), BF),
+        v((32, WIDTH), F32),
+        v((32, HALF), F32),
+        v((2, 16, 128), F32),
         pltpu.SemaphoreType.DMA((N_SENDS,)),
         pltpu.SemaphoreType.DMA((N_COPIES,)),
-        pltpu.SemaphoreType.DMA((18,)),
+        pltpu.SemaphoreType.DMA((19,)),
     ]
 
 
@@ -1070,7 +1132,7 @@
     parts = pl.pallas_call(
         kernel,
         out_shape=(
-            array(ROWS, WIDTH, dtype=BF), array(ROWS, WIDTH, dtype=BF), array(2, 16, 16, PIECE // 2, dtype=BF),
+            array(ROWS, WIDTH, dtype=BF), array(ROWS, WIDTH, dtype=BF), array(2, 16, 16, PIECE, dtype=BF),
         ),
         in_specs=[anywhere, smem, vmem] + [anywhere] * 4 + [vmem] * 11 + [anywhere] * 4,
         out_specs=(anywhere,) * 3,
@@ -1094,7 +1156,8 @@
             array(QUERY_HEADS, HEAD, HEAD), array(KEY_VALUE_HEADS, HEAD, HEAD), array(16, 128),
         ),
         in_specs=[vmem] * 3,
-        out_specs=(vmem,) * 14,
+        out_specs=(anywhere,) * 2 + (vmem,) * 12,
+        scratch_shapes=[pltpu.SemaphoreType.DMA((2,))],
     )(*parts)
     (
         block_out, grad_tokens, gain_attn, qa, qb, ka, kb, va, vb, oa, ob, feat_q, feat_k, gain_mlp,

time: 182 us -> 173 us (0.951)
  Pallas kernels: 181 us -> 172 us
    pallas_call x1, Pallas kernels: 177 us -> 169 us  [body(): pl.pallas_call(kernel, out_shape=(array(ROWS, WIDTH, dtype=BF), array(ROW...]
where the time goes in v5:
time: 173 us
  Pallas kernels  172 us (99%)
    pallas_call x1, Pallas kernels, body(): pl.pallas_call(kernel, out_shape=(array(ROWS, WIDTH, dtype=BF), array(ROW...  169 us
    pallas_call x1, Pallas kernels, body(): pl.pallas_call(finish, out_shape=(array(ROWS, WIDTH, dtype=BF), array(ROW...  3.49 us

profile of v5, /device:TPU:1, one launch (start us, length us, event | category | flops | bytes accessed | tf_op | source)
XLA Modules:
  0.0 173.2 jit_solution(15659159836675347150)
XLA Ops:
  0.7 168.9 %shard_map.317 = (bf16[128,2048]{1,0:T(8,128)(2,1)}, bf16[128,2048]{1,0:T(8,128)(2,1)}, bf16[2,16,16,512]{3,2,1,0:T(8,128)(2,1)}) custom-call(bf16[128,2048]{1,0:T(8,128)(2,1)} %tok.1, s32[8]{0:T(128)} %lens.1, bf16[16,128]{1,0:T(8,128)(2,1)} %bitcast.16, bf16[16,2048]{1,0:T(8,128)(2,1)} %qw.1, bf16[16,256]{1,0:T(8,128)(2,1)} %kw.1, bf16[16,256]{1,0:T(8,128)(2,1)} %vw.1, ...), custom_call_target="tpu_custom_call" | custom-call | tf_op jit(solution)/shard_map/pallas_call | solution.py:1132
  169.5 3.5 %shard_map.318 = (bf16[128,2048]{1,0:T(8,128)(2,1)}, bf16[128,2048]{1,0:T(8,128)(2,1)}, f32[16,128]{1,0:T(8,128)}, f32[8,2048]{1,0:T(8,128)}, f32[8,2048]{1,0:T(...) custom-call(bf16[128,2048]{1,0:T(8,128)(2,1)} %get-tuple-element.31., ...), custom_call_target="tpu_custom_call" | custom-call | tf_op jit(solution)/shard_map/pallas_call | solution.py:1150

commit v6 on v5

--- a/solution.py
+++ b/solution.py
@@ -22,7 +22,8 @@
 SLICE = FF // 4
 AUG = 80
 RANK = 8
-PIECE = 512
+EARLY_BLOCKS = 4
+LATE_BLOCKS = 2
 EPSILON = 1e-05
 MESH = pl.DeviceIdType.MESH
 F32 = jnp.float32
@@ -96,7 +97,8 @@
         return copy
 
     def note(self):
-        self.heard = [copy.index for copy in self.all if copy.landed]
+        last = {copy.index: copy for copy in self.all}
+        self.heard = [index for index, copy in last.items() if copy.landed]
 
     def reuse(self):
         self.free = self.heard
@@ -245,6 +247,57 @@
             copy.wait_recv()
 
 
+class Sums:
+    def __init__(self, copies, device, at, sibling, buffers, share):
+        self.copies, self.device, self.sibling, self.share = copies, device, sibling, share
+        self.x, self.y, self.z, self.c = at
+        self.plane = self.x * 4 + self.y
+        self.own, self.got, self.line, self.all = buffers
+
+    def put(self, k, value):
+        self.own[k // self.share, :, (k % self.share) * 128 : (k % self.share + 1) * 128] = value.astype(BF)
+
+    def round(self, send):
+        return [send(i, j) for i in range(4) for j in range(4) if i + j > 0]
+
+    def scatter(self):
+        def send(i, j):
+            to = wrap(self.x + i) * 4 + wrap(self.y + j)
+            return self.copies.start(self.own.at[to], self.got.at[self.plane], self.device({"x": i, "y": j}))
+
+        self.fly = self.round(send)
+        self.got[self.plane] = self.own[self.plane]
+
+    def along(self):
+        for copy in self.fly:
+            copy.wait_recv()
+        total = self.got[0].astype(F32)
+        for k in range(1, 16):
+            total += self.got[k].astype(F32)
+        self.line[self.z] = total.astype(BF)
+        mine = self.line.at[self.z]
+        self.fly = [self.copies.start(mine, mine, self.device({"z": i})) for i in (1, 2, 3)]
+
+    def gather(self):
+        for copy in self.fly:
+            copy.wait_recv()
+        total = self.line[0].astype(F32)
+        for k in range(1, 4):
+            total += self.line[k].astype(F32)
+        self.all[self.c, self.plane] = total.astype(BF)
+        piece = self.all.at[self.c, self.plane]
+        self.fly = self.round(lambda i, j: self.copies.start(piece, piece, self.device({"x": i, "y": j})))
+
+    def cross(self):
+        for copy in self.fly:
+            copy.wait_recv()
+        half = self.all.at[self.c]
+        self.fly = [self.copies.start(half, half, self.sibling)]
+
+    def finish(self):
+        self.fly[0].wait_recv()
+
+
 EARLY = ("kv.b0", "q.b0", "o.b0", "d.b0", "kv.e0", "u.b0", "g.b0", "kv.b1",)
 PLAN = (
     "o.e0", "q.e0", "q.b1", "d.e0", "kv.m1", "d.b1", "o.b1", "q.m1", "kv.e1", "g.e0", "u.e0", "kv.b2",
@@ -256,12 +309,12 @@
 
 
 def kernel(
-    tok, lens, gain_a, qw, kw, vw, ow, qa, qb, ka, kb, va, vb, oa, ob, fq, fk, gain_b, gw, uw, dw, og,
-    blk_out, gtok_out, red_out,
-    wa, wf, stage, tok2, ogo, gains, r1, aall, ball, oac, ob2, masks, far_masks, bias, hid1, low, qt, kt, vt, knat, vnat,
+    tok, lens, gain_a, qw, kw, vw, ow, qa, qb, ka, kb, va, vb, oa, ob, maps, fk, gain_b, gw, uw, dw, og,
+    blk_out, gtok_out, early_out, late_out, gain_out,
+    wa, wf, stage, tok2, fq, ogo, gains, r1, aall, ball, oac, ob2, masks, far_masks, bias, hid1, low, qt, kt, vt, knat, vnat,
     kfeat, st, comb, comb_t, wts, qfeat, mixf, damp, den, mixn, lowo, outs, outr, mid, ht, ogx, gg, inner, ug, rbt, rbb,
-    mgrad, bg, ngt, dgr, sig, qlg, gt, gnat, lowg, ones, kacc, vacc, fsend, frecv, hsend, hrecv, red, redb, rr, rz, fin,
-    apart, asib, gsum, send, recv, loc,
+    mgrad, bg, ngt, dgr, sig, qlg, gt, gnat, lowg, ones, kacc, vacc, fsend, frecv, hsend, hrecv,
+    e_own, e_got, e_line, e_all, l_own, l_got, l_line, l_all, gsum, gplane, gline, gain_all, send, recv, loc,
 ):
     me = lax.axis_index("seq")
     c = lax.rem(me, 2)
@@ -300,6 +353,7 @@
         mine = src.at[:, pl.ds(pl.multiple_of(c * count, count), count)]
         here(mine, own.at[:, pl.ds(at, count)])
     here(tok, tok2.at[c])
+    here(maps.at[pl.ds(c * 16, 16)], fq)
     here(og, ogx.at[pl.ds(0, ROWS)])
     here(og, ogo)
 
@@ -408,7 +462,7 @@
         seen = (iu <= it) & ((iu < 64) == (it < 64)) & (lax.rem(iu, STRETCH) < room)
         bias[p] = jnp.where(seen, 0.0, -1e30)
 
-    for copy in local[4:7]:
+    for copy in local[4:8]:
         copy.wait()
     tok_copy.wait_recv()
 
@@ -546,7 +600,7 @@
         g = n // 2
         rows = [pl.ds(pl.multiple_of(n * 256 + k * HEAD, HEAD), HEAD) for k in range(4)]
         for k in range(4):
-            qfeat[rows[k], :] = softmax_rows(tn(fq[c * 16 + n * 4 + k], qt[rows[k], :]))
+            qfeat[rows[k], :] = softmax_rows(tn(fq[n * 4 + k], qt[rows[k], :]))
         for p in range(2):
             cols = slice(p * 128, (p + 1) * 128)
             q = lanes([qt[r, cols] for r in rows])
@@ -664,9 +718,9 @@
         gg[:, cols] = (d * up * s * (1.0 + gate * (1.0 - s))).astype(BF)
         ug[:, cols] = (d * swish).astype(BF)
 
-    for n in range(5):
-        cols = slice(n * 256, (n + 1) * 256)
-        activate(nn(ht[...], ff_cols(n * 256, 256)), nn(ht[...], ff_cols(SLICE + n * 256, 256)), cols)
+    for at, count in ((0, 512), (512, 512), (1024, 256)):
+        cols = slice(at, at + count)
+        activate(nn(ht[...], ff_cols(at, count)), nn(ht[...], ff_cols(SLICE + at, count)), cols)
     both = nn(ht[...], jnp.concatenate([ff_cols(1280, 128), ff_cols(SLICE + 1280, 128)], 1))
     activate(both[:, :128], both[:, 128:], slice(1280, SLICE))
 
@@ -697,9 +751,9 @@
         ht[:, cols] = nt(inner[...], ff_rows(n, 2 * SLICE)).astype(BF)
         return carry
 
-    lax.fori_loop(0, 4, block_columns, 0)
-    blk_fly = give_back(ht, rbb, pl.ds(0, HALF))
-    lax.fori_loop(4, 8, block_columns, 0)
+    lax.fori_loop(0, 6, block_columns, 0)
+    blk_fly = give_back(ht, rbb, pl.ds(0, 1536))
+    lax.fori_loop(6, 8, block_columns, 0)
     for copy in two_fly:
         copy.wait_recv()
 
@@ -774,8 +828,9 @@
     folded = sg_states[3]
     for s in (2, 1, 0):
         folded = sg_states[s] + gates[s + 1] * folded
+    copies.note()
     fly = gather_plane(1, folded)
-    blk_fly += give_back(ht, rbb, pl.ds(HALF, HALF))
+    blk_fly += give_back(ht, rbb, pl.ds(1536, 512))
 
     for k in range(4):
         kacc[k] = jnp.zeros((HEAD, 128), F32)
@@ -800,18 +855,30 @@
                 qlg[rows[k], cols] = (f * (qg - jnp.sum(f * qg, 0, keepdims=True))).astype(BF)
             near = split(nn(kt[g, :, cols], sgr))
             for k in range(4):
-                far = nn(fq[c * 16 + n * 4 + k], qlg[rows[k], cols])
+                far = nn(fq[n * 4 + k], qlg[rows[k], cols])
                 gt[rows[k], cols] = (near[k] * 0.125 + far).astype(BF)
             kacc[g * 2 + p] = kacc[g * 2 + p] + nt(lanes([qt[r, cols] for r in rows]), sgr)
             vacc[g * 2 + p] = vacc[g * 2 + p] + nt(ngs, ws)
         return carry
 
     lax.fori_loop(0, 4, back_four, 0)
+    early = Sums(copies, device, (x, y, z, c), sibling, (e_own, e_got, e_line, e_all), EARLY_BLOCKS)
+    late = Sums(copies, device, (x, y, z, c), sibling, (l_own, l_got, l_line, l_all), LATE_BLOCKS)
     lowo_t = lowo[...].astype(F32).T.astype(BF)
     olg_t = olg.T.astype(BF)
-    apart[24:32] = 2.0 * nn(lowo_t[:16], bg[...].reshape(CHIP, WIDTH))[:8]
-    red[72:80, :HALF] = nn(olg_t[:16], mixn[...])[:8]
-
+    low_t = low[...].astype(F32).T.astype(BF)
+    lowg_q = nn(ball[:16, :HALF], gt[:HALF, :]).astype(BF)
+    grads = jnp.concatenate(
+        [nn(lowg_q, hid1[...])[:8], 2.0 * nn(lowo_t[:16], bg[...].reshape(CHIP, WIDTH))[:8]], 0
+    )
+    for j in range(16):
+        early.put(40 + j, grads[:, j * 128 : (j + 1) * 128])
+    grads = jnp.concatenate([2.0 * nt(low_t[:16], gt[:HALF, :])[:8], nn(olg_t[:16], mixn[...])[:8]], 0)
+    for j in range(8):
+        early.put(32 + j, grads[:, j * 128 : (j + 1) * 128])
+    early.put(56, jnp.concatenate([gain_mlp[:, k * 128 : (k + 1) * 128] for k in range(16)], 0))
+    for k in range(57, 64):
+        early.put(k, jnp.zeros((16, 128), F32))
 
     def grad_rows(n, carry):
         rows = pl.ds(pl.multiple_of(n * 256, 256), 256)
@@ -823,11 +890,14 @@
     def feat_pairs(n, carry):
         rows = pl.ds(pl.multiple_of(n * 128, 128), 128)
         r = nt(qt[rows, :], qlg[rows, :])
-        red[0:64, rows] = jnp.where(low_lane, r[:HEAD], r[HEAD:])
+        r = jnp.where(low_lane, r[:HEAD], r[HEAD:]).astype(BF)
+        for k in range(4):
+            e_own[2 * k + n // 4, :, pl.ds(pl.multiple_of(lax.rem(n, 4) * 128, 128), 128)] = r[k * 16 : (k + 1) * 16]
         return carry
 
     lax.fori_loop(0, 8, feat_pairs, 0)
 
+    early.scatter()
     part, fly = fold_plane(1, fly)
 
     def one_queries(n, carry):
@@ -847,6 +917,9 @@
 
     lax.fori_loop(0, 8, one_queries, 0)
     suffix = fold_line(1, part, fly)
+    used = {copy.index for copy in copies.all if not copy.landed}
+    copies.heard = [index for index in copies.heard if index not in used]
+    copies.reuse()
     states = [None, None, None, suffix]
     for s in (2, 1, 0):
         states[s] = gates[s + 1] * (states[s + 1] + st[s + 1])
@@ -882,8 +955,8 @@
         o = o + nt(gnat[:, HALF:], w) + nn(lowg[...], aall[:, cols])
         normed = [tok2[side, :, cols].astype(F32) * r1[side, :, :1] for side in range(2)]
         gain = jnp.sum(o[:ROWS] * normed[0] + o[ROWS:] * normed[1], 0, keepdims=True)
-        gsum[0, pl.ds(2 * n, 1), :] = gain[:, :128]
-        gsum[0, pl.ds(2 * n + 1, 1), :] = gain[:, 128:]
+        gsum[pl.ds(2 * n, 1), :] = gain[:, :128]
+        gsum[pl.ds(2 * n + 1, 1), :] = gain[:, 128:]
         ones[:, cols] = jnp.where(c == 0, o[:ROWS], o[ROWS:])
         outs[:, cols] = jnp.where(c == 0, o[ROWS:], o[:ROWS]).astype(BF)
 
@@ -895,76 +968,33 @@
         one_columns(n, mixf)
         return carry
 
-    apart[0:24] = nn(lowg_t[:32], hid1[...])[:24]
-    for k in range(16):
-        gsum[1, k : k + 1, :] = gain_mlp[:, k * 128 : (k + 1) * 128]
-    theirs = pl.ds(pl.multiple_of((1 - c) * HALF, HALF), HALF)
-    mine = pl.ds(pl.multiple_of(c * HALF, HALF), HALF)
-    a_copy = copies.start(apart.at[:, theirs], asib, sibling)
+    r = nt(kt[...].reshape(128, CHIP), qlg[HALF:, :])
+    r = jnp.where(low_lane, r[:HEAD], r[HEAD:])
+    for k in range(4):
+        late.put(k, r[k * 16 : (k + 1) * 16])
+    up = 2.0 * nt(low_t[:32], gt[HALF:, :])
+    late.put(4, jnp.concatenate([up[8:16, :NARROW], up[16:24, NARROW:]], 0))
+    down = nn(lowg_t[:32], hid1[...])
+    for j in range(16):
+        late.put(5 + j, down[8:24, j * 128 : (j + 1) * 128])
+    for k in range(21, 32):
+        late.put(k, jnp.zeros((16, 128), F32))
+    late.scatter()
+
     copies.sent(out_copy)
     lax.fori_loop(0, 4, one_first, 0)
     lax.fori_loop(4, 8, one_second, 0)
     one_copy = copies.start(outs, outr, sibling)
 
-    r = nt(kt[...].reshape(128, CHIP), qlg[HALF:, :])
-    red[0:64, HALF : HALF + 128] = jnp.where(low_lane, r[:HEAD], r[HEAD:])
-
-    low_t = low[...].astype(F32).T.astype(BF)
-    up = 2.0 * nt(low_t[:32], gt[...])
-    red[64:72, :HALF] = up[0:8, :HALF]
-    red[64:72, HALF : HALF + NARROW] = up[8:16, HALF : HALF + NARROW]
-    red[64:72, HALF + NARROW :] = up[16:24, HALF + NARROW :]
-
-    def block(k, value):
-        redb[k // 4, :, (k % 4) * 128 : (k % 4 + 1) * 128] = value.astype(BF)
-
-    def feat_blocks(k, carry):
-        rows = pl.ds(pl.multiple_of(k * 16, 16), 16)
-        for j in range(8):
-            redb[2 * k + j // 4, :, (j % 4) * 128 : (j % 4 + 1) * 128] = red[rows, j * 128 : (j + 1) * 128].astype(BF)
-        redb[8, :, pl.ds(pl.multiple_of(k * 128, 128), 128)] = red[rows, HALF : HALF + 128].astype(BF)
-        return carry
-
-    lax.fori_loop(0, 4, feat_blocks, 0)
-    for j in range(8):
-        block(36 + j, red[64:80, j * 128 : (j + 1) * 128])
-    block(44, jnp.concatenate([red[64:72, HALF : HALF + NARROW], red[64:72, HALF + NARROW :]], 0))
-    a_copy.wait_recv()
-    summed = apart[:, mine] + asib[...]
-    for j in range(8):
-        block(45 + j, summed[:16, j * 128 : (j + 1) * 128])
-        block(53 + j, summed[16:, j * 128 : (j + 1) * 128])
-    block(61, gsum[0])
-    block(62, gsum[1])
-    block(63, jnp.zeros((16, 128), F32))
-    fly = []
-    for i in range(4):
-        for j in range(4):
-            if i + j > 0:
-                to = wrap(x + i) * 4 + wrap(y + j)
-                fly.append(copies.start(redb.at[to], rr.at[plane], device({"x": i, "y": j})))
-    rr[plane] = redb[plane]
-    for copy in blk_fly:
-        copy.wait_recv()
-
-    def block_rows(i, carry):
-        rows = pl.ds(i * 16, 16)
-        t = mid[rows, :] + ht[rows, :].astype(F32)
-        for k in range(3):
-            t += rbb[k, rows, :].astype(F32)
-        ht[rows, :] = t.astype(BF)
-        return carry
-
-    copies.sent(blk_fly)
-    lax.fori_loop(0, ROWS // 16, block_rows, 0)
-    here(ht.at[pl.ds(0, ROWS)], blk_out)
-    for copy in fly:
-        copy.wait_recv()
-    total = rr[0].astype(F32)
-    for k in range(1, 16):
-        total += rr[k].astype(F32)
-    rz[z] = total.astype(BF)
-    line = [copies.start(rz.at[z], rz.at[z], device({"z": i})) for i in (1, 2, 3)]
+    gplane[plane] = gsum[...]
+    gain_fly = [
+        copies.start(gsum, gplane.at[plane], device({"x": i, "y": j}))
+        for i in range(4)
+        for j in range(4)
+        if i + j > 0
+    ]
+    early.along()
+    late.along()
     one_copy.wait_recv()
     copies.sent([one_copy])
 
@@ -979,30 +1009,54 @@
         return carry
 
     lax.fori_loop(0, ROWS // 32, token_rows, 0)
-    for copy in line:
+    early.gather()
+    for copy in gain_fly:
         copy.wait_recv()
-    total = sum((rz[k].astype(F32) for k in range(1, 4)), rz[0].astype(F32))
-    fin[c, plane] = total.astype(BF)
-    piece = fin.at[c, plane]
-    fly = [
-        copies.start(piece, piece, device({"x": i, "y": j})) for i in range(4) for j in range(4) if i + j > 0
-    ]
+    total = gplane[0]
+    for k in range(1, 16):
+        total += gplane[k]
+    gline[z, c] = total
+    mine = gline.at[z, c]
+    gain_fly = [copies.start(mine, mine, device({"z": i}, cross)) for cross in (0, 1) for i in range(4) if i + cross > 0]
+    late.gather()
+    for copy in blk_fly:
+        copy.wait_recv()
+
+    def block_rows(i, carry):
+        rows = pl.ds(i * 16, 16)
+        t = mid[rows, :] + ht[rows, :].astype(F32)
+        for k in range(3):
+            t += rbb[k, rows, :].astype(F32)
+        ht[rows, :] = t.astype(BF)
+        return carry
+
+    copies.sent(blk_fly)
+    lax.fori_loop(0, ROWS // 16, block_rows, 0)
+    here(ht.at[pl.ds(0, ROWS)], blk_out)
     lax.fori_loop(ROWS // 32, ROWS // 16, token_rows, 0)
     here(outs, gtok_out)
-    for copy in fly:
+    for copy in gain_fly:
         copy.wait_recv()
-    f_copy = copies.start(fin.at[c], fin.at[c], sibling)
-    here(fin.at[c], red_out.at[c])
-    f_copy.wait_recv()
-
-    here(fin.at[1 - c], red_out.at[1 - c])
-    for copy in local[-4:]:
+    total = gline[0, 0] + gline[0, 1]
+    for k in range(1, 4):
+        total += gline[k, 0] + gline[k, 1]
+    gain_all[...] = total
+    here(gain_all, gain_out)
+    early.cross()
+    here(e_all.at[c], early_out.at[c])
+    late.cross()
+    here(l_all.at[c], late_out.at[c])
+    early.finish()
+    here(e_all.at[1 - c], early_out.at[1 - c])
+    late.finish()
+    here(l_all.at[1 - c], late_out.at[1 - c])
+    for copy in local[-7:]:
         copy.wait()
     copies.drain()
 
 
 def finish(
-    blk, gtok, fin,
+    blk, gtok, early, late, gain,
     blk_out, gtok_out, gain_a_out, qa_out, qb_out, ka_out, kb_out, va_out, vb_out, oa_out, ob_out, fq_out, fk_out,
     gain_b_out, sem,
 ):
@@ -1010,35 +1064,48 @@
     for copy in copies:
         copy.start()
 
-    def block(side, k):
-        return fin[side, k // 4, :, (k % 4) * 128 : (k % 4 + 1) * 128].astype(F32)
+    def block(sums, share, side, k):
+        return sums[side, k // share, :, (k % share) * 128 : (k % share + 1) * 128].astype(F32)
+
+    def first(side, k):
+        return block(early, EARLY_BLOCKS, side, k)
+
+    def second(side, k):
+        return block(late, LATE_BLOCKS, side, k)
 
     for side in range(2):
         at = side * HALF
         for k in range(4):
             rows = slice(k * 16, (k + 1) * 16)
             for j in range(9):
-                v = block(side, k * 8 + j if j < 8 else 32 + k)
+                v = first(side, k * 8 + j) if j < 8 else second(side, k)
                 out, head = (fq_out, side * 16 + 2 * j) if j < 8 else (fk_out, side * 2)
                 out[head, rows, :] = v[:, :64]
                 out[head + 1, rows, :] = pltpu.roll(v, 64, 1)[:, :64]
         for j in range(8):
             cols = slice(at + j * 128, at + (j + 1) * 128)
-            for k, over, under in ((36, qb_out, oa_out), (45, qa_out, ka_out), (53, va_out, ob_out)):
-                v = block(side, k + j)
-                over[:, cols] = v[:8]
-                under[:, cols] = v[8:]
-        v = block(side, 44)
+            v = first(side, 32 + j)
+            qb_out[:, cols] = v[:8]
+            oa_out[:, cols] = v[8:]
+        v = second(side, 4)
         kb_out[:, side * NARROW : (side + 1) * NARROW] = v[:8]
         vb_out[:, side * NARROW : (side + 1) * NARROW] = v[8:]
-    gain_a_out[...] = block(0, 61) + block(1, 61)
-    gain_b_out[...] = block(0, 62) + block(1, 62)
+    for j in range(16):
+        cols = slice(j * 128, (j + 1) * 128)
+        v = first(0, 40 + j) + first(1, 40 + j)
+        qa_out[:, cols] = v[:8]
+        ob_out[:, cols] = v[8:]
+        v = second(0, 5 + j) + second(1, 5 + j)
+        ka_out[:, cols] = v[:8]
+        va_out[:, cols] = v[8:]
+    gain_a_out[...] = gain[...]
+    gain_b_out[...] = first(0, 56) + first(1, 56)
     for copy in copies:
         copy.wait()
 
 
 N_COPIES = 193
-N_SENDS = 64
+N_SENDS = 48
 
 
 def scratch():
@@ -1048,6 +1115,7 @@
         v((4, 2, 2, 2, 2, 2, 16, 3 * SLICE), BF),
         v((2, 2, 16, 3 * SLICE), BF),
         v((2, ROWS, WIDTH), BF),
+        v((QUERY_HEADS // 2, HEAD, HEAD), BF),
         v((ROWS, WIDTH), BF),
         v((8, WIDTH), F32),
         v((2, ROWS, 128), F32),
@@ -1102,17 +1170,21 @@
         v((2, 16, AUG, 128), BF),
         v((2, AUG, 128), BF),
         v((2, 3, AUG, 128), BF),
-        v((80, QKV), F32),
-        v((16, 16, PIECE), BF),
-        v((16, 16, PIECE), BF),
-        v((4, 16, PIECE), BF),
-        v((2, 16, 16, PIECE), BF),
-        v((32, WIDTH), F32),
-        v((32, HALF), F32),
-        v((2, 16, 128), F32),
+        v((16, 16, EARLY_BLOCKS * 128), BF),
+        v((16, 16, EARLY_BLOCKS * 128), BF),
+        v((4, 16, EARLY_BLOCKS * 128), BF),
+        v((2, 16, 16, EARLY_BLOCKS * 128), BF),
+        v((16, 16, LATE_BLOCKS * 128), BF),
+        v((16, 16, LATE_BLOCKS * 128), BF),
+        v((4, 16, LATE_BLOCKS * 128), BF),
+        v((2, 16, 16, LATE_BLOCKS * 128), BF),
+        v((16, 128), F32),
+        v((16, 16, 128), F32),
+        v((4, 2, 16, 128), F32),
+        v((16, 128), F32),
         pltpu.SemaphoreType.DMA((N_SENDS,)),
         pltpu.SemaphoreType.DMA((N_COPIES,)),
-        pltpu.SemaphoreType.DMA((19,)),
+        pltpu.SemaphoreType.DMA((23,)),
     ]
 
 
@@ -1132,10 +1204,12 @@
     parts = pl.pallas_call(
         kernel,
         out_shape=(
-            array(ROWS, WIDTH, dtype=BF), array(ROWS, WIDTH, dtype=BF), array(2, 16, 16, PIECE, dtype=BF),
+            array(ROWS, WIDTH, dtype=BF), array(ROWS, WIDTH, dtype=BF), array(2, 16, 16, EARLY_BLOCKS * 128, dtype=BF),
+            array(2, 16, 16, LATE_BLOCKS * 128, dtype=BF),
+            array(16, 128),
         ),
-        in_specs=[anywhere, smem, vmem] + [anywhere] * 4 + [vmem] * 11 + [anywhere] * 4,
-        out_specs=(anywhere,) * 3,
+        in_specs=[anywhere, smem, vmem] + [anywhere] * 4 + [vmem] * 8 + [anywhere] + [vmem] * 2 + [anywhere] * 4,
+        out_specs=(anywhere,) * 5,
         scratch_shapes=scratch(),
         compiler_params=pltpu.CompilerParams(
             collective_id=0, has_side_effects=True, vmem_limit_bytes=64 * 1024 * 1024
@@ -1155,7 +1229,7 @@
             array(RANK, WIDTH), array(RANK, 2 * NARROW), array(RANK, WIDTH), array(RANK, WIDTH),
             array(QUERY_HEADS, HEAD, HEAD), array(KEY_VALUE_HEADS, HEAD, HEAD), array(16, 128),
         ),
-        in_specs=[vmem] * 3,
+        in_specs=[vmem] * 5,
         out_specs=(anywhere,) * 2 + (vmem,) * 12,
         scratch_shapes=[pltpu.SemaphoreType.DMA((2,))],
     )(*parts)

time: 173 us -> 168 us (0.971)
  Pallas kernels: 172 us -> 167 us
    pallas_call x1, Pallas kernels: 169 us -> 163 us  [body(): pl.pallas_call(kernel, out_shape=(array(ROWS, WIDTH, dtype=BF), array(ROW...]
where the time goes in v6:
time: 168 us
  Pallas kernels  167 us (99%)
    pallas_call x1, Pallas kernels, body(): pl.pallas_call(kernel, out_shape=(array(ROWS, WIDTH, dtype=BF), array(ROW...  163 us
    pallas_call x1, Pallas kernels, body(): pl.pallas_call(finish, out_shape=(array(ROWS, WIDTH, dtype=BF), array(ROW...  3.6 us

profile of v6, /device:TPU:1, one launch (start us, length us, event | category | flops | bytes accessed | tf_op | source)
XLA Modules:
  0.0 167.6 jit_solution(5835845008858490834)
XLA Ops:
  0.7 163.2 %shard_map.317 = (bf16[128,2048]{1,0:T(8,128)(2,1)}, bf16[128,2048]{1,0:T(8,128)(2,1)}, bf16[2,16,16,512]{3,2,1,0:T(8,128)(2,1)}, bf16[2,16,16,256]{3,2,1,0:T(8,128)(2,1)}, f32[16,128]{1,0:T(8,128)}) custom-call(bf16[128,2048]{1,0:T(8,128)(2,1)} %tok.1, s32[8]{0:T(128)} %lens.1, bf16[16,128]{1,0:T(8,128)(2,1)} %bitcast.16, bf16[16,2048]{1,0:T(8,128)(2,1)} %qw.1, ...), custom_call_target="tpu_custom_call" | custom-call | tf_op jit(solution)/shard_map/pallas_call | solution.py:1204
  163.8 3.6 %shard_map.318 = (bf16[128,2048]{1,0:T(8,128)(2,1)}, bf16[128,2048]{1,0:T(8,128)(2,1)}, f32[16,128]{1,0:T(8,128)}, f32[8,2048]{1,0:T(8,128)}, f32[8,2048]{1,0:T(...) custom-call(bf16[128,2048]{1,0:T(8,128)(2,1)} %get-tuple-element.33., ...), custom_call_target="tpu_custom_call" | custom-call | tf_op jit(solution)/shard_map/pallas_call | solution.py:1224

commit v7 on v6

--- a/solution.py
+++ b/solution.py
@@ -57,51 +57,44 @@
     return lax.rem(value, 4)
 
 
-class Copy:
-    def __init__(self, copy, index):
-        self.copy, self.index, self.landed = copy, index, False
-        self.wait_send = copy.wait_send
-
-    def wait_recv(self):
-        self.copy.wait_recv()
-        self.landed = True
+class Group:
+    def __init__(self, copies, index):
+        self.copies, self.index, self.members = copies, index, []
+
+    def start(self, src, dst, device):
+        self.members.append(self.copies.start(src, dst, device, self.index))
+
+    def wait(self, ref):
+        pltpu.make_async_copy(ref, ref, self.copies.recv.at[self.index]).wait()
 
 
 class Copies:
     def __init__(self, send, recv):
-        self.send, self.recv, self.count, self.open = send, recv, 0, {}
-        self.all, self.heard, self.free, self.indices = [], [], [], 0
-
-    def start(self, src, dst, device):
+        self.send, self.recv, self.count, self.open, self.indices = send, recv, 0, {}, 0
+
+    def index(self):
+        self.indices += 1
+        return self.indices - 1
+
+    def group(self):
+        return Group(self, self.index())
+
+    def start(self, src, dst, device, index=None):
         slot = self.count % N_SENDS
         if slot in self.open:
             self.open.pop(slot).wait_send()
-        if self.free:
-            index = self.free.pop()
-        else:
-            index = self.indices
-            self.indices += 1
         copy = pltpu.make_async_remote_copy(
             src_ref=src,
             dst_ref=dst,
             send_sem=self.send.at[slot],
-            recv_sem=self.recv.at[index],
+            recv_sem=self.recv.at[self.index() if index is None else index],
             device_id=(device,),
             device_id_type=MESH,
         )
         self.count += 1
         copy.start()
-        copy = Copy(copy, index)
         self.open[slot] = copy
-        self.all.append(copy)
         return copy
-
-    def note(self):
-        last = {copy.index: copy for copy in self.all}
-        self.heard = [index for index, copy in last.items() if copy.landed]
-
-    def reuse(self):
-        self.free = self.heard
 
     def sent(self, copies):
         for slot in [k for k, copy in self.open.items() if any(copy is other for other in copies)]:
@@ -130,44 +123,44 @@
         for part, (order, src, at, first, count) in enumerate(self.parts):
             axis = order[phase]
             cols = pl.ds(first, count)
-            fly = []
+            group = self.flying[phase, part] = self.copies.group()
             if phase == 0:
                 for step in (1, 3, 2):
                     for cross in (0, 1):
                         core = 1 - c if cross else c
                         piece = src.at[:, pl.ds(pl.multiple_of(core * (src.shape[1] // 2) + at, 128), count)]
                         dst = self.wa.at[self.where["z"], self.where["x"], self.where["y"], c, :, cols]
-                        fly.append(self.copies.start(piece, dst, self.device({axis: step}, cross)))
+                        group.start(piece, dst, self.device({axis: step}, cross))
             else:
                 own = self.block(order, phase, self.where[axis], cols)
-                fly = [self.copies.start(own, own, self.device({axis: step})) for step in (1, 3)]
-            self.flying[phase, part] = fly
+                for step in (1, 3):
+                    group.start(own, own, self.device({axis: step}))
 
     def middle(self, phase):
         for part, (order, src, at, first, count) in enumerate(self.parts):
             axis = order[phase]
-            for copy in self.flying[phase, part]:
-                copy.wait_recv()
+            cols = pl.ds(first, count)
+            self.flying[phase, part].wait(self.block(order, phase, pl.ds(0, 2), cols))
             here = self.where[axis]
-            left = self.block(order, phase, wrap(here + 3), pl.ds(first, count), 0)
-            right = self.block(order, phase, wrap(here + 1), pl.ds(first, count), 1)
-            self.flying[phase, part] = [
-                self.copies.start(left, left, self.device({axis: 1})),
-                self.copies.start(right, right, self.device({axis: 3})),
-            ]
+            left = self.block(order, phase, wrap(here + 3), cols, 0)
+            right = self.block(order, phase, wrap(here + 1), cols, 1)
+            group = self.flying[phase, part] = self.copies.group()
+            group.start(left, left, self.device({axis: 1}))
+            group.start(right, right, self.device({axis: 3}))
 
     def end(self, phase):
         self.settled()
-        for part in range(len(self.parts)):
-            for copy in self.flying[phase, part]:
-                copy.wait_recv()
+        for part, (order, src, at, first, count) in enumerate(self.parts):
+            at = pl.ds(0, 3) if phase == 0 else 0
+            self.flying[phase, part].wait(self.block(order, phase, at, pl.ds(first, count)))
 
 
 class Units:
     def __init__(self, copies, here, wf, stage, where, device, sibling, parts):
         self.copies, self.here, self.wf, self.stage = copies, here, wf, stage
         self.where, self.device, self.sibling, self.parts = where, device, sibling, parts
-        self.flying, self.handed, self.own = {}, [], []
+        self.flying, self.own = {}, []
+        self.handed = [copies.group() for _ in parts]
 
     def rows(self, order, along, across, cols):
         w = self.where
@@ -179,15 +172,15 @@
     def line(self, z, cols):
         return self.wf.at[z, :, :, :, :, self.where["c"], :, cols]
 
-    def hand_on(self, block):
-        self.handed.append(self.copies.start(block, block, self.sibling))
+    def hand_on(self, part, block):
+        self.handed[part].start(block, block, self.sibling)
 
     def begin(self, phase):
         w = self.where
         for part, (order, src, at, first, count) in enumerate(self.parts):
             cols = pl.ds(first, count)
             a, b = order
-            fly = []
+            group = self.flying[phase, part] = self.copies.group()
             if phase == 0:
                 for d in (1, 3, 2, 0):
                     for e in (0, 1):
@@ -201,50 +194,54 @@
                         if d == 0:
                             self.own.append(self.here(piece, dst))
                         else:
-                            fly.append(self.copies.start(piece, dst, self.device({a: d})))
+                            group.start(piece, dst, self.device({a: d}))
             elif phase == 1:
                 mine = self.rows(order, None, w[b], cols)
                 other = self.stage.at[:, :, :, cols]
-                fly = [
-                    self.copies.start(other, mine, self.device({b: 1})),
-                    self.copies.start(other, mine, self.device({b: 3})),
-                    self.copies.start(mine, mine, self.device({b: 2})),
-                ]
+                group.start(other, mine, self.device({b: 1}))
+                group.start(other, mine, self.device({b: 3}))
+                group.start(mine, mine, self.device({b: 2}))
             else:
                 block = self.line(w["z"], cols)
-                self.hand_on(block)
-                fly = [self.copies.start(block, block, self.device({"z": step})) for step in (1, 3)]
-            self.flying[phase, part] = fly
+                self.hand_on(part, block)
+                for step in (1, 3):
+                    group.start(block, block, self.device({"z": step}))
+
+    def some(self, phase, cols):
+        if phase == 0:
+            return self.wf.at[pl.ds(0, 3), 0, 0, 0, 0, :, :, cols]
+        if phase == 1:
+            return self.wf.at[pl.ds(0, 3), :, :, 0, 0, 0, :, cols]
+        return self.wf.at[pl.ds(0, 2), :, :, :, :, 0, :, cols]
 
     def middle(self, phase):
         z = self.where["z"]
         for part, (order, src, at, first, count) in enumerate(self.parts):
-            for copy in self.flying[phase, part]:
-                copy.wait_recv()
+            cols = pl.ds(first, count)
+            self.flying[phase, part].wait(self.some(2, cols))
             one = (count // 256) * 128
             before, after = wrap(z + 3), wrap(z + 1)
             left = self.line(before, pl.ds(first, one))
             right = self.line(after, pl.ds(first + one, count - one))
-            self.flying[phase, part] = [
-                self.copies.start(left, left, self.device({"z": 1})),
-                self.copies.start(right, right, self.device({"z": 3})),
-            ]
-            self.hand_on(self.line(before, pl.ds(first, count)))
-            self.hand_on(self.line(after, pl.ds(first, count)))
+            group = self.flying[phase, part] = self.copies.group()
+            group.start(left, left, self.device({"z": 1}))
+            group.start(right, right, self.device({"z": 3}))
+            self.hand_on(part, self.line(before, cols))
+            self.hand_on(part, self.line(after, cols))
 
     def end(self, phase):
         if phase == 0:
             for copy in self.own:
                 copy.wait()
         for part, (order, src, at, first, count) in enumerate(self.parts):
-            for copy in self.flying[phase, part]:
-                copy.wait_recv()
+            cols = pl.ds(first, count)
+            self.flying[phase, part].wait(self.line(0, cols) if phase == 2 else self.some(phase, cols))
             if phase == 2:
-                self.hand_on(self.line(wrap(self.where["z"] + 2), pl.ds(first, count)))
+                self.hand_on(part, self.line(wrap(self.where["z"] + 2), cols))
 
     def settle(self):
-        for copy in self.handed:
-            copy.wait_recv()
+        for part, (order, src, at, first, count) in enumerate(self.parts):
+            self.handed[part].wait(self.wf.at[:, :, :, :, :, 0, :, pl.ds(first, count)])
 
 
 class Sums:
@@ -257,45 +254,45 @@
     def put(self, k, value):
         self.own[k // self.share, :, (k % self.share) * 128 : (k % self.share + 1) * 128] = value.astype(BF)
 
-    def round(self, send):
-        return [send(i, j) for i in range(4) for j in range(4) if i + j > 0]
+    def others(self):
+        return [(i, j) for i in range(4) for j in range(4) if i + j > 0]
 
     def scatter(self):
-        def send(i, j):
+        self.fly = self.copies.group()
+        for i, j in self.others():
             to = wrap(self.x + i) * 4 + wrap(self.y + j)
-            return self.copies.start(self.own.at[to], self.got.at[self.plane], self.device({"x": i, "y": j}))
-
-        self.fly = self.round(send)
+            self.fly.start(self.own.at[to], self.got.at[self.plane], self.device({"x": i, "y": j}))
         self.got[self.plane] = self.own[self.plane]
 
     def along(self):
-        for copy in self.fly:
-            copy.wait_recv()
+        self.fly.wait(self.got.at[pl.ds(0, 15)])
         total = self.got[0].astype(F32)
         for k in range(1, 16):
             total += self.got[k].astype(F32)
         self.line[self.z] = total.astype(BF)
         mine = self.line.at[self.z]
-        self.fly = [self.copies.start(mine, mine, self.device({"z": i})) for i in (1, 2, 3)]
+        self.fly = self.copies.group()
+        for i in (1, 2, 3):
+            self.fly.start(mine, mine, self.device({"z": i}))
 
     def gather(self):
-        for copy in self.fly:
-            copy.wait_recv()
+        self.fly.wait(self.line.at[pl.ds(0, 3)])
         total = self.line[0].astype(F32)
         for k in range(1, 4):
             total += self.line[k].astype(F32)
         self.all[self.c, self.plane] = total.astype(BF)
         piece = self.all.at[self.c, self.plane]
-        self.fly = self.round(lambda i, j: self.copies.start(piece, piece, self.device({"x": i, "y": j})))
+        self.fly = self.copies.group()
+        for i, j in self.others():
+            self.fly.start(piece, piece, self.device({"x": i, "y": j}))
 
     def cross(self):
-        for copy in self.fly:
-            copy.wait_recv()
+        self.fly.wait(self.all.at[0, pl.ds(0, 15)])
         half = self.all.at[self.c]
-        self.fly = [self.copies.start(half, half, self.sibling)]
+        self.fly = self.copies.start(half, half, self.sibling)
 
     def finish(self):
-        self.fly[0].wait_recv()
+        self.fly.wait_recv()
 
 
 EARLY = ("kv.b0", "q.b0", "o.b0", "d.b0", "kv.e0", "u.b0", "g.b0", "kv.b1",)
@@ -314,7 +311,7 @@
     wa, wf, stage, tok2, fq, ogo, gains, r1, aall, ball, oac, ob2, masks, far_masks, bias, hid1, low, qt, kt, vt, knat, vnat,
     kfeat, st, comb, comb_t, wts, qfeat, mixf, damp, den, mixn, lowo, outs, outr, mid, ht, ogx, gg, inner, ug, rbt, rbb,
     mgrad, bg, ngt, dgr, sig, qlg, gt, gnat, lowg, ones, kacc, vacc, fsend, frecv, hsend, hrecv,
-    e_own, e_got, e_line, e_all, l_own, l_got, l_line, l_all, gsum, gplane, gline, gain_all, send, recv, loc,
+    e_own, e_got, e_line, e_all, l_own, l_got, l_line, l_all, gsum, gplane, gline, gain_all, send, recv, loc, two_send, two_recv,
 ):
     me = lax.axis_index("seq")
     c = lax.rem(me, 2)
@@ -485,30 +482,31 @@
 
     def gather_plane(base, folded):
         fsend[base] = folded.astype(BF)
-        fly = []
+        frecv[base, plane] = folded.astype(BF)
+        fly = copies.group()
         for i in range(4):
             for j in range(4):
                 if i + j > 0:
-                    fly.append(copies.start(fsend.at[base], frecv.at[base, plane], device({"x": i, "y": j})))
-        frecv[base, plane] = folded.astype(BF)
+                    fly.start(fsend.at[base], frecv.at[base, plane], device({"x": i, "y": j}))
         return fly
 
     def fold_plane(base, fly):
-        for copy in fly:
-            copy.wait_recv()
-        part = jnp.zeros((AUG, 128), F32)
+        fly.wait(frecv.at[base, pl.ds(0, 15)])
         whole = jnp.zeros((AUG, 128), F32)
         for k in range(16):
-            f = frecv[base, k].astype(F32)
-            part += masks[2 * base, k : k + 1, :] * f
-            whole += masks[2 * base + 1, k : k + 1, :] * f
+            whole += masks[2 * base + 1, k : k + 1, :] * frecv[base, k].astype(F32)
         hsend[base] = whole.astype(BF)
-        fly = [copies.start(hsend.at[base], hrecv.at[base, i - 1], device({"z": i})) for i in (1, 2, 3)]
+        fly = copies.group()
+        for i in (1, 2, 3):
+            fly.start(hsend.at[base], hrecv.at[base, i - 1], device({"z": i}))
+        part = jnp.zeros((AUG, 128), F32)
+        for k in range(16):
+            part += masks[2 * base, k : k + 1, :] * frecv[base, k].astype(F32)
         return part, fly
 
     def fold_line(base, part, fly):
-        for i, copy in zip((1, 2, 3), fly):
-            copy.wait_recv()
+        fly.wait(hrecv.at[base])
+        for i in (1, 2, 3):
             part += far_masks[base, pl.ds(wrap(z + 4 - i), 1), :] * hrecv[base, i - 1].astype(F32)
         return part
 
@@ -529,10 +527,10 @@
             comb_t[base + k] = tall.T.astype(BF)
 
     def share(src, dst):
-        return [
-            copies.start(src.at[pl.ds(r, n)], dst.at[pl.ds(at, n)], device({"x": i, "y": j}))
-            for i, j, r, n, at in SHARES
-        ]
+        fly = copies.group()
+        for i, j, r, n, at in SHARES:
+            fly.start(src.at[pl.ds(r, n)], dst.at[pl.ds(at, n)], device({"x": i, "y": j}))
+        return fly
 
     def lower():
         low[...] = nt(hid1[...], aall[...]).astype(BF)
@@ -568,7 +566,6 @@
         folded = st[0]
         for s in (1, 2, 3):
             folded = st[s] + gates[s] * folded
-        copies.note()
         waiting["plane"] = gather_plane(0, folded)
 
     def send_line():
@@ -655,7 +652,8 @@
             waiting["out"].append(copies.start(outs.at[:, cols], outr.at[:, cols], sibling))
 
     def middle():
-        arrived("out")
+        for copy in waiting["out"]:
+            copy.wait_recv()
 
         def middle_rows(i, carry):
             rows = pl.ds(i * 32, 32)
@@ -674,8 +672,7 @@
         waiting["og"] = share(ogo, ogx)
 
     def arrived(name):
-        for copy in waiting[name]:
-            copy.wait_recv()
+        waiting[name].wait(ogx.at[pl.ds(ROWS, 384)])
 
     def ff_cols(first, count):
         return wf[:, :, :, :, :, :, :, pl.ds(first, count)].reshape(WIDTH, count)
@@ -707,7 +704,6 @@
             advance(name)
         else:
             steps[name]()
-    copies.reuse()
     og_fly, ht_fly, out_copy = waiting["og"], waiting["ht"], waiting["out"]
 
     def activate(gate, up, cols):
@@ -727,8 +723,8 @@
     def ff_rows(n, at):
         return wf[n // 2, lax.rem(n, 2), :, :, :, :, :, pl.ds(at, SLICE)].reshape(256, SLICE)
 
-    copies.sent(ht_fly)
-    copies.sent(og_fly)
+    copies.sent(ht_fly.members)
+    copies.sent(og_fly.members)
 
     def two_columns(n, carry):
         cols = pl.ds(pl.multiple_of(n * 256, 256), 256)
@@ -736,15 +732,35 @@
         return carry
 
     def give_back(src, dst, cols):
-        return [
-            copies.start(src.at[pl.ds(at, n), cols], dst.at[k // 2 - (k > 5), pl.ds(r, n), cols], device({"x": (4 - i) % 4, "y": (4 - j) % 4}))
-            for k, (i, j, r, n, at) in enumerate(SHARES)
-        ]
-
-    two_fly = []
-    for at, end in ((0, 2), (2, 4), (4, 6), (6, 8)):
-        lax.fori_loop(at, end, two_columns, 0)
-        two_fly += give_back(ogx, rbt, pl.ds(at * 256, (end - at) * 256))
+        fly = copies.group()
+        for k, (i, j, r, n, at) in enumerate(SHARES):
+            there = dst.at[k // 2 - (k > 5), pl.ds(r, n), cols]
+            fly.start(src.at[pl.ds(at, n), cols], there, device({"x": (4 - i) % 4, "y": (4 - j) % 4}))
+        return [(fly, dst.at[:, :, cols])]
+
+    def two_step(n, carry):
+        two_columns(n, carry)
+        cols = pl.ds(pl.multiple_of(n * 256, 256), 256)
+        for k, (i, j, r, count, at) in enumerate(SHARES):
+            pltpu.make_async_remote_copy(
+                src_ref=ogx.at[pl.ds(at, count), cols],
+                dst_ref=rbt.at[k // 2 - (k > 5), pl.ds(r, count), cols],
+                send_sem=two_send.at[n],
+                recv_sem=two_recv.at[n],
+                device_id=(device({"x": (4 - i) % 4, "y": (4 - j) % 4}),),
+                device_id_type=MESH,
+            ).start()
+        return carry
+
+    lax.fori_loop(0, 8, two_step, 0)
+
+    def two_wait(n, carry):
+        cols = pl.ds(pl.multiple_of(n * 256, 256), 256)
+        here_to = ogx.at[pl.ds(ROWS, 384), cols]
+        pltpu.make_async_copy(here_to, here_to, two_send.at[n]).wait()
+        come = rbt.at[:, :, cols]
+        pltpu.make_async_copy(come, come, two_recv.at[n]).wait()
+        return carry
 
     def block_columns(n, carry):
         cols = pl.ds(pl.multiple_of(n * 256, 256), 256)
@@ -754,8 +770,7 @@
     lax.fori_loop(0, 6, block_columns, 0)
     blk_fly = give_back(ht, rbb, pl.ds(0, 1536))
     lax.fori_loop(6, 8, block_columns, 0)
-    for copy in two_fly:
-        copy.wait_recv()
+    lax.fori_loop(0, 8, two_wait, 0)
 
     def middle_back(i, acc):
         rows = pl.ds(i * 16, 16)
@@ -828,7 +843,6 @@
     folded = sg_states[3]
     for s in (2, 1, 0):
         folded = sg_states[s] + gates[s + 1] * folded
-    copies.note()
     fly = gather_plane(1, folded)
     blk_fly += give_back(ht, rbb, pl.ds(1536, 512))
 
@@ -917,9 +931,6 @@
 
     lax.fori_loop(0, 8, one_queries, 0)
     suffix = fold_line(1, part, fly)
-    used = {copy.index for copy in copies.all if not copy.landed}
-    copies.heard = [index for index in copies.heard if index not in used]
-    copies.reuse()
     states = [None, None, None, suffix]
     for s in (2, 1, 0):
         states[s] = gates[s + 1] * (states[s + 1] + st[s + 1])
@@ -987,12 +998,9 @@
     one_copy = copies.start(outs, outr, sibling)
 
     gplane[plane] = gsum[...]
-    gain_fly = [
-        copies.start(gsum, gplane.at[plane], device({"x": i, "y": j}))
-        for i in range(4)
-        for j in range(4)
-        if i + j > 0
-    ]
+    gain_fly = copies.group()
+    for i, j in early.others():
+        gain_fly.start(gsum, gplane.at[plane], device({"x": i, "y": j}))
     early.along()
     late.along()
     one_copy.wait_recv()
@@ -1010,17 +1018,20 @@
 
     lax.fori_loop(0, ROWS // 32, token_rows, 0)
     early.gather()
-    for copy in gain_fly:
-        copy.wait_recv()
+    gain_fly.wait(gplane.at[pl.ds(0, 15)])
     total = gplane[0]
     for k in range(1, 16):
         total += gplane[k]
     gline[z, c] = total
     mine = gline.at[z, c]
-    gain_fly = [copies.start(mine, mine, device({"z": i}, cross)) for cross in (0, 1) for i in range(4) if i + cross > 0]
+    same, cross = copies.group(), copies.group()
+    for i in (1, 2, 3):
+        same.start(mine, mine, device({"z": i}))
+    for i in range(4):
+        cross.start(mine, mine, device({"z": i}, 1))
     late.gather()
-    for copy in blk_fly:
-        copy.wait_recv()
+    for fly, ref in blk_fly:
+        fly.wait(ref)
 
     def block_rows(i, carry):
         rows = pl.ds(i * 16, 16)
@@ -1030,13 +1041,13 @@
         ht[rows, :] = t.astype(BF)
         return carry
 
-    copies.sent(blk_fly)
+    copies.sent([copy for fly, ref in blk_fly for copy in fly.members])
     lax.fori_loop(0, ROWS // 16, block_rows, 0)
     here(ht.at[pl.ds(0, ROWS)], blk_out)
     lax.fori_loop(ROWS // 32, ROWS // 16, token_rows, 0)
     here(outs, gtok_out)
-    for copy in gain_fly:
-        copy.wait_recv()
+    same.wait(gline.at[pl.ds(0, 3), 0])
+    cross.wait(gline.at[:, 0])
     total = gline[0, 0] + gline[0, 1]
     for k in range(1, 4):
         total += gline[k, 0] + gline[k, 1]
@@ -1104,7 +1115,7 @@
         copy.wait()
 
 
-N_COPIES = 193
+N_COPIES = 79
 N_SENDS = 48
 
 
@@ -1185,6 +1196,8 @@
         pltpu.SemaphoreType.DMA((N_SENDS,)),
         pltpu.SemaphoreType.DMA((N_COPIES,)),
         pltpu.SemaphoreType.DMA((23,)),
+        pltpu.SemaphoreType.DMA((8,)),
+        pltpu.SemaphoreType.DMA((8,)),
     ]
 
 

time: 168 us -> 166 us (0.988)
  Pallas kernels: 167 us -> 165 us
    pallas_call x1, Pallas kernels: 163 us -> 161 us  [body(): pl.pallas_call(kernel, out_shape=(array(ROWS, WIDTH, dtype=BF), array(ROW...]
where the time goes in v7:
time: 166 us; the launch traced here: 165 us
  Pallas kernels  165 us (99%)
    pallas_call x1, Pallas kernels, body(): pl.pallas_call(kernel, out_shape=(array(ROWS, WIDTH, dtype=BF), array(ROW...  161 us
    pallas_call x1, Pallas kernels, body(): pl.pallas_call(finish, out_shape=(array(ROWS, WIDTH, dtype=BF), array(ROW...  3.6 us

profile of v7, /device:TPU:1, one launch (start us, length us, event | category | flops | bytes accessed | tf_op | source)
XLA Modules:
  0.0 165.4 jit_solution(2993445918069550652)
XLA Ops:
  0.7 161.0 %shard_map.317 = (bf16[128,2048]{1,0:T(8,128)(2,1)}, bf16[128,2048]{1,0:T(8,128)(2,1)}, bf16[2,16,16,512]{3,2,1,0:T(8,128)(2,1)}, bf16[2,16,16,256]{3,2,1,0:T(8,128)(2,1)}, f32[16,128]{1,0:T(8,128)}) custom-call(bf16[128,2048]{1,0:T(8,128)(2,1)} %tok.1, s32[8]{0:T(128)} %lens.1, bf16[16,128]{1,0:T(8,128)(2,1)} %bitcast.16, bf16[16,2048]{1,0:T(8,128)(2,1)} %qw.1, ...), custom_call_target="tpu_custom_call" | custom-call | tf_op jit(solution)/shard_map/pallas_call | solution.py:1217
  161.7 3.6 %shard_map.318 = (bf16[128,2048]{1,0:T(8,128)(2,1)}, bf16[128,2048]{1,0:T(8,128)(2,1)}, f32[16,128]{1,0:T(8,128)}, f32[8,2048]{1,0:T(8,128)}, f32[8,2048]{1,0:T(...) custom-call(bf16[128,2048]{1,0:T(8,128)(2,1)} %get-tuple-element.33., ...), custom_call_target="tpu_custom_call" | custom-call | tf_op jit(solution)/shard_map/pallas_call | solution.py:1237

commit v8 on v7

--- a/solution.py
+++ b/solution.py
@@ -301,7 +301,7 @@
     "d.e1", "d.b2", "q.e1", "o.m1", "g.b1", "u.b1", "kv.m2", "q.b2", "g.e1", "g.b2", "o.e1", "kv.e2",
     "low", "d.m2", "u.e1", "kvc", "pls", "o.b2", "lns", "q.m2", "u.b2", "o.m2", "g.m2", "d.e2",
     "lnw", "q.e2", "qc", "ogs", "att", "o.e2", "oproj", "mid", "u.m2", "hts", "g.e2", "ogw",
-    "ds", "ig", "u.e2", "gs", "us", "htw",
+    "ds", "ig", "gs", "go", "u.e2", "us", "uo", "htw",
 )
 
 
@@ -311,7 +311,7 @@
     wa, wf, stage, tok2, fq, ogo, gains, r1, aall, ball, oac, ob2, masks, far_masks, bias, hid1, low, qt, kt, vt, knat, vnat,
     kfeat, st, comb, comb_t, wts, qfeat, mixf, damp, den, mixn, lowo, outs, outr, mid, ht, ogx, gg, inner, ug, rbt, rbb,
     mgrad, bg, ngt, dgr, sig, qlg, gt, gnat, lowg, ones, kacc, vacc, fsend, frecv, hsend, hrecv,
-    e_own, e_got, e_line, e_all, l_own, l_got, l_line, l_all, gsum, gplane, gline, gain_all, send, recv, loc, two_send, two_recv,
+    gown, e_own, e_got, e_line, e_all, l_own, l_got, l_line, l_all, gsum, gplane, gline, gain_all, send, recv, loc, two_send, two_recv,
 ):
     me = lax.axis_index("seq")
     c = lax.rem(me, 2)
@@ -680,6 +680,25 @@
     def inner_gradient():
         gg[...] = nn(ogx[...], ff_cols(2 * SLICE, SLICE)).astype(BF)
 
+    def activate(gate, up, rows, cols):
+        s = 0.5 * jnp.tanh(0.5 * gate) + 0.5
+        swish = gate * s
+        inner[rows, cols] = (swish * up).astype(BF)
+        d = gg[rows, cols].astype(F32)
+        gg[rows, cols] = (d * up * s * (1.0 + gate * (1.0 - s))).astype(BF)
+        ug[rows, cols] = (d * swish).astype(BF)
+
+    owned, own_chunks = slice(0, ROWS), ((0, 512), (512, 512), (1024, 384))
+
+    def own_gate():
+        for at, count in own_chunks:
+            gown[:, at : at + count] = nn(ht[owned, :], ff_cols(at, count))
+
+    def own_up():
+        for at, count in own_chunks:
+            cols = slice(at, at + count)
+            activate(gown[:, cols], nn(ht[owned, :], ff_cols(SLICE + at, count)), owned, cols)
+
     steps = {
         "low": lower,
         "kvc": keys,
@@ -698,6 +717,8 @@
         "gs": streams["g"].settle,
         "us": streams["u"].settle,
         "ig": inner_gradient,
+        "go": own_gate,
+        "uo": own_up,
     }
     for name in PLAN:
         if "." in name:
@@ -706,19 +727,13 @@
             steps[name]()
     og_fly, ht_fly, out_copy = waiting["og"], waiting["ht"], waiting["out"]
 
-    def activate(gate, up, cols):
-        s = 0.5 * jnp.tanh(0.5 * gate) + 0.5
-        swish = gate * s
-        inner[:, cols] = (swish * up).astype(BF)
-        d = gg[:, cols].astype(F32)
-        gg[:, cols] = (d * up * s * (1.0 + gate * (1.0 - s))).astype(BF)
-        ug[:, cols] = (d * swish).astype(BF)
-
+    others = slice(ROWS, 512)
     for at, count in ((0, 512), (512, 512), (1024, 256)):
         cols = slice(at, at + count)
-        activate(nn(ht[...], ff_cols(at, count)), nn(ht[...], ff_cols(SLICE + at, count)), cols)
-    both = nn(ht[...], jnp.concatenate([ff_cols(1280, 128), ff_cols(SLICE + 1280, 128)], 1))
-    activate(both[:, :128], both[:, 128:], slice(1280, SLICE))
+        gate, up = nn(ht[others, :], ff_cols(at, count)), nn(ht[others, :], ff_cols(SLICE + at, count))
+        activate(gate, up, others, cols)
+    both = nn(ht[others, :], jnp.concatenate([ff_cols(1280, 128), ff_cols(SLICE + 1280, 128)], 1))
+    activate(both[:, :128], both[:, 128:], others, slice(1280, SLICE))
 
     def ff_rows(n, at):
         return wf[n // 2, lax.rem(n, 2), :, :, :, :, :, pl.ds(at, SLICE)].reshape(256, SLICE)
@@ -1181,6 +1196,7 @@
         v((2, 16, AUG, 128), BF),
         v((2, AUG, 128), BF),
         v((2, 3, AUG, 128), BF),
+        v((ROWS, SLICE), F32),
         v((16, 16, EARLY_BLOCKS * 128), BF),
         v((16, 16, EARLY_BLOCKS * 128), BF),
         v((4, 16, EARLY_BLOCKS * 128), BF),

time: 166 us -> 165 us (level)
  no operation moved by 1% of the time
where the time goes in v8:
time: 165 us
  Pallas kernels  164 us (99%)
    pallas_call x1, Pallas kernels, body(): pl.pallas_call(kernel, out_shape=(array(ROWS, WIDTH, dtype=BF), array(ROW...  161 us
    pallas_call x1, Pallas kernels, body(): pl.pallas_call(finish, out_shape=(array(ROWS, WIDTH, dtype=BF), array(ROW...  3.6 us

profile of v8, /device:TPU:1, one launch (start us, length us, event | category | flops | bytes accessed | tf_op | source)
XLA Modules:
  0.0 165.0 jit_solution(5151568078667009382)
XLA Ops:
  0.7 160.5 %shard_map.317 = (bf16[128,2048]{1,0:T(8,128)(2,1)}, bf16[128,2048]{1,0:T(8,128)(2,1)}, bf16[2,16,16,512]{3,2,1,0:T(8,128)(2,1)}, bf16[2,16,16,256]{3,2,1,0:T(8,128)(2,1)}, f32[16,128]{1,0:T(8,128)}) custom-call(bf16[128,2048]{1,0:T(8,128)(2,1)} %tok.1, s32[8]{0:T(128)} %lens.1, bf16[16,128]{1,0:T(8,128)(2,1)} %bitcast.16, bf16[16,2048]{1,0:T(8,128)(2,1)} %qw.1, ...), custom_call_target="tpu_custom_call" | custom-call | tf_op jit(solution)/shard_map/pallas_call | solution.py:1233
  161.2 3.6 %shard_map.318 = (bf16[128,2048]{1,0:T(8,128)(2,1)}, bf16[128,2048]{1,0:T(8,128)(2,1)}, f32[16,128]{1,0:T(8,128)}, f32[8,2048]{1,0:T(8,128)}, f32[8,2048]{1,0:T(...) custom-call(bf16[128,2048]{1,0:T(8,128)(2,1)} %get-tuple-element.33., ...), custom_call_target="tpu_custom_call" | custom-call | tf_op jit(solution)/shard_map/pallas_call | solution.py:1253

commit v9 on v8

--- a/solution.py
+++ b/solution.py
@@ -893,6 +893,8 @@
     lax.fori_loop(0, 4, back_four, 0)
     early = Sums(copies, device, (x, y, z, c), sibling, (e_own, e_got, e_line, e_all), EARLY_BLOCKS)
     late = Sums(copies, device, (x, y, z, c), sibling, (l_own, l_got, l_line, l_all), LATE_BLOCKS)
+    for k in range(21, 32):
+        late.put(k, jnp.zeros((16, 128), F32))
     lowo_t = lowo[...].astype(F32).T.astype(BF)
     olg_t = olg.T.astype(BF)
     low_t = low[...].astype(F32).T.astype(BF)
@@ -969,10 +971,8 @@
             ).astype(BF)
 
     lowg_t = nn(ball[...], gt[...])
-    lowg[...] = lowg_t.T.astype(BF)
-    lowg_t = lowg_t.astype(BF)
-
-    grad_rows(4, 0)
+    lowg_low = lowg_t.astype(BF)
+
 
     def one_columns(n, had):
         cols = pl.ds(pl.multiple_of(n * 256, 256), 256)
@@ -1000,12 +1000,12 @@
         late.put(k, r[k * 16 : (k + 1) * 16])
     up = 2.0 * nt(low_t[:32], gt[HALF:, :])
     late.put(4, jnp.concatenate([up[8:16, :NARROW], up[16:24, NARROW:]], 0))
-    down = nn(lowg_t[:32], hid1[...])
+    down = nn(lowg_low[:32], hid1[...])
     for j in range(16):
         late.put(5 + j, down[8:24, j * 128 : (j + 1) * 128])
-    for k in range(21, 32):
-        late.put(k, jnp.zeros((16, 128), F32))
     late.scatter()
+    lowg[...] = lowg_t.T.astype(BF)
+    grad_rows(4, 0)
 
     copies.sent(out_copy)
     lax.fori_loop(0, 4, one_first, 0)

time: 165 us -> 165 us (level)
  no operation moved by 1% of the time
where the time goes in v9:
time: 165 us
  Pallas kernels  164 us (99%)
    pallas_call x1, Pallas kernels, body(): pl.pallas_call(kernel, out_shape=(array(ROWS, WIDTH, dtype=BF), array(ROW...  161 us
    pallas_call x1, Pallas kernels, body(): pl.pallas_call(finish, out_shape=(array(ROWS, WIDTH, dtype=BF), array(ROW...  3.6 us

profile of v9, /device:TPU:1, one launch (start us, length us, event | category | flops | bytes accessed | tf_op | source)
XLA Modules:
  0.0 165.1 jit_solution(6416814825602290750)
XLA Ops:
  0.7 160.7 %shard_map.317 = (bf16[128,2048]{1,0:T(8,128)(2,1)}, bf16[128,2048]{1,0:T(8,128)(2,1)}, bf16[2,16,16,512]{3,2,1,0:T(8,128)(2,1)}, bf16[2,16,16,256]{3,2,1,0:T(8,128)(2,1)}, f32[16,128]{1,0:T(8,128)}) custom-call(bf16[128,2048]{1,0:T(8,128)(2,1)} %tok.1, s32[8]{0:T(128)} %lens.1, bf16[16,128]{1,0:T(8,128)(2,1)} %bitcast.16, bf16[16,2048]{1,0:T(8,128)(2,1)} %qw.1, ...), custom_call_target="tpu_custom_call" | custom-call | tf_op jit(solution)/shard_map/pallas_call | solution.py:1233
  161.3 3.6 %shard_map.318 = (bf16[128,2048]{1,0:T(8,128)(2,1)}, bf16[128,2048]{1,0:T(8,128)(2,1)}, f32[16,128]{1,0:T(8,128)}, f32[8,2048]{1,0:T(8,128)}, f32[8,2048]{1,0:T(...) custom-call(bf16[128,2048]{1,0:T(8,128)(2,1)} %get-tuple-element.33., ...), custom_call_target="tpu_custom_call" | custom-call | tf_op jit(solution)/shard_map/pallas_call | solution.py:1253
